TPU v7x, 256 devices: a whole 4x4x8 slice. The times are simulated.
256 devices in a mesh: slab: 4 (over x), grp: 64 (over y, z, core).
Axes of the slice: x: 4, y: 4, z: 8, core: 2. Of those that a mesh axis runs over, the one named last changes fastest.
Arguments:
- contact_jac: float32 [16384, 3, 64, 128], P(('slab', 'grp')), may hold values from -0.5 to 0.5
- contact_bodies: int32 [16384, 2], P(('slab', 'grp')), may hold values from 0 to 2047
- contact_class: int32 [16384, 64], P(('slab', 'grp')), may hold values from 0 to 7
- contact_count: int32 [256], P(('slab', 'grp')), may hold values from 16 to 64, as said below
- face_jac: float32 [4096, 3, 64, 128], P(('slab', 'grp')), may hold values from -0.5 to 0.5
- face_own: int32 [4096], P(('slab', 'grp')), may hold values from 0 to 2047
- face_far: int32 [4096], P(('slab', 'grp')), may hold values from 0 to 2047
- face_class: int32 [4096, 64], P(('slab', 'grp')), may hold values from 0 to 7
- warm_contact: float32 [16384, 192], P(('slab', 'grp')), may hold values from -6 to 6
- warm_face: float32 [4096, 192], P(('slab', 'grp')), may hold values from -6 to 6
- free_velocity: float32 [524288], P(('slab', 'grp')), may hold values from -6 to 6
- inverse_mass: float32 [524288], P(('slab', 'grp')), may hold values from 0.25 to 4
- friction_table: float32 [8], replicated, may hold values from 0.1 to 1
- first_step: float32 [1], replicated, may hold values from 0.05 to 0.2
Outputs:
- contact_impulse: float32 [16384, 192], P(('slab', 'grp'))
- face_impulse: float32 [4096, 192], P(('slab', 'grp'))
- body_velocity: float32 [524288], P(('slab', 'grp'))
Inputs may be any that keep to these rules, and one draw needn't show every extreme that they name: `contact_count`: 64 on some device in every draw.
All inputs are finite; a program needn't handle non-finite values.
Results may differ from a plain program's by a relative error of at most 0.0003.
Values sent between devices are 32-bit elements; how exact they have to be, the bound alone decides.
No kernel may reach another device: no remote copies, remote signals or barrier semaphores. Data moves between devices by JAX's collectives and lax.ppermute only.
A program may use at most 64 MiB of HBM per device.

v0:
```python
import math

import jax
import jax.numpy as jnp
from jax import lax
from jax.sharding import PartitionSpec as P

BLK = 64
COMP = 3
ITERS = 3


regular_weight = 0.05
tiny_sum = 1e-06


def shifted(x, axis, by):
    devices = lax.axis_size(axis)
    return lax.ppermute(x, axis, [(i, (i + by) % devices) for i in range(devices)])


def momentum_weights(count):
    theta = 1.0
    weights = []
    for turn in range(count):
        following = (theta * math.sqrt(theta * theta + 4.0) - theta * theta) / 2.0
        weights.append(theta * (1.0 - theta) / (theta * theta + following))
        theta = following
    return weights


def cone_project(pushed, friction, width):
    normal = pushed[:, :width]
    first = pushed[:, width : 2 * width]
    second = pushed[:, 2 * width :]
    tangent = jnp.sqrt(first * first + second * second)
    inside = tangent <= friction * normal
    vanish = friction * tangent <= -normal
    onto = jnp.logical_not(jnp.logical_or(inside, vanish))
    normal_new = (friction * tangent + normal) / (friction * friction + 1.0)
    ratio = jnp.where(onto, friction * normal_new / jnp.where(onto, tangent, 1.0), 1.0)
    keep = jnp.where(inside, 1.0, jnp.where(vanish, 0.0, ratio))
    normal_out = jnp.where(inside, normal, jnp.where(vanish, 0.0, normal_new))
    return jnp.concatenate([normal_out, first * keep, second * keep], 1)


def class_lookup(classes, table):
    levels = jnp.arange(table.shape[0], dtype=jnp.int32)
    picked = (classes[:, :, None] == levels).astype(jnp.float32)
    return jnp.sum(picked * table, axis=2)


def on_device(
    contact_jac,
    contact_bodies,
    contact_class,
    contact_count,
    face_jac,
    face_own,
    face_far,
    face_class,
    warm_contact,
    warm_face,
    free_velocity,
    inverse_mass,
    friction_table,
    first_step,
):
    highest = lax.Precision.HIGHEST
    contact_rows = contact_jac.shape[0]
    face_rows = face_jac.shape[0]
    block_count = lax.axis_size("grp") * (free_velocity.shape[0] // BLK)
    slots = jnp.arange(contact_rows, dtype=jnp.int32)
    live = (slots < contact_count[0]).astype(jnp.float32)[:, None]
    body_first = contact_bodies[:, 0]
    body_second = contact_bodies[:, 1]
    friction_contact = class_lookup(contact_class, friction_table)
    friction_face = class_lookup(face_class, friction_table)

    def force_panel(contact_y, face_y):
        contact_terms = jnp.einsum(
            "kcij,kci->kj",
            contact_jac,
            contact_y.reshape(contact_rows, COMP, BLK),
            precision=highest,
        )
        face_terms = jnp.einsum(
            "kcij,kci->kj", face_jac, face_y.reshape(face_rows, COMP, BLK), precision=highest
        )
        arriving = shifted(face_terms[:, BLK:], "slab", 1)
        total = jnp.zeros((block_count, BLK), jnp.float32)
        total = total.at[body_first].add(contact_terms[:, :BLK])
        total = total.at[body_second].add(contact_terms[:, BLK:])
        total = total.at[face_own].add(face_terms[:, :BLK])
        total = total.at[face_far].add(arriving)
        return total.reshape(-1)

    betas = momentum_weights(ITERS)
    contact_now = warm_contact * live
    face_now = warm_face
    contact_y, face_y = (contact_now, face_now)
    last_cy, last_fy, last_cg, last_fg = (contact_y, face_y, contact_y, face_y)
    for turn in range(ITERS):
        if turn > 0:
            change_c = contact_y - last_cy
            change_f = face_y - last_fy
            local_spread = jnp.sum(change_c * change_c) + jnp.sum(change_f * change_f)
        velocity_total = force_panel(contact_y, face_y)
        owned = lax.psum_scatter(velocity_total, "grp", scatter_dimension=0, tiled=True)
        panel = lax.all_gather(free_velocity + inverse_mass * owned, "grp", axis=0, tiled=True)
        blocks = panel.reshape(block_count, BLK)
        joined = jnp.concatenate([blocks[body_first], blocks[body_second]], 1)
        contact_grad = jnp.einsum("kcij,kj->kci", contact_jac, joined, precision=highest).reshape(
            contact_rows, COMP * BLK
        )
        contact_grad = (contact_grad + regular_weight * contact_y) * live
        returning = shifted(blocks[face_far], "slab", -1)
        face_joined = jnp.concatenate([blocks[face_own], returning], 1)
        face_grad = jnp.einsum("kcij,kj->kci", face_jac, face_joined, precision=highest).reshape(
            face_rows, COMP * BLK
        )
        face_grad = face_grad + regular_weight * face_y
        contact_grad, face_grad = (contact_grad, face_grad)
        if turn == 0:
            step = first_step[0]
        else:
            local_curve = jnp.sum(change_c * (contact_grad - last_cg)) + jnp.sum(
                change_f * (face_grad - last_fg)
            )
            spread, curve = lax.psum((local_spread, local_curve), ("slab", "grp"))
            step = (spread + tiny_sum) / (curve + tiny_sum)
        contact_new = cone_project(contact_y - step * contact_grad, friction_contact, BLK) * live
        face_new = cone_project(face_y - step * face_grad, friction_face, BLK)
        last_cy, last_fy, last_cg, last_fg = (contact_y, face_y, contact_grad, face_grad)
        contact_y = contact_new + betas[turn] * (contact_new - contact_now)
        face_y = face_new + betas[turn] * (face_new - face_now)
        contact_now, face_now = (contact_new, face_new)
    final_total = force_panel(contact_now, face_now)
    owned_final = lax.psum_scatter(final_total, "grp", scatter_dimension=0, tiled=True)
    return (contact_now, face_now, free_velocity + inverse_mass * owned_final)


def solution(mesh):
    return jax.shard_map(
        on_device,
        mesh=mesh,
        in_specs=(
            P(("slab", "grp"), None, None, None),
            P(("slab", "grp"), None),
            P(("slab", "grp"), None),
            P(("slab", "grp")),
            P(("slab", "grp"), None, None, None),
            P(("slab", "grp")),
            P(("slab", "grp")),
            P(("slab", "grp"), None),
            P(("slab", "grp"), None),
            P(("slab", "grp"), None),
            P(("slab", "grp")),
            P(("slab", "grp")),
            P(),
            P(),
        ),
        out_specs=(P(("slab", "grp"), None), P(("slab", "grp"), None), P(("slab", "grp"))),
        check_vma=False,
    )
```

profile of v0, /device:TPU:32, one launch (start us, length us, event | category | flops | bytes accessed | tf_op | source)
XLA Modules:
  0.0 1192.6 jit_solution(9207752094910273176)
XLA Ops:
  15.6 7.4 fusion.48
  32.1 177.4 %all-reduce.11.cloned.1.call-done = f32[131072]{0:T(1024)} async-done(((f32[131072]{0:T(1024)}), f32[131072]{0:T(1024)}) %all-reduce.11.cloned.1.call-update) | async-done | bytes 524304
  210.3 50.3 %all_gather.9 = f32[131072]{0:T(1024)S(1)} all-gather(f32[2048]{0:T(1024)S(1)} %fusion.45), channel_id=1, replica_groups=mesh['slab'=4,'grp'=64] {'grp'}, dimensions={0}, use_global_device_ids=true | all-gather | bytes 532480 | tf_op jit(solution)/shard_map/all_gather | solution.py:110
  261.4 3.0 collective-permute-start.1
  265.7 15.1 %fusion.50 = f32[64,1,3,64]{3,1,2,0:T(1,128)S(1)} fusion(f32[64,128,1,1]{1,2,3,0:T(1,128)S(1)} %bitcast.144, f32[64,3,64,128]{3,2,1,0:T(8,128)} %param.14), kind=kOutput, calls=%fused_computation.190 | convolution fusion | flops 18874368 | bytes 6373376 | tf_op jit(solution)/shard_map/kcij,kj->kci/dot_general | solution.py:113
  282.9 3.3 fusion.51
  290.1 7.4 fusion.52
  303.6 177.3 %all-reduce.13.cloned.1.call-done = f32[131072]{0:T(1024)} async-done(((f32[131072]{0:T(1024)}), f32[131072]{0:T(1024)}) %all-reduce.13.cloned.1.call-update) | async-done | bytes 524304
  481.5 50.2 %all_gather.10 = f32[131072]{0:T(1024)S(1)} all-gather(f32[2048]{0:T(1024)S(1)} %fusion.44), channel_id=1, replica_groups=mesh['slab'=4,'grp'=64] {'grp'}, dimensions={0}, use_global_device_ids=true | all-gather | bytes 532480 | tf_op jit(solution)/shard_map/all_gather | solution.py:110
  534.1 2.9 collective-permute-start.3
  537.1 15.1 %fusion.54 = f32[64,1,3,64]{3,1,2,0:T(1,128)S(1)} fusion(f32[64,128,1,1]{1,2,3,0:T(1,128)S(1)} %bitcast.145, f32[64,3,64,128]{3,2,1,0:T(8,128)} %param.14), kind=kOutput, calls=%fused_computation.194 | convolution fusion | flops 18874368 | bytes 6373376 | tf_op jit(solution)/shard_map/kcij,kj->kci/dot_general | solution.py:113
  554.5 3.3 fusion.55
  562.0 74.9 %all-reduce.5 = (f32[]{:T(128)}, f32[]{:T(128)}) all-reduce(f32[]{:T(128)S(6)} %add.219, f32[]{:T(128)S(6)} %add.224), channel_id=1, replica_groups=mesh['slab'=4,'grp'=64] {'slab','grp'}, use_global_device_ids=true, to_apply=%region_9.10 | all-reduce | flops 2 | bytes 16 | tf_op jit(solution)/shard_map/psum | solution.py:130
  643.3 7.4 fusion.15
  656.8 175.9 %all-reduce.15.cloned.1.call-done = f32[131072]{0:T(1024)} async-done(((f32[131072]{0:T(1024)}), f32[131072]{0:T(1024)}) %all-reduce.15.cloned.1.call-update) | async-done | bytes 524304
  833.4 50.2 %all_gather.11 = f32[131072]{0:T(1024)S(1)} all-gather(f32[2048]{0:T(1024)S(1)} %fusion.43), channel_id=1, replica_groups=mesh['slab'=4,'grp'=64] {'grp'}, dimensions={0}, use_global_device_ids=true | all-gather | bytes 532480 | tf_op jit(solution)/shard_map/all_gather | solution.py:110
  885.9 3.0 collective-permute-start.5
  889.0 15.1 %fusion.56 = f32[64,1,3,64]{3,1,2,0:T(1,128)S(1)} fusion(f32[64,128,1,1]{1,2,3,0:T(1,128)S(1)} %bitcast.146, f32[64,3,64,128]{3,2,1,0:T(8,128)} %param.14), kind=kOutput, calls=%fused_computation.196 | convolution fusion | flops 18874368 | bytes 6373376 | tf_op jit(solution)/shard_map/kcij,kj->kci/dot_general | solution.py:113
  904.3 1.6 multiply_reduce_fusion
  906.7 3.3 fusion.57
  910.1 1.5 multiply_reduce_fusion.4
  914.2 74.9 %all-reduce.4 = (f32[]{:T(128)}, f32[]{:T(128)}) all-reduce(f32[]{:T(128)S(6)} %add.232, f32[]{:T(128)S(6)} %add.239), channel_id=1, replica_groups=mesh['slab'=4,'grp'=64] {'slab','grp'}, use_global_device_ids=true, to_apply=%region_20.21 | all-reduce | flops 2 | bytes 16 | tf_op jit(solution)/shard_map/psum | solution.py:130
  994.9 7.4 fusion.13
  1009.1 175.2 %all-reduce.17.cloned.1.call-done = f32[131072]{0:T(1024)} async-done(((f32[131072]{0:T(1024)}), f32[131072]{0:T(1024)}) %all-reduce.17.cloned.1.call-update) | async-done | bytes 524304
  (207 shorter events, 64.5 us)
Async XLA Ops:
  7.2 202.4 %all-reduce.11.cloned.1.call-start = ((), (), s32[]{:S(2)}) async-start(), calls=%async_computation | async-start | bytes 1048576
  10.1 199.5 %copy-start.9 = (f32[2048]{0:T(1024)S(1)}, f32[2048]{0:T(1024)}, u32[]{:S(2)}) copy-start(f32[2048]{0:T(1024)} %param.24) | copy-start | bytes 24580
  10.1 199.5 %copy-start.13 = (f32[2048]{0:T(1024)S(1)}, f32[2048]{0:T(1024)}, u32[]{:S(2)}) copy-start(f32[2048]{0:T(1024)} %param.25) | copy-start | bytes 24580
  10.2 16.4 %collective-permute-start = (f32[16,64]{1,0:T(8,128)S(1)}, f32[16,64]{1,0:T(8,128)S(1)}, u32[]{:S(2)}, u32[]{:S(2)}) collective-permute-start(f32[16,64]{1,0:T(8,128)S(1)} %slice.171), channel_id=1, source_target_pairs={{0,64},{64,128},{128,192},{192,0},{1,65},{65,129},{129,193},{193,1... | collective-permute-start | bytes 12296 | tf_op jit(solution)/shard_map/ppermute | solution.py:19
  14.9 245.7 %copy-start.37 = (s32[16]{0:T(128)}, s32[16]{0:T(128)S(1)}, u32[]{:S(2)}) copy-start(s32[16]{0:T(128)S(1)} %compare_select_fusion.1) | copy-start | bytes 196
  23.0 257.7 %copy-start.31 = (s32[1024]{0:T(1024)}, s32[1024]{0:T(1024)S(1)}, u32[]{:S(2)}) copy-start(s32[1024]{0:T(1024)S(1)} %get-tuple-element.43) | copy-start | bytes 12292
  23.0 257.7 %copy-start.32 = (s32[1024]{0:T(1024)}, s32[1024]{0:T(1024)S(1)}, u32[]{:S(2)}) copy-start(s32[1024]{0:T(1024)S(1)} %get-tuple-element.44) | copy-start | bytes 12292
  23.0 257.7 %copy-start.33 = (s32[1024]{0:T(1024)}, s32[1024]{0:T(1024)S(1)}, u32[]{:S(2)}) copy-start(s32[1024]{0:T(1024)S(1)} %pad_clamp_fusion) | copy-start | bytes 12292
  26.6 254.4 %copy-start.1 = (f32[64,192]{1,0:T(8,128)S(1)}, f32[64,192]{1,0:T(8,128)}, u32[]{:S(2)}) copy-start(f32[64,192]{1,0:T(8,128)} %param.22) | copy-start | bytes 147460
  26.6 254.4 %copy-start.22 = (f32[64]{0:T(128)S(1)}, f32[64]{0:T(128)}, u32[]{:S(2)}) copy-start(f32[64]{0:T(128)} %copy-done.21) | copy-start | bytes 772
  28.7 452.1 %all-reduce.13.cloned.1.call-start = ((), (), s32[]{:S(2)}) async-start(), calls=%async_computation.1 | async-start | bytes 1048576
  261.4 21.4 %collective-permute-start.1 = (f32[16,64]{1,0:T(8,128)S(1)}, f32[16,64]{1,0:T(8,128)S(1)}, u32[]{:S(2)}, u32[]{:S(2)}) collective-permute-start(f32[16,64]{1,0:T(8,128)S(1)} %gather_fusion.3), channel_id=1, source_target_pairs={{0,192},{64,0},{128,64},{192,128},{1,193},{65,1},{129,65},{193,129... | collective-permute-start | bytes 12296 | tf_op jit(solution)/shard_map/ppermute | solution.py:19
  289.6 191.3 %copy-start.10 = (f32[2048]{0:T(1024)S(1)}, f32[2048]{0:T(1024)}, u32[]{:S(2)}) copy-start(f32[2048]{0:T(1024)} %param.24) | copy-start | bytes 24580
  289.6 191.3 %copy-start.14 = (f32[2048]{0:T(1024)S(1)}, f32[2048]{0:T(1024)}, u32[]{:S(2)}) copy-start(f32[2048]{0:T(1024)} %param.25) | copy-start | bytes 24580
  289.6 11.8 collective-permute-start.2
  303.5 529.2 %all-reduce.15.cloned.1.call-start = ((), (), s32[]{:S(2)}) async-start(), calls=%async_computation.2 | async-start | bytes 1048576
  534.1 20.3 %collective-permute-start.3 = (f32[16,64]{1,0:T(8,128)S(1)}, f32[16,64]{1,0:T(8,128)S(1)}, u32[]{:S(2)}, u32[]{:S(2)}) collective-permute-start(f32[16,64]{1,0:T(8,128)S(1)} %gather_fusion.7), channel_id=1, source_target_pairs={{0,192},{64,0},{128,64},{192,128},{1,193},{65,1},{129,65},{193,129... | collective-permute-start | bytes 12296 | tf_op jit(solution)/shard_map/ppermute | solution.py:19
  642.0 190.7 %copy-start.11 = (f32[2048]{0:T(1024)S(1)}, f32[2048]{0:T(1024)}, u32[]{:S(2)}) copy-start(f32[2048]{0:T(1024)} %param.24) | copy-start | bytes 24580
  642.0 190.7 %copy-start.15 = (f32[2048]{0:T(1024)S(1)}, f32[2048]{0:T(1024)}, u32[]{:S(2)}) copy-start(f32[2048]{0:T(1024)} %param.25) | copy-start | bytes 24580
  642.2 12.4 %collective-permute-start.4 = (f32[16,64]{1,0:T(8,128)S(1)}, f32[16,64]{1,0:T(8,128)S(1)}, u32[]{:S(2)}, u32[]{:S(2)}) collective-permute-start(f32[16,64]{1,0:T(8,128)S(1)} %slice.191), channel_id=1, source_target_pairs={{0,64},{64,128},{128,192},{192,0},{1,65},{65,129},{129,193},{193,1... | collective-permute-start | bytes 12296 | tf_op jit(solution)/shard_map/ppermute | solution.py:19
  656.8 527.5 %all-reduce.17.cloned.1.call-start = ((), (), s32[]{:S(2)}) async-start(), calls=%async_computation.3 | async-start | bytes 1048576
  885.9 20.6 %collective-permute-start.5 = (f32[16,64]{1,0:T(8,128)S(1)}, f32[16,64]{1,0:T(8,128)S(1)}, u32[]{:S(2)}, u32[]{:S(2)}) collective-permute-start(f32[16,64]{1,0:T(8,128)S(1)} %gather_fusion.11), channel_id=1, source_target_pairs={{0,192},{64,0},{128,64},{192,128},{1,193},{65,1},{129,65},{193,129... | collective-permute-start | bytes 12296 | tf_op jit(solution)/shard_map/ppermute | solution.py:19
  993.7 190.6 %copy-start.16 = (f32[2048]{0:T(1024)S(1)}, f32[2048]{0:T(1024)}, u32[]{:S(2)}) copy-start(f32[2048]{0:T(1024)} %param.25) | copy-start | bytes 24580
  993.7 12.5 %collective-permute-start.6 = (f32[16,64]{1,0:T(8,128)S(1)}, f32[16,64]{1,0:T(8,128)S(1)}, u32[]{:S(2)}, u32[]{:S(2)}) collective-permute-start(f32[16,64]{1,0:T(8,128)S(1)} %slice.201), channel_id=1, source_target_pairs={{0,64},{64,128},{128,192},{192,0},{1,65},{65,129},{129,193},{193,1... | collective-permute-start | bytes 12296 | tf_op jit(solution)/shard_map/ppermute | solution.py:19
  (26 other events, 988.8 us)
Sparse Core Ops, SparseCore 0:
  28.8 180.7 all-reduce.10
  303.6 177.1 all-reduce.12
  656.9 175.7 all-reduce.14
  1008.5 175.7 all-reduce.16
where the time goes:
time: 1200 us; the launch traced here: 1190 us
  waiting for transfers between devices  706 us (59%)
  blocking collectives  301 us (25%)
  matrix products  90.7 us (8%)
  other arithmetic  41 us (3%)
  between operations  24.8 us (2%)
  local copies, waits for them, and re-layouts  16.6 us (1%)
  starting transfers between devices  13 us (1%)
    unnamed x8, waiting for transfers between devices  706 us
    all_gather x3, blocking collectives, on_device(): lax.all_gather(free_velocity + inverse_mass * owned, 'grp', axis=0, tiled...  151 us
    psum x2, blocking collectives, on_device(): spread, curve = lax.psum((local_spread, local_curve), ('slab', 'grp'))  150 us
    dot_general x3, matrix products, on_device(): jnp.einsum('kcij,kj->kci', contact_jac, joined, precision=highest)  45.2 us
    dot_general x4, matrix products, force_panel(): jnp.einsum('kcij,kci->kj', contact_jac, contact_y.reshape(contact_rows, C...  29.7 us
  transfers between devices with their start and end apart: 11, of which 4 were waited for; matrix products, arithmetic and copies ran while one was open for 9% of the time, Pallas kernels for 0%

commit v1 on v0

v1 whole, which is shorter than its diff:
```python
import functools
import math

import jax
import jax.numpy as jnp
from jax import lax
from jax.experimental import pallas as pl
from jax.experimental.pallas import tpu as pltpu
from jax.sharding import PartitionSpec as P

BLK = 64
COMP = 3
ITERS = 3
NY, NZ, NC = 4, 8, 2
CHIPS = NY * NZ
OWN = 16

KC, KF = 64, 16
GC, GF = 128 // KC, 128 // KF
IC, IF = BLK // GC, BLK // GF
SC, SF = COMP * IC, COMP * IF

regular_weight = 0.05
tiny_sum = 1e-06
vmem = pl.BlockSpec(memory_space=pltpu.VMEM)
smem = pl.BlockSpec(memory_space=pltpu.SMEM)
hbm = pl.BlockSpec(memory_space=pltpu.HBM)
f32 = jnp.float32


def shape(*dims):
    return jax.ShapeDtypeStruct(dims, f32)


def kernel_call(body, out, specs, scratch=(), megabytes=4, out_specs=None):
    return pl.pallas_call(
        body,
        out_shape=out,
        in_specs=specs,
        out_specs=out_specs or jax.tree.map(lambda _: vmem, out),
        scratch_shapes=list(scratch),
        compiler_params=pltpu.CompilerParams(vmem_limit_bytes=megabytes << 20),
    )


def shifted(x, axis, by):
    devices = lax.axis_size(axis)
    return lax.ppermute(x, axis, [(i, (i + by) % devices) for i in range(devices)])


def other_core(x):
    devices = CHIPS * NC
    return lax.ppermute(x, "grp", [(i, i ^ 1) for i in range(devices)])


def momentum_weights(count):
    theta = 1.0
    weights = []
    for turn in range(count):
        following = (theta * math.sqrt(theta * theta + 4.0) - theta * theta) / 2.0
        weights.append(theta * (1.0 - theta) / (theta * theta + following))
        theta = following
    return weights


def class_lookup(classes, table):
    levels = jnp.arange(table.shape[0], dtype=jnp.int32)
    picked = (classes[:, :, None] == levels).astype(f32)
    return jnp.sum(picked * table, axis=2)


def to_lanes(x, parts):
    k, width = x.shape
    x = x.reshape(k, width // BLK, parts, BLK // parts)
    return x.transpose(1, 3, 2, 0).reshape(width // parts, 128)


def from_lanes(x, parts):
    x = x.reshape(-1, BLK // parts, parts, 128 // parts)
    return x.transpose(3, 0, 2, 1).reshape(128 // parts, -1)


def left_half(rows):
    return lax.broadcasted_iota(jnp.int32, (rows, 128), 1) < BLK


def rows_of(slice_at):
    return pl.ds(pl.multiple_of(slice_at * 128, 128), 128)


def accumulate(jac, y, first, count, total):
    def add(s, total):
        return total + jac[rows_of(s), :] * y[pl.ds(s, 1), :]

    return lax.fori_loop(first, first + count, add, total, unroll=4)


def folded(total, parts):
    turned = total.T
    k = 128 // parts
    return sum(turned[p * k : (p + 1) * k] for p in range(parts))


def product(jac, velocity, partial, first, count):
    def one(s, _):
        terms = jac[rows_of(s), :] * velocity
        partial[pl.ds(pl.multiple_of(s * 8, 8), 8), :] = jnp.sum(
            terms.reshape(16, 8, 128), axis=0
        )
        return _

    lax.fori_loop(first, first + count, one, 0, unroll=4)


def summed(partial, slices):
    return sum(partial[pl.ds(q, slices, stride=8), :] for q in range(8))


def first_force_kernel(cjac, fjac, cwarm, fwarm, terms, cbuf, fbuf, partial, csem, fsem):
    parts = 4
    share = KC // parts * COMP * BLK
    ccopies = [
        pltpu.make_async_copy(
            cjac.at[pl.ds(p * share, share)], cbuf.at[pl.ds(p * share, share)], csem.at[p]
        )
        for p in range(parts)
    ]
    fcopy = pltpu.make_async_copy(fjac, fbuf, fsem)
    fcopy.start()
    for copy in ccopies:
        copy.start()
    width = COMP * BLK
    rows = jnp.concatenate([cwarm[...], fwarm[...], jnp.zeros((128 - KC - KF, width), f32)], 0)
    rows = jnp.concatenate([rows, jnp.zeros((128, 256 - width), f32)], 1)
    turned = jnp.concatenate([rows[:, :128].T, rows[:, 128:].T], 0)[:width]

    def block(jac, at, k):
        y = jnp.broadcast_to(turned[:, k : k + 1], (width, 128))
        terms_k = jac[at * width : (at + 1) * width, :] * y
        partial[k * 8 : (k + 1) * 8, :] = jnp.sum(terms_k.reshape(width // 8, 8, 128), 0)

    fcopy.wait()
    for m in range(KF):
        block(fbuf, m, KC + m)
    for p, copy in enumerate(ccopies):
        copy.wait()
        for m in range(KC // parts):
            block(cbuf, p * (KC // parts) + m, p * (KC // parts) + m)
    terms[...] = sum(partial[pl.ds(q, KC + KF, stride=8), :] for q in range(8))


def layout_kernel(cjac, fjac, cout, fout, cbuf, fbuf, cturn, fturn, sems, outs):
    copies = [pltpu.make_async_copy(fjac, fbuf, sems.at[0])]
    copies.append(pltpu.make_async_copy(cjac, cbuf, sems.at[1]))
    for copy in copies:
        copy.start()

    def turn(jac, out, parts, depth, first, count):
        k = 128 // parts

        def one(s, _):
            row = s // depth * BLK + s % depth
            rows = [
                jac[pl.ds(row + p * depth, k, stride=COMP * BLK), :] for p in range(parts)
            ]
            out[rows_of(s), :] = jnp.concatenate(rows, 0).T
            return _

        lax.fori_loop(first, first + count, one, 0, unroll=8)

    copies[0].wait()
    turn(fbuf, fturn, GF, IF, 0, SF)
    leaving = [pltpu.make_async_copy(fturn, fout, outs.at[0])]
    leaving[0].start()
    copies[1].wait()
    for part in range(4):
        share = SC // 4
        turn(cbuf, cturn, GC, IC, part * share, share)
        rows = pl.ds(part * share * 128, share * 128)
        copy = pltpu.make_async_copy(cturn.at[rows], cout.at[rows], outs.at[part + 1])
        copy.start()
        leaving.append(copy)
    for copy in leaving:
        copy.wait()


def streamed(jac, buf, sems, slices, work, ahead):
    parts = sems.shape[0]
    share = slices // parts
    copies = []
    for p in range(parts):
        rows = pl.ds(p * share * 128, share * 128)
        copies.append(pltpu.make_async_copy(jac.at[rows], buf.at[rows], sems.at[p]))
    for copy in copies:
        copy.start()
    carry = ahead()
    for p, copy in enumerate(copies):
        copy.wait()
        carry = work(p * share, share, carry)
    return carry


def force_kernel(jac, y, terms, buf, sems):
    total = streamed(
        jac,
        buf,
        sems,
        SC,
        lambda first, count, total: accumulate(buf, y, first, count, total),
        lambda: jnp.zeros((128, 128), f32),
    )
    terms[...] = folded(total, GC)


def scatter_kernel(rows, swap, cterms, fterms, arriving, own, other, total, wide):
    left = left_half(KC)
    near = left_half(KF)
    wide[0:KC, :] = jnp.where(left, cterms[...], 0.0)
    wide[KC : 2 * KC, :] = jnp.where(left, 0.0, cterms[...])
    wide[2 * KC : 2 * KC + KF, :] = jnp.where(near, fterms[...], 0.0)
    wide[2 * KC + KF :, :] = jnp.where(near, 0.0, arriving[...])
    x = wide[...]
    wide[...] = jnp.where(swap[...] > 0, pltpu.roll(x, BLK, 1), x)
    total[...] = jnp.zeros_like(total)
    for m in range(2 * KC + 2 * KF):
        at = pl.ds(rows[m], 1)
        total[at, :] = total[at, :] + wide[m : m + 1, :]
    half = CHIPS * OWN
    own[...] = total[0:half, :].reshape(own.shape)
    other[...] = total[half:, :].reshape(other.shape)


def owner_kernel(with_sums, received, free, mass, last, spread, owned, pieces):
    total = jnp.sum(received[...], 0)
    owned[...] = total
    piece = free[...] + mass[...] * total
    if with_sums:
        change = total - last[...]
        curve = jnp.sum(mass[...] * change * change)
        row = lax.broadcasted_iota(jnp.int32, (8, 128), 0)
        sums = jnp.where(row == 0, jnp.sum(spread[...]), curve)
        piece = jnp.concatenate([piece, sums], 0)
    pieces[...] = jnp.broadcast_to(piece, pieces.shape)


def far_kernel(with_sums, rows, swap, panel, far, *sums):
    base = 2 * KC + KF
    picked = jnp.concatenate([panel[pl.ds(rows[base + m], 1), :] for m in range(KF)], 0)
    far[0:KF, :] = jnp.where(swap[base:, :] > 0, pltpu.roll(picked, BLK, 1), picked)
    if with_sums:
        size = OWN + 8
        total = sum(
            panel[p * size + OWN : (p + 1) * size, :] for p in range(NC * CHIPS)
        )
        sums[0][...] = total
        far[KF:, :] = total


def gradient_kernel(rows, swap, panel, jac, y, live, grad, fown, picked, partial, buf, sems):
    def ahead():
        for m in range(2 * KC + KF):
            picked[m : m + 1, :] = panel[pl.ds(rows[m], 1), :]
        x = picked[...]
        x = jnp.where(swap[0 : 2 * KC + KF, :] > 0, pltpu.roll(x, BLK, 1), x)
        fown[...] = x[2 * KC :]
        joined = jnp.where(left_half(KC), x[0:KC], x[KC : 2 * KC])
        return jnp.concatenate([joined] * GC, 0).T

    def work(first, count, velocity):
        product(buf, velocity, partial, first, count)
        return velocity

    streamed(jac, buf, sems, SC, work, ahead)
    grad[...] = (summed(partial, SC) + regular_weight * y[...]) * live[...]


def cone(pushed, friction):
    normal, first, second = pushed
    tangent = jnp.sqrt(first * first + second * second)
    inside = tangent <= friction * normal
    vanish = friction * tangent <= -normal
    onto = jnp.logical_not(jnp.logical_or(inside, vanish))
    normal_new = (friction * tangent + normal) / (friction * friction + 1.0)
    ratio = jnp.where(onto, friction * normal_new / jnp.where(onto, tangent, 1.0), 1.0)
    keep = jnp.where(inside, 1.0, jnp.where(vanish, 0.0, ratio))
    normal_out = jnp.where(inside, normal, jnp.where(vanish, 0.0, normal_new))
    return jnp.concatenate([normal_out, first * keep, second * keep], 0)


def update_kernel(
    first, beta, last, *refs
):
    (s0, s1, s2, grad, fown, far, jac, cy, fy, cnow, fnow, live, cfric, ffric) = refs[:14]
    (cnew, fnew, cnext, fnext, spread, fterms, partial, buf, sems) = refs[14:]

    def ahead():
        joined = jnp.where(left_half(KF), fown[...], far[0:KF, :])
        return jnp.concatenate([joined] * GF, 0).T

    def work(first_slice, count, velocity):
        product(buf, velocity, partial, first_slice, count)
        return velocity

    streamed(jac, buf, sems, SF, work, ahead)
    fgrad = summed(partial, SF) + regular_weight * fy[...]
    if first:
        step = s0[...]
    else:
        sums = s0[...] + s1[...] + s2[...] + far[KF:, :]
        total = sums[0:1]
        curve = sums[1:2] + regular_weight * total
        step = (total + tiny_sum) / (curve + tiny_sum)

    def project(y, g, friction, depth):
        pushed = y - step * g
        return cone([pushed[c * depth : (c + 1) * depth] for c in range(COMP)], friction)

    cfresh = project(cy[...], grad[...], cfric[...], IC) * live[...]
    ffresh = project(fy[...], fgrad, ffric[...], IF)
    cnew[...] = cfresh
    fnew[...] = ffresh
    if last:
        fnext[...] = ffresh
        cnext[...] = cfresh
        spread[...] = jnp.zeros_like(spread)
    else:
        cafter = cfresh + beta * (cfresh - cnow[...])
        fafter = ffresh + beta * (ffresh - fnow[...])
        cnext[...] = cafter
        fnext[...] = fafter
        cmove, fmove = cafter - cy[...], fafter - fy[...]
        spread[...] = jnp.sum((cmove * cmove).reshape(SC // 8, 8, 128), 0) + jnp.sum(
            (fmove * fmove).reshape(SF // 8, 8, 128), 0
        )
    total = accumulate(buf, fnext, 0, SF, jnp.zeros((128, 128), f32))
    fterms[...] = folded(total, GF)


def exchange(parts):
    groups = [[chip * NC + core for chip in range(CHIPS)] for core in range(NC)]
    return lax.all_to_all(parts, "grp", 0, 0, axis_index_groups=groups, tiled=True)


def all_gather(pieces):
    half = exchange(pieces)
    return jnp.stack([half, other_core(half)]).reshape(-1, 128)


def on_device(
    contact_jac,
    contact_bodies,
    contact_class,
    contact_count,
    face_jac,
    face_own,
    face_far,
    face_class,
    warm_contact,
    warm_face,
    free_velocity,
    inverse_mass,
    friction_table,
    first_step,
):
    free_own = free_velocity.reshape(OWN, 128)
    mass_own = inverse_mass.reshape(OWN, 128)
    slots = jnp.arange(128, dtype=jnp.int32) % KC
    live = (slots < contact_count[0]).astype(f32)[None, :]

    targets = jnp.concatenate(
        [contact_bodies[:, 0], contact_bodies[:, 1], face_own, face_far]
    )
    owner = targets // (2 * OWN)
    slot = (owner - lax.axis_index("grp")) % NC * CHIPS + owner // NC
    row = targets % (2 * OWN) // 2
    sum_rows = slot * OWN + row
    panel_rows = [slot * OWN + row] + [slot * (OWN + 8) + row] * (ITERS - 1)
    order = jnp.arange(targets.shape[0])
    right = ((order >= KC) & (order < 2 * KC)) | (order >= 2 * KC + KF)
    swap = jnp.broadcast_to(
        ((targets % 2 == 1) != right).astype(f32)[:, None], (targets.shape[0], 128)
    )
    cfric = to_lanes(class_lookup(contact_class, friction_table), GC)
    ffric = to_lanes(class_lookup(face_class, friction_table), GF)

    def reduced(cterms, fterms, arriving):
        halves = kernel_call(
            scatter_kernel,
            (shape(CHIPS, OWN, 128), shape(CHIPS, OWN, 128)),
            [smem] + [vmem] * 4,
            [pltpu.VMEM((NC * CHIPS * OWN, 128), f32), pltpu.VMEM((2 * KC + 2 * KF, 128), f32)],
        )(sum_rows, swap, cterms, fterms, arriving)
        return exchange(halves[0] + other_core(halves[1]))

    betas = momentum_weights(ITERS)
    cwarm = warm_contact * live[0, :KC, None]
    crows, frows = contact_jac.reshape(-1, 128), face_jac.reshape(-1, 128)
    cbuf, fbuf = pltpu.VMEM((SC * 128, 128), f32), pltpu.VMEM((SF * 128, 128), f32)
    terms = kernel_call(
        first_force_kernel,
        shape(KC + KF, 128),
        [hbm, hbm, vmem, vmem],
        [
            cbuf,
            fbuf,
            pltpu.VMEM(((KC + KF) * 8, 128), f32),
            pltpu.SemaphoreType.DMA((4,)),
            pltpu.SemaphoreType.DMA,
        ],
        16,
    )(crows, frows, cwarm, warm_face)
    cterms, fterms = terms[:KC], terms[KC:]
    arriving = shifted(fterms, "slab", 1)
    cjac, fjac = kernel_call(
        layout_kernel,
        (shape(SC * 128, 128), shape(SF * 128, 128)),
        [hbm, hbm],
        [cbuf, fbuf, cbuf, fbuf, pltpu.SemaphoreType.DMA((2,)), pltpu.SemaphoreType.DMA((5,))],
        24,
        (hbm, hbm),
    )(crows, frows)
    cnow = to_lanes(cwarm, GC)
    fnow = to_lanes(warm_face, GF)
    cy, fy = cnow, fnow
    spread = jnp.zeros((8, 128), f32)
    owned = free_own
    for turn in range(ITERS):
        received = reduced(cterms, fterms, arriving)
        extra = 8 if turn > 0 else 0
        owned, pieces = kernel_call(
            functools.partial(owner_kernel, turn > 0),
            (shape(OWN, 128), shape(CHIPS, OWN + extra, 128)),
            [vmem] * 5,
        )(received, free_own, mass_own, owned, spread)
        panel = all_gather(pieces)
        picked = kernel_call(
            functools.partial(far_kernel, turn > 0),
            (shape(KF + extra, 128), shape(8, 128))[: 2 if turn > 0 else 1],
            [smem, vmem, vmem],
        )(panel_rows[turn], swap, panel)
        returning = shifted(picked[0], "slab", -1)
        if turn == 0:
            steps = [jnp.broadcast_to(first_step[:, None], (1, 128))] * 3
        else:
            steps = [picked[1]] + [shifted(picked[1], "slab", by) for by in (1, 2)]
        grad, fown = kernel_call(
            gradient_kernel,
            (shape(SC, 128), shape(KF, 128)),
            [smem, vmem, vmem, hbm, vmem, vmem],
            [
                pltpu.VMEM((2 * KC + KF, 128), f32),
                pltpu.VMEM((SC * 8, 128), f32),
                cbuf,
                pltpu.SemaphoreType.DMA((6,)),
            ],
            16,
        )(panel_rows[turn], swap, panel, cjac, cy, live)
        body = functools.partial(update_kernel, turn == 0, betas[turn], turn == ITERS - 1)
        cnow, fnow, cy, fy, spread, fterms = kernel_call(
            body,
            (
                shape(SC, 128),
                shape(SF, 128),
                shape(SC, 128),
                shape(SF, 128),
                shape(8, 128),
                shape(KF, 128),
            ),
            [vmem] * 6 + [hbm] + [vmem] * 7,
            [pltpu.VMEM((SF * 8, 128), f32), fbuf, pltpu.SemaphoreType.DMA((2,))],
        )(*steps, grad, fown, returning, fjac, cy, fy, cnow, fnow, live, cfric, ffric)
        arriving = shifted(fterms, "slab", 1)
        cterms = kernel_call(
            force_kernel,
            shape(KC, 128),
            [hbm, vmem],
            [cbuf, pltpu.SemaphoreType.DMA((6,))],
            16,
        )(cjac, cy)
    received = reduced(cterms, fterms, arriving)
    final = free_own + mass_own * jnp.sum(received, 0)
    return (from_lanes(cnow, GC), from_lanes(fnow, GF), final.reshape(-1))


def solution(mesh):
    return jax.shard_map(
        on_device,
        mesh=mesh,
        in_specs=(
            P(("slab", "grp"), None, None, None),
            P(("slab", "grp"), None),
            P(("slab", "grp"), None),
            P(("slab", "grp")),
            P(("slab", "grp"), None, None, None),
            P(("slab", "grp")),
            P(("slab", "grp")),
            P(("slab", "grp"), None),
            P(("slab", "grp"), None),
            P(("slab", "grp"), None),
            P(("slab", "grp")),
            P(("slab", "grp")),
            P(),
            P(),
        ),
        out_specs=(P(("slab", "grp"), None), P(("slab", "grp"), None), P(("slab", "grp"))),
        check_vma=False,
    )
```

time: 1200 us -> 222 us (0.18)
  waiting for transfers between devices: 706 us -> 39 us
  blocking collectives: 301 us -> 112 us
  matrix products: 90.7 us -> 0 us
  other arithmetic: 41 us -> 2.91 us
  Pallas kernels: 0 us -> 33 us
  between operations: 24.8 us -> 2.46 us
    unnamed x8 -> x0, waiting for transfers between devices: 706 us -> none
    all_gather x3 -> x0, blocking collectives: 151 us -> none  [on_device(): lax.all_gather(free_velocity + inverse_mass * owned, 'grp', axis=0, tiled...]
    psum x2 -> x0, blocking collectives: 150 us -> none  [on_device(): spread, curve = lax.psum((local_spread, local_curve), ('slab', 'grp'))]
    all_to_all x0 -> x6, blocking collectives: none -> 112 us  [exchange(): lax.all_to_all(parts, 'grp', 0, 0, axis_index_groups=groups, tiled=True)]
    dot_general x14 -> x0, matrix products: 90.7 us -> none  [the longest x3 45.2 us: on_device(): jnp.einsum('kcij,kj->kci', contact_jac, joined, precision=highest)]
    pallas_call x0 -> x21, Pallas kernels: none -> 33 us  [the longest x1 9.67 us: on_device(): kernel_call(layout_kernel, (shape(SC * 128, 128), shape(SF * 128, 128)),...]
    scatter-add x16 -> x0, other arithmetic: 19.4 us -> none  [the longest x4 5.87 us: force_panel(): total = total.at[body_second].add(contact_terms[:, BLK:])]
    ppermute x7 -> x11, waiting for transfers between devices: 0.02 us -> 17.1 us  [shifted(): lax.ppermute(x, axis, [(i, (i + by) % devices) for i in range(devices)])]
  transfers between devices with their start and end apart: 11 -> 19, of which waited for: 4 -> 16; matrix products, arithmetic and copies ran while one was open for 9% -> 1% of each run, Pallas kernels for 0% -> 9%
where the time goes in v1:
time: 222 us; the launch traced here: 221 us
  blocking collectives  112 us (50%)
  waiting for transfers between devices  39 us (18%)
  Pallas kernels  33 us (15%)
  local copies, waits for them, and re-layouts  17.6 us (8%)
  starting transfers between devices  14.8 us (7%)
  other arithmetic  2.91 us (1%)
  between operations  2.46 us (1%)
    all_to_all x6, blocking collectives, exchange(): lax.all_to_all(parts, 'grp', 0, 0, axis_index_groups=groups, tiled=True)  112 us
    ppermute x11, waiting for transfers between devices, shifted(): lax.ppermute(x, axis, [(i, (i + by) % devices) for i in range(devices)])  17.1 us
    unnamed x39, local copies, waits for them, and re-layouts  16.5 us
    all_to_all x1, waiting for transfers between devices, exchange(): lax.all_to_all(parts, 'grp', 0, 0, axis_index_groups=groups, tiled=True)  10.9 us
    ppermute x7, waiting for transfers between devices, other_core(): return lax.ppermute(x, 'grp', [(i, i ^ 1) for i in range(devices)])  10.9 us
    ppermute x11, starting transfers between devices, shifted(): lax.ppermute(x, axis, [(i, (i + by) % devices) for i in range(devices)])  9.75 us
    pallas_call x1, Pallas kernels, on_device(): kernel_call(layout_kernel, (shape(SC * 128, 128), shape(SF * 128, 128)),...  9.67 us
    pallas_call x3, Pallas kernels, on_device(): kernel_call(gradient_kernel, (shape(SC, 128), shape(KF, 128)), [smem, vme...  5.99 us
  transfers between devices with their start and end apart: 19, of which 16 were waited for; matrix products, arithmetic and copies ran while one was open for 1% of the time, Pallas kernels for 9%

profile of v1, /device:TPU:32, one launch (start us, length us, event | category | flops | bytes accessed | tf_op | source)
XLA Modules:
  0.0 221.5 jit_solution(17058741251158109161)
XLA Ops:
  2.4 2.8 %copy-done.2 = f32[64,3,64,128]{3,2,1,0:T(8,128)S(1)} copy-done((f32[64,3,64,128]{3,2,1,0:T(8,128)S(1)}, f32[64,3,64,128]{3,2,1,0:T(8,128)}, u32[]{:S(2)}) %copy-start.2) | copy-done | bytes 6291480
  7.3 3.2 %shard_map.158 = f32[80,128]{1,0:T(8,128)S(1)} custom-call(f32[12288,128]{1,0:T(8,128)S(1)} %bitcast.49, f32[3072,128]{1,0:T(8,128)S(1)} %bitcast.55, f32[64,192]{1,0:T(8,128)S(1)} %broadcast_multiply_fusion.cwarm, f32[16,192]{1,0:T(8,128)S(1)} %copy-done.10), custom_call_target="tpu_custom_call" | custom-call | tf_op jit(solution)/shard_map/pallas_call | solution.py:399
  12.2 3.2 %collective-permute-done.arriving = f32[16,128]{1,0:T(8,128)S(1)} collective-permute-done((f32[16,128]{1,0:T(8,128)S(1)}, f32[16,128]{1,0:T(8,128)S(1)}, u32[]{:S(2)}, u32[]{:S(2)}) %collective-permute-start) | collective-permute-done | bytes 8224 | tf_op jit(solution)/shard_map/ppermute | solution.py:48
  18.5 23.7 %all_to_all.35.received = f32[32,16,128]{2,1,0:T(8,128)S(1)} all-to-all(f32[32,16,128]{2,1,0:T(8,128)S(1)} %add.67), channel_id=1, replica_groups={{0,2,4,6,8,10,12,14,16,18,20,22,24,26,28,30,32,34,36,38,40,42,44,46,48,..., dimensions={0} | all-to-all | bytes 524288 | tf_op jit(solution)/shard_map/all_to_all | solution.py:341
  42.4 16.2 %all_to_all.36 = f32[32,16,128]{2,1,0:T(8,128)S(1)} all-to-all(f32[32,16,128]{2,1,0:T(8,128)S(1)} %get-tuple-element.47), channel_id=1, replica_groups={{0,2,4,6,8,10,12,14,16,18,20,22,24,26,28,30,32,34,36,38,40,42,44,46,48,..., dimensions={0} | all-to-all | bytes 524288 | tf_op jit(solution)/shard_map/all_to_all | solution.py:341
  63.4 2.8 %copy-done.3 = f32[64,3,64,128]{3,2,1,0:T(8,128)S(1)} copy-done((f32[64,3,64,128]{3,2,1,0:T(8,128)S(1)}, f32[64,3,64,128]{3,2,1,0:T(8,128)}, u32[]{:S(2)}) %copy-start.3) | copy-done | bytes 6291480
  66.2 9.7 %shard_map.157 = (f32[12288,128]{1,0:T(8,128)S(1)}, f32[3072,128]{1,0:T(8,128)S(1)}) custom-call(f32[12288,128]{1,0:T(8,128)S(1)} %bitcast.50, f32[3072,128]{1,0:T(8,128)S(1)} %bitcast.56), custom_call_target="tpu_custom_call" | custom-call | tf_op jit(solution)/shard_map/pallas_call | solution.py:414
  75.9 2.7 %copy-done = f32[12288,128]{1,0:T(8,128)} copy-done((f32[12288,128]{1,0:T(8,128)}, f32[12288,128]{1,0:T(8,128)S(1)}, u32[]{:S(2)}) %copy-start) | copy-done | bytes 6291480
  79.9 2.8 %copy-done.1 = f32[12288,128]{1,0:T(8,128)S(1)} copy-done((f32[12288,128]{1,0:T(8,128)S(1)}, f32[12288,128]{1,0:T(8,128)}, u32[]{:S(2)}) %copy-start.1) | copy-done | bytes 6291480
  83.7 2.0 shard_map.161
  88.3 3.3 %collective-permute-done.4.arriving = f32[16,128]{1,0:T(8,128)S(1)} collective-permute-done((f32[16,128]{1,0:T(8,128)S(1)}, f32[16,128]{1,0:T(8,128)S(1)}, u32[]{:S(2)}, u32[]{:S(2)}) %collective-permute-start.4) | collective-permute-done | bytes 8224 | tf_op jit(solution)/shard_map/ppermute | solution.py:48
  94.6 17.0 %all_to_all.37.received = f32[32,16,128]{2,1,0:T(8,128)S(1)} all-to-all(f32[32,16,128]{2,1,0:T(8,128)S(1)} %add.68), channel_id=1, replica_groups={{0,2,4,6,8,10,12,14,16,18,20,22,24,26,28,30,32,34,36,38,40,42,44,46,48,..., dimensions={0} | all-to-all | bytes 524288 | tf_op jit(solution)/shard_map/all_to_all | solution.py:341
  111.7 18.9 %all_to_all.38 = f32[32,24,128]{2,1,0:T(8,128)S(1)} all-to-all(f32[32,24,128]{2,1,0:T(8,128)S(1)} %get-tuple-element.57), channel_id=1, replica_groups={{0,2,4,6,8,10,12,14,16,18,20,22,24,26,28,30,32,34,36,38,40,42,44,46,48,..., dimensions={0} | all-to-all | bytes 786432 | tf_op jit(solution)/shard_map/all_to_all | solution.py:341
  130.6 1.7 collective-permute-done.6
  135.1 2.0 shard_map.168
  142.2 2.9 %collective-permute-done.10.arriving = f32[16,128]{1,0:T(8,128)S(1)} collective-permute-done((f32[16,128]{1,0:T(8,128)S(1)}, f32[16,128]{1,0:T(8,128)S(1)}, u32[]{:S(2)}, u32[]{:S(2)}) %collective-permute-start.10) | collective-permute-done | bytes 8224 | tf_op jit(solution)/shard_map/ppermute | solution.py:48
  148.1 17.1 %all_to_all.39.received = f32[32,16,128]{2,1,0:T(8,128)S(1)} all-to-all(f32[32,16,128]{2,1,0:T(8,128)S(1)} %add.69), channel_id=1, replica_groups={{0,2,4,6,8,10,12,14,16,18,20,22,24,26,28,30,32,34,36,38,40,42,44,46,48,..., dimensions={0} | all-to-all | bytes 524288 | tf_op jit(solution)/shard_map/all_to_all | solution.py:341
  165.8 18.9 %all_to_all.40 = f32[32,24,128]{2,1,0:T(8,128)S(1)} all-to-all(f32[32,24,128]{2,1,0:T(8,128)S(1)} %get-tuple-element.71), channel_id=1, replica_groups={{0,2,4,6,8,10,12,14,16,18,20,22,24,26,28,30,32,34,36,38,40,42,44,46,48,..., dimensions={0} | all-to-all | bytes 786432 | tf_op jit(solution)/shard_map/all_to_all | solution.py:341
  184.7 1.7 collective-permute-done.12
  189.3 2.0 shard_map.174
  191.3 1.8 collective-permute-done.14.refs_2_
  196.7 3.1 %collective-permute-done.16.arriving = f32[16,128]{1,0:T(8,128)S(1)} collective-permute-done((f32[16,128]{1,0:T(8,128)S(1)}, f32[16,128]{1,0:T(8,128)S(1)}, u32[]{:S(2)}, u32[]{:S(2)}) %collective-permute-start.16) | collective-permute-done | bytes 8224 | tf_op jit(solution)/shard_map/ppermute | solution.py:48
  203.5 4.7 %all-to-all-start.6 = ((f32[32,16,128]{2,1,0:T(8,128)}), f32[32,16,128]{2,1,0:T(8,128)S(1)}, u32[]{:S(2)}, u32[]{:S(2)}) async-start(f32[32,16,128]{2,1,0:T(8,128)} %add.70), calls=%async_computation.6 | async-start | bytes 524288 | tf_op jit(solution)/shard_map/all_to_all | solution.py:341
  209.9 10.9 %all-to-all-done.6 = f32[32,16,128]{2,1,0:T(8,128)S(1)} async-done(((f32[32,16,128]{2,1,0:T(8,128)}), f32[32,16,128]{2,1,0:T(8,128)S(1)}, u32[]{:S(2)}, u32[]{:S(2)}) %all-to-all-start.6) | async-done | bytes 262176 | tf_op jit(solution)/shard_map/all_to_all | solution.py:341
  (118 shorter events, 44.1 us)
Async XLA Ops:
  0.6 62.7 %copy-start.11 = (f32[16,192]{1,0:T(8,128)S(1)}, f32[16,192]{1,0:T(8,128)}, u32[]{:S(2)}) copy-start(f32[16,192]{1,0:T(8,128)} %fwarm.1) | copy-start | bytes 36868
  0.7 57.9 %copy-start.14 = (f32[8]{0:T(128)S(1)}, f32[8]{0:T(128)}, u32[]{:S(2)}) copy-start(f32[8]{0:T(128)} %param.26) | copy-start | bytes 100
  0.7 57.8 %copy-start.12 = (s32[64,64]{1,0:T(8,128)S(1)}, s32[64,64]{1,0:T(8,128)}, u32[]{:S(2)}) copy-start(s32[64,64]{1,0:T(8,128)} %param.16) | copy-start | bytes 49156
  0.7 62.4 %copy-start.13 = (s32[16,64]{1,0:T(8,128)S(1)}, s32[16,64]{1,0:T(8,128)}, u32[]{:S(2)}) copy-start(s32[16,64]{1,0:T(8,128)} %param.21) | copy-start | bytes 12292
  7.3 56.1 %copy-start.5 = (f32[16,3,64,128]{3,2,1,0:T(8,128)S(1)}, f32[16,3,64,128]{3,2,1,0:T(8,128)}, u32[]{:S(2)}) copy-start(f32[16,3,64,128]{3,2,1,0:T(8,128)} %param.18) | copy-start | bytes 4718596
  10.5 4.9 %collective-permute-start = (f32[16,128]{1,0:T(8,128)S(1)}, f32[16,128]{1,0:T(8,128)S(1)}, u32[]{:S(2)}, u32[]{:S(2)}) collective-permute-start(f32[16,128]{1,0:T(8,128)S(1)} %slice.21.fterms), channel_id=1, source_target_pairs={{0,64},{64,128},{128,192},{192,0},{1,65},{65,129},{129,193},{193,1... | collective-permute-start | bytes 24584 | tf_op jit(solution)/shard_map/ppermute | solution.py:48
  16.9 1.6 collective-permute-start.1
  58.5 1.5 collective-permute-start.2
  61.5 24.2 %collective-permute-start.3 = (f32[16,128]{1,0:T(8,128)S(1)}, f32[16,128]{1,0:T(8,128)S(1)}, u32[]{:S(2)}, u32[]{:S(2)}) collective-permute-start(f32[16,128]{1,0:T(8,128)S(1)} %shard_map.162), channel_id=1, source_target_pairs={{0,192},{64,0},{128,64},{192,128},{1,193},{65,1},{129,65},{193,129... | collective-permute-start | bytes 24584 | tf_op jit(solution)/shard_map/ppermute | solution.py:48
  86.5 5.1 %collective-permute-start.4 = (f32[16,128]{1,0:T(8,128)S(1)}, f32[16,128]{1,0:T(8,128)S(1)}, u32[]{:S(2)}, u32[]{:S(2)}) collective-permute-start(f32[16,128]{1,0:T(8,128)S(1)} %get-tuple-element.52.fterms), channel_id=1, source_target_pairs={{0,64},{64,128},{128,192},{192,0},{1,65},{65,129},{129,193},{193,1... | collective-permute-start | bytes 24584 | tf_op jit(solution)/shard_map/ppermute | solution.py:48
  93.0 1.6 collective-permute-start.5
  130.6 1.7 collective-permute-start.6
  133.1 6.3 %collective-permute-start.9 = (f32[24,128]{1,0:T(8,128)S(1)}, f32[24,128]{1,0:T(8,128)S(1)}, u32[]{:S(2)}, u32[]{:S(2)}) collective-permute-start(f32[24,128]{1,0:T(8,128)S(1)} %get-tuple-element.61), channel_id=1, source_target_pairs={{0,192},{64,0},{128,64},{192,128},{1,193},{65,1},{129,65},{193,129... | collective-permute-start | bytes 36872 | tf_op jit(solution)/shard_map/ppermute | solution.py:48
  133.1 5.2 %collective-permute-start.8 = (f32[8,128]{1,0:T(8,128)S(1)}, f32[8,128]{1,0:T(8,128)S(1)}, u32[]{:S(2)}, u32[]{:S(2)}) collective-permute-start(f32[8,128]{1,0:T(8,128)S(1)} %get-tuple-element.58.refs_0_), channel_id=1, source_target_pairs={{0,128},{64,192},{128,0},{192,64},{1,129},{65,193},{129,1},{193,65... | collective-permute-start | bytes 12296 | tf_op jit(solution)/shard_map/ppermute | solution.py:48
  134.4 5.0 %collective-permute-start.7 = (f32[8,128]{1,0:T(8,128)S(1)}, f32[8,128]{1,0:T(8,128)S(1)}, u32[]{:S(2)}, u32[]{:S(2)}) collective-permute-start(f32[8,128]{1,0:T(8,128)S(1)} %get-tuple-element.58.refs_0_), channel_id=1, source_target_pairs={{0,64},{64,128},{128,192},{192,0},{1,65},{65,129},{129,193},{193,1... | collective-permute-start | bytes 12296 | tf_op jit(solution)/shard_map/ppermute | solution.py:48
  140.1 4.9 %collective-permute-start.10 = (f32[16,128]{1,0:T(8,128)S(1)}, f32[16,128]{1,0:T(8,128)S(1)}, u32[]{:S(2)}, u32[]{:S(2)}) collective-permute-start(f32[16,128]{1,0:T(8,128)S(1)} %get-tuple-element.66.fterms), channel_id=1, source_target_pairs={{0,64},{64,128},{128,192},{192,0},{1,65},{65,129},{129,193},{193,1... | collective-permute-start | bytes 24584 | tf_op jit(solution)/shard_map/ppermute | solution.py:48
  146.4 1.6 collective-permute-start.11
  184.7 1.7 collective-permute-start.12
  187.1 6.6 %collective-permute-start.15 = (f32[24,128]{1,0:T(8,128)S(1)}, f32[24,128]{1,0:T(8,128)S(1)}, u32[]{:S(2)}, u32[]{:S(2)}) collective-permute-start(f32[24,128]{1,0:T(8,128)S(1)} %get-tuple-element.75), channel_id=1, source_target_pairs={{0,192},{64,0},{128,64},{192,128},{1,193},{65,1},{129,65},{193,129... | collective-permute-start | bytes 36872 | tf_op jit(solution)/shard_map/ppermute | solution.py:48
  187.9 5.1 %collective-permute-start.14 = (f32[8,128]{1,0:T(8,128)S(1)}, f32[8,128]{1,0:T(8,128)S(1)}, u32[]{:S(2)}, u32[]{:S(2)}) collective-permute-start(f32[8,128]{1,0:T(8,128)S(1)} %get-tuple-element.72.refs_0_), channel_id=1, source_target_pairs={{0,128},{64,192},{128,0},{192,64},{1,129},{65,193},{129,1},{193,65... | collective-permute-start | bytes 12296 | tf_op jit(solution)/shard_map/ppermute | solution.py:48
  188.8 4.8 %collective-permute-start.13 = (f32[8,128]{1,0:T(8,128)S(1)}, f32[8,128]{1,0:T(8,128)S(1)}, u32[]{:S(2)}, u32[]{:S(2)}) collective-permute-start(f32[8,128]{1,0:T(8,128)S(1)} %get-tuple-element.72.refs_0_), channel_id=1, source_target_pairs={{0,64},{64,128},{128,192},{192,0},{1,65},{65,129},{129,193},{193,1... | collective-permute-start | bytes 12296 | tf_op jit(solution)/shard_map/ppermute | solution.py:48
  194.9 4.9 %collective-permute-start.16 = (f32[16,128]{1,0:T(8,128)S(1)}, f32[16,128]{1,0:T(8,128)S(1)}, u32[]{:S(2)}, u32[]{:S(2)}) collective-permute-start(f32[16,128]{1,0:T(8,128)S(1)} %get-tuple-element.82.fterms), channel_id=1, source_target_pairs={{0,64},{64,128},{128,192},{192,0},{1,65},{65,129},{129,193},{193,1... | collective-permute-start | bytes 24584 | tf_op jit(solution)/shard_map/ppermute | solution.py:48
  201.2 1.6 collective-permute-start.17
  203.5 17.3 %all-to-all-start.6 = ((f32[32,16,128]{2,1,0:T(8,128)}), f32[32,16,128]{2,1,0:T(8,128)S(1)}, u32[]{:S(2)}, u32[]{:S(2)}) async-start(f32[32,16,128]{2,1,0:T(8,128)} %add.70), calls=%async_computation.6 | async-start | bytes 524288 | tf_op jit(solution)/shard_map/all_to_all | solution.py:341
  (13 other events, 132.4 us)

commit v2 on v1

--- a/solution.py
+++ b/solution.py
@@ -14,6 +14,7 @@
 NY, NZ, NC = 4, 8, 2
 CHIPS = NY * NZ
 OWN = 16
+STRIP = NY * OWN
 
 KC, KF = 64, 16
 GC, GF = 128 // KC, 128 // KF
@@ -32,14 +33,15 @@
     return jax.ShapeDtypeStruct(dims, f32)
 
 
-def kernel_call(body, out, specs, scratch=(), megabytes=4, out_specs=None):
+def kernel_call(body, out, specs, scratch=(), megabytes=4, cost=None):
     return pl.pallas_call(
         body,
         out_shape=out,
         in_specs=specs,
-        out_specs=out_specs or jax.tree.map(lambda _: vmem, out),
+        out_specs=jax.tree.map(lambda _: vmem, out),
         scratch_shapes=list(scratch),
         compiler_params=pltpu.CompilerParams(vmem_limit_bytes=megabytes << 20),
+        cost_estimate=cost,
     )
 
 
@@ -88,11 +90,11 @@
     return pl.ds(pl.multiple_of(slice_at * 128, 128), 128)
 
 
-def accumulate(jac, y, first, count, total):
+def accumulate(jac, y, slices):
     def add(s, total):
         return total + jac[rows_of(s), :] * y[pl.ds(s, 1), :]
 
-    return lax.fori_loop(first, first + count, add, total, unroll=4)
+    return lax.fori_loop(0, slices, add, jnp.zeros((128, 128), f32), unroll=4)
 
 
 def folded(total, parts):
@@ -101,7 +103,7 @@
     return sum(turned[p * k : (p + 1) * k] for p in range(parts))
 
 
-def product(jac, velocity, partial, first, count):
+def product(jac, velocity, partial, slices):
     def one(s, _):
         terms = jac[rows_of(s), :] * velocity
         partial[pl.ds(pl.multiple_of(s * 8, 8), 8), :] = jnp.sum(
@@ -109,10 +111,7 @@
         )
         return _
 
-    lax.fori_loop(first, first + count, one, 0, unroll=4)
-
-
-def summed(partial, slices):
+    lax.fori_loop(0, slices, one, 0, unroll=4)
     return sum(partial[pl.ds(q, slices, stride=8), :] for q in range(8))
 
 
@@ -149,13 +148,13 @@
     terms[...] = sum(partial[pl.ds(q, KC + KF, stride=8), :] for q in range(8))
 
 
-def layout_kernel(cjac, fjac, cout, fout, cbuf, fbuf, cturn, fturn, sems, outs):
+def layout_kernel(cjac, fjac, after, cout, fout, done, cbuf, fbuf, sems):
     copies = [pltpu.make_async_copy(fjac, fbuf, sems.at[0])]
     copies.append(pltpu.make_async_copy(cjac, cbuf, sems.at[1]))
     for copy in copies:
         copy.start()
 
-    def turn(jac, out, parts, depth, first, count):
+    def turn(jac, out, parts, depth, slices):
         k = 128 // parts
 
         def one(s, _):
@@ -166,50 +165,17 @@
             out[rows_of(s), :] = jnp.concatenate(rows, 0).T
             return _
 
-        lax.fori_loop(first, first + count, one, 0, unroll=8)
+        lax.fori_loop(0, slices, one, 0, unroll=8)
 
     copies[0].wait()
-    turn(fbuf, fturn, GF, IF, 0, SF)
-    leaving = [pltpu.make_async_copy(fturn, fout, outs.at[0])]
-    leaving[0].start()
+    turn(fbuf, fout, GF, IF, SF)
     copies[1].wait()
-    for part in range(4):
-        share = SC // 4
-        turn(cbuf, cturn, GC, IC, part * share, share)
-        rows = pl.ds(part * share * 128, share * 128)
-        copy = pltpu.make_async_copy(cturn.at[rows], cout.at[rows], outs.at[part + 1])
-        copy.start()
-        leaving.append(copy)
-    for copy in leaving:
-        copy.wait()
-
-
-def streamed(jac, buf, sems, slices, work, ahead):
-    parts = sems.shape[0]
-    share = slices // parts
-    copies = []
-    for p in range(parts):
-        rows = pl.ds(p * share * 128, share * 128)
-        copies.append(pltpu.make_async_copy(jac.at[rows], buf.at[rows], sems.at[p]))
-    for copy in copies:
-        copy.start()
-    carry = ahead()
-    for p, copy in enumerate(copies):
-        copy.wait()
-        carry = work(p * share, share, carry)
-    return carry
-
-
-def force_kernel(jac, y, terms, buf, sems):
-    total = streamed(
-        jac,
-        buf,
-        sems,
-        SC,
-        lambda first, count, total: accumulate(buf, y, first, count, total),
-        lambda: jnp.zeros((128, 128), f32),
-    )
-    terms[...] = folded(total, GC)
+    turn(cbuf, cout, GC, IC, SC)
+    done[...] = jnp.zeros_like(done)
+
+
+def force_kernel(jac, y, terms):
+    terms[...] = folded(accumulate(jac, y, SC), GC)
 
 
 def scatter_kernel(rows, swap, cterms, fterms, arriving, own, other, total, wide):
@@ -230,16 +196,20 @@
     other[...] = total[half:, :].reshape(other.shape)
 
 
-def owner_kernel(with_sums, received, free, mass, last, spread, owned, pieces):
-    total = jnp.sum(received[...], 0)
-    owned[...] = total
-    piece = free[...] + mass[...] * total
+def strip_kernel(received, spread, after, strip):
+    strip[0:STRIP, :] = jnp.sum(received[...], 0)
+    strip[STRIP:, :] = jnp.broadcast_to(jnp.sum(spread[...]), (8, 128))
+
+
+def owner_kernel(with_sums, s0, s1, s2, s3, free, mass, last, total, pieces):
+    both = s0[...] + s1[...] + s2[...] + s3[...]
+    total[...] = both[0:STRIP]
+    piece = free[...] + mass[...] * both[0:STRIP]
     if with_sums:
-        change = total - last[...]
+        change = both[0:STRIP] - last[...]
         curve = jnp.sum(mass[...] * change * change)
         row = lax.broadcasted_iota(jnp.int32, (8, 128), 0)
-        sums = jnp.where(row == 0, jnp.sum(spread[...]), curve)
-        piece = jnp.concatenate([piece, sums], 0)
+        piece = jnp.concatenate([piece, jnp.where(row == 0, both[STRIP:], curve)], 0)
     pieces[...] = jnp.broadcast_to(piece, pieces.shape)
 
 
@@ -248,30 +218,22 @@
     picked = jnp.concatenate([panel[pl.ds(rows[base + m], 1), :] for m in range(KF)], 0)
     far[0:KF, :] = jnp.where(swap[base:, :] > 0, pltpu.roll(picked, BLK, 1), picked)
     if with_sums:
-        size = OWN + 8
-        total = sum(
-            panel[p * size + OWN : (p + 1) * size, :] for p in range(NC * CHIPS)
-        )
+        size = STRIP + 8
+        total = sum(panel[p * size + STRIP : (p + 1) * size, :] for p in range(NC * NZ))
         sums[0][...] = total
         far[KF:, :] = total
 
 
-def gradient_kernel(rows, swap, panel, jac, y, live, grad, fown, picked, partial, buf, sems):
-    def ahead():
-        for m in range(2 * KC + KF):
-            picked[m : m + 1, :] = panel[pl.ds(rows[m], 1), :]
-        x = picked[...]
-        x = jnp.where(swap[0 : 2 * KC + KF, :] > 0, pltpu.roll(x, BLK, 1), x)
-        fown[...] = x[2 * KC :]
-        joined = jnp.where(left_half(KC), x[0:KC], x[KC : 2 * KC])
-        return jnp.concatenate([joined] * GC, 0).T
-
-    def work(first, count, velocity):
-        product(buf, velocity, partial, first, count)
-        return velocity
-
-    streamed(jac, buf, sems, SC, work, ahead)
-    grad[...] = (summed(partial, SC) + regular_weight * y[...]) * live[...]
+def gradient_kernel(rows, swap, panel, jac, y, live, grad, fown, picked, partial):
+    for m in range(2 * KC + KF):
+        picked[m : m + 1, :] = panel[pl.ds(rows[m], 1), :]
+    x = picked[...]
+    x = jnp.where(swap[0 : 2 * KC + KF, :] > 0, pltpu.roll(x, BLK, 1), x)
+    fown[...] = x[2 * KC :]
+    joined = jnp.where(left_half(KC), x[0:KC], x[KC : 2 * KC])
+    velocity = jnp.concatenate([joined] * GC, 0).T
+    raw = product(jac, velocity, partial, SC)
+    grad[...] = (raw + regular_weight * y[...]) * live[...]
 
 
 def cone(pushed, friction):
@@ -291,18 +253,10 @@
     first, beta, last, *refs
 ):
     (s0, s1, s2, grad, fown, far, jac, cy, fy, cnow, fnow, live, cfric, ffric) = refs[:14]
-    (cnew, fnew, cnext, fnext, spread, fterms, partial, buf, sems) = refs[14:]
-
-    def ahead():
-        joined = jnp.where(left_half(KF), fown[...], far[0:KF, :])
-        return jnp.concatenate([joined] * GF, 0).T
-
-    def work(first_slice, count, velocity):
-        product(buf, velocity, partial, first_slice, count)
-        return velocity
-
-    streamed(jac, buf, sems, SF, work, ahead)
-    fgrad = summed(partial, SF) + regular_weight * fy[...]
+    (cnew, fnew, cnext, fnext, spread, fterms, partial) = refs[14:]
+    joined = jnp.where(left_half(KF), fown[...], far[0:KF, :])
+    velocity = jnp.concatenate([joined] * GF, 0).T
+    fgrad = product(jac, velocity, partial, SF) + regular_weight * fy[...]
     if first:
         step = s0[...]
     else:
@@ -332,12 +286,20 @@
         spread[...] = jnp.sum((cmove * cmove).reshape(SC // 8, 8, 128), 0) + jnp.sum(
             (fmove * fmove).reshape(SF // 8, 8, 128), 0
         )
-    total = accumulate(buf, fnext, 0, SF, jnp.zeros((128, 128), f32))
-    fterms[...] = folded(total, GF)
+    fterms[...] = folded(accumulate(jac, fnext, SF), GF)
+
+
+def along_y(x, by):
+    line = NZ * NC
+    return lax.ppermute(
+        x, "grp", [(i, (i + by * line) % (NY * line)) for i in range(NY * line)]
+    )
 
 
 def exchange(parts):
-    groups = [[chip * NC + core for chip in range(CHIPS)] for core in range(NC)]
+    groups = [
+        [(y * NZ + z) * NC + core for z in range(NZ)] for y in range(NY) for core in range(NC)
+    ]
     return lax.all_to_all(parts, "grp", 0, 0, axis_index_groups=groups, tiled=True)
 
 
@@ -371,10 +333,19 @@
         [contact_bodies[:, 0], contact_bodies[:, 1], face_own, face_far]
     )
     owner = targets // (2 * OWN)
-    slot = (owner - lax.axis_index("grp")) % NC * CHIPS + owner // NC
-    row = targets % (2 * OWN) // 2
-    sum_rows = slot * OWN + row
-    panel_rows = [slot * OWN + row] + [slot * (OWN + 8) + row] * (ITERS - 1)
+    me = lax.axis_index("grp")
+    slot = (owner - me) % NC * NZ + owner // NC % NZ
+    row = owner // (NC * NZ) * OWN + targets % (2 * OWN) // 2
+    sum_rows = slot * STRIP + row
+    panel_rows = [slot * STRIP + row] + [slot * (STRIP + 8) + row] * (ITERS - 1)
+    my_y = me // (NC * NZ)
+
+    def strip_of(x):
+        parts = jnp.stack([x] + [along_y(x, by) for by in range(1, NY)])
+        return parts[(my_y - jnp.arange(NY)) % NY].reshape(-1, x.shape[-1])
+
+    constants = strip_of(jnp.concatenate([free_own, mass_own], 1))
+    free_strip, mass_strip = constants[:, :128], constants[:, 128:]
     order = jnp.arange(targets.shape[0])
     right = ((order >= KC) & (order < 2 * KC)) | (order >= 2 * KC + KF)
     swap = jnp.broadcast_to(
@@ -383,14 +354,14 @@
     cfric = to_lanes(class_lookup(contact_class, friction_table), GC)
     ffric = to_lanes(class_lookup(face_class, friction_table), GF)
 
-    def reduced(cterms, fterms, arriving):
+    def core_half(cterms, fterms, arriving):
         halves = kernel_call(
             scatter_kernel,
-            (shape(CHIPS, OWN, 128), shape(CHIPS, OWN, 128)),
+            (shape(NZ, STRIP, 128), shape(NZ, STRIP, 128)),
             [smem] + [vmem] * 4,
             [pltpu.VMEM((NC * CHIPS * OWN, 128), f32), pltpu.VMEM((2 * KC + 2 * KF, 128), f32)],
         )(sum_rows, swap, cterms, fterms, arriving)
-        return exchange(halves[0] + other_core(halves[1]))
+        return halves[0] + other_core(halves[1])
 
     betas = momentum_weights(ITERS)
     cwarm = warm_contact * live[0, :KC, None]
@@ -407,31 +378,37 @@
             pltpu.SemaphoreType.DMA((4,)),
             pltpu.SemaphoreType.DMA,
         ],
-        16,
+        60,
     )(crows, frows, cwarm, warm_face)
     cterms, fterms = terms[:KC], terms[KC:]
     arriving = shifted(fterms, "slab", 1)
-    cjac, fjac = kernel_call(
-        layout_kernel,
-        (shape(SC * 128, 128), shape(SF * 128, 128)),
-        [hbm, hbm],
-        [cbuf, fbuf, cbuf, fbuf, pltpu.SemaphoreType.DMA((2,)), pltpu.SemaphoreType.DMA((5,))],
-        24,
-        (hbm, hbm),
-    )(crows, frows)
     cnow = to_lanes(cwarm, GC)
     fnow = to_lanes(warm_face, GF)
     cy, fy = cnow, fnow
     spread = jnp.zeros((8, 128), f32)
-    owned = free_own
+    total = free_strip
     for turn in range(ITERS):
-        received = reduced(cterms, fterms, arriving)
+        half = core_half(cterms, fterms, arriving)
+        received = exchange(half)
+        if turn == 0:
+            cjac, fjac, done = kernel_call(
+                layout_kernel,
+                (shape(SC * 128, 128), shape(SF * 128, 128), shape(8, 128)),
+                [hbm, hbm, vmem],
+                [cbuf, fbuf, pltpu.SemaphoreType.DMA((2,))],
+                20,
+                pl.CostEstimate(flops=0, bytes_accessed=40 << 20, transcendentals=0),
+            )(crows, frows, half)
+        strip = kernel_call(strip_kernel, shape(STRIP + 8, 128), [vmem] * 3)(
+            received, spread, done
+        )
+        strips = [strip] + [along_y(strip, by) for by in range(1, NY)]
         extra = 8 if turn > 0 else 0
-        owned, pieces = kernel_call(
+        total, pieces = kernel_call(
             functools.partial(owner_kernel, turn > 0),
-            (shape(OWN, 128), shape(CHIPS, OWN + extra, 128)),
-            [vmem] * 5,
-        )(received, free_own, mass_own, owned, spread)
+            (shape(STRIP, 128), shape(NZ, STRIP + extra, 128)),
+            [vmem] * 7,
+        )(*strips, free_strip, mass_strip, total)
         panel = all_gather(pieces)
         picked = kernel_call(
             functools.partial(far_kernel, turn > 0),
@@ -446,14 +423,8 @@
         grad, fown = kernel_call(
             gradient_kernel,
             (shape(SC, 128), shape(KF, 128)),
-            [smem, vmem, vmem, hbm, vmem, vmem],
-            [
-                pltpu.VMEM((2 * KC + KF, 128), f32),
-                pltpu.VMEM((SC * 8, 128), f32),
-                cbuf,
-                pltpu.SemaphoreType.DMA((6,)),
-            ],
-            16,
+            [smem] + [vmem] * 5,
+            [pltpu.VMEM((2 * KC + KF, 128), f32), pltpu.VMEM((SC * 8, 128), f32)],
         )(panel_rows[turn], swap, panel, cjac, cy, live)
         body = functools.partial(update_kernel, turn == 0, betas[turn], turn == ITERS - 1)
         cnow, fnow, cy, fy, spread, fterms = kernel_call(
@@ -466,19 +437,19 @@
                 shape(8, 128),
                 shape(KF, 128),
             ),
-            [vmem] * 6 + [hbm] + [vmem] * 7,
-            [pltpu.VMEM((SF * 8, 128), f32), fbuf, pltpu.SemaphoreType.DMA((2,))],
+            [vmem] * 14,
+            [pltpu.VMEM((SF * 8, 128), f32)],
         )(*steps, grad, fown, returning, fjac, cy, fy, cnow, fnow, live, cfric, ffric)
         arriving = shifted(fterms, "slab", 1)
-        cterms = kernel_call(
-            force_kernel,
-            shape(KC, 128),
-            [hbm, vmem],
-            [cbuf, pltpu.SemaphoreType.DMA((6,))],
-            16,
-        )(cjac, cy)
-    received = reduced(cterms, fterms, arriving)
-    final = free_own + mass_own * jnp.sum(received, 0)
+        cterms = kernel_call(force_kernel, shape(KC, 128), [vmem] * 2)(cjac, cy)
+    received = exchange(core_half(cterms, fterms, arriving))
+    strip = jnp.sum(received, 0).reshape(NY, OWN, 128)
+
+    def block_at(by):
+        return lax.dynamic_index_in_dim(strip, (my_y + by) % NY, 0, keepdims=False)
+
+    owned = block_at(0) + sum(along_y(block_at(by), by) for by in range(1, NY))
+    final = free_own + mass_own * owned
     return (from_lanes(cnow, GC), from_lanes(fnow, GF), final.reshape(-1))
 
 

time: 222 us -> 233 us (1.050)
  blocking collectives: 112 us -> 73.7 us
  starting transfers between devices: 14.8 us -> 43.2 us
  waiting for transfers between devices: 39 us -> 58.5 us
  local copies, waits for them, and re-layouts: 17.6 us -> 14.1 us
    all_to_all x6 -> x5, blocking collectives: 112 us -> 73.7 us  [exchange(): lax.all_to_all(parts, 'grp', 0, 0, axis_index_groups=groups, tiled=True)]
    ppermute x0 -> x15, starting transfers between devices: none -> 21.6 us  [along_y(): lax.ppermute(x, 'grp', [(i, (i + by * line) % (NY * line)) for i in range...]
    ppermute x0 -> x15, waiting for transfers between devices: none -> 14.9 us  [along_y(): lax.ppermute(x, 'grp', [(i, (i + by * line) % (NY * line)) for i in range...]
    all_to_all x1 -> x2, starting transfers between devices: 4.67 us -> 13.3 us  [exchange(): lax.all_to_all(parts, 'grp', 0, 0, axis_index_groups=groups, tiled=True)]
    unnamed x39, local copies, waits for them, and re-layouts: 16.5 us -> 11 us
    ppermute x11, waiting for transfers between devices: 17.1 us -> 21.9 us  [shifted(): lax.ppermute(x, axis, [(i, (i + by) % devices) for i in range(devices)])]
    pallas_call x1, Pallas kernels: 3.17 us -> 6.83 us  [on_device(): kernel_call(first_force_kernel, shape(KC + KF, 128), [hbm, hbm, vmem, vme...]
    pallas_call x14 -> x17, Pallas kernels: 25.4 us -> 23 us  [the longest x1 9.95 us: on_device(): kernel_call(layout_kernel, (shape(SC * 128, 128), shape(SF * 128, 128), s...]
  transfers between devices with their start and end apart: 19 -> 35, of which waited for: 16 -> 29; matrix products, arithmetic and copies ran while one was open for 1% -> 2% of each run, Pallas kernels for 9% -> 7%
where the time goes in v2:
time: 233 us; the launch traced here: 230 us
  blocking collectives  73.7 us (32%)
  waiting for transfers between devices  58.5 us (25%)
  starting transfers between devices  43.2 us (19%)
  Pallas kernels  33.8 us (15%)
  local copies, waits for them, and re-layouts  14.1 us (6%)
  other arithmetic  4.27 us (2%)
  between operations  2.57 us (1%)
    all_to_all x5, blocking collectives, exchange(): lax.all_to_all(parts, 'grp', 0, 0, axis_index_groups=groups, tiled=True)  73.7 us
    ppermute x11, waiting for transfers between devices, shifted(): lax.ppermute(x, axis, [(i, (i + by) % devices) for i in range(devices)])  21.9 us
    ppermute x15, starting transfers between devices, along_y(): lax.ppermute(x, 'grp', [(i, (i + by * line) % (NY * line)) for i in range...  21.6 us
    ppermute x15, waiting for transfers between devices, along_y(): lax.ppermute(x, 'grp', [(i, (i + by * line) % (NY * line)) for i in range...  14.9 us
    all_to_all x2, starting transfers between devices, exchange(): lax.all_to_all(parts, 'grp', 0, 0, axis_index_groups=groups, tiled=True)  13.3 us
    all_to_all x2, waiting for transfers between devices, exchange(): lax.all_to_all(parts, 'grp', 0, 0, axis_index_groups=groups, tiled=True)  11 us
    unnamed x39, local copies, waits for them, and re-layouts  11 us
    ppermute x7, waiting for transfers between devices, other_core(): return lax.ppermute(x, 'grp', [(i, i ^ 1) for i in range(devices)])  10.6 us
  transfers between devices with their start and end apart: 35, of which 29 were waited for; matrix products, arithmetic and copies ran while one was open for 2% of the time, Pallas kernels for 7%

profile of v2, /device:TPU:32, one launch (start us, length us, event | category | flops | bytes accessed | tf_op | source)
XLA Modules:
  0.0 230.2 jit_solution(9488756049492012019)
XLA Ops:
  3.0 6.8 %shard_map.157 = f32[80,128]{1,0:T(8,128)} custom-call(f32[12288,128]{1,0:T(8,128)} %bitcast.74, f32[3072,128]{1,0:T(8,128)} %bitcast.76, f32[64,192]{1,0:T(8,128)} %broadcast_multiply_fusion.cwarm, f32[16,192]{1,0:T(8,128)} %fwarm.1), custom_call_target="tpu_custom_call" | custom-call | tf_op jit(solution)/shard_map/pallas_call | solution.py:370
  13.0 2.5 %collective-permute-done.arriving = f32[16,128]{1,0:T(8,128)S(1)} collective-permute-done((f32[16,128]{1,0:T(8,128)S(1)}, f32[16,128]{1,0:T(8,128)S(1)}, u32[]{:S(2)}, u32[]{:S(2)}) %collective-permute-start) | collective-permute-done | bytes 8224 | tf_op jit(solution)/shard_map/ppermute | solution.py:50
  19.3 8.6 %all-to-all-start = ((f32[8,64,128]{2,1,0:T(8,128)}), f32[8,64,128]{2,1,0:T(8,128)S(1)}, u32[]{:S(2)}, u32[]{:S(2)}) async-start(f32[8,64,128]{2,1,0:T(8,128)} %add.144.after), calls=%async_computation | async-start | bytes 524288 | tf_op jit(solution)/shard_map/all_to_all | solution.py:303
  27.9 3.1 %collective-permute-start.7 = (f32[16,256]{1,0:T(8,128)S(1)}, f32[16,256]{1,0:T(8,128)S(1)}, u32[]{:S(2)}, u32[]{:S(2)}) collective-permute-start(f32[16,256]{1,0:T(8,128)S(1)} %get-tuple-element.104), channel_id=1, source_target_pairs={{0,48},{1,49},{2,50},{3,51},{4,52},{5,53},{6,54},{7,55},{8,56},{9,... | collective-permute-start | bytes 49160 | tf_op jit(solution)/shard_map/ppermute | solution.py:294
  32.6 3.6 %collective-permute-done.6 = f32[16,256]{1,0:T(8,128)S(1)} collective-permute-done((f32[16,256]{1,0:T(8,128)S(1)}, f32[16,256]{1,0:T(8,128)S(1)}, u32[]{:S(2)}, u32[]{:S(2)}) %collective-permute-start.6) | collective-permute-done | bytes 16416 | tf_op jit(solution)/shard_map/ppermute | solution.py:294
  37.2 2.8 %copy-done.2 = f32[64,3,64,128]{3,2,1,0:T(8,128)S(1)} copy-done((f32[64,3,64,128]{3,2,1,0:T(8,128)S(1)}, f32[64,3,64,128]{3,2,1,0:T(8,128)}, u32[]{:S(2)}) %copy-start.2) | copy-done | bytes 6291480
  39.9 9.9 %shard_map.159 = (f32[12288,128]{1,0:T(8,128)S(1)}, f32[3072,128]{1,0:T(8,128)S(1)}, f32[8,128]{1,0:T(8,128)S(1)}) custom-call(f32[12288,128]{1,0:T(8,128)S(1)} %bitcast.75, f32[3072,128]{1,0:T(8,128)S(1)} %bitcast.77, f32[8,64,128]{2,1,0:T(8,128)} %add.144.after), custom_call_target="tpu_custom_call" | custom-call | bytes 41943040 | tf_op jit(solution)/shard_map/pallas_call | solution.py:394
  49.9 2.6 %copy-done = f32[12288,128]{1,0:T(8,128)} copy-done((f32[12288,128]{1,0:T(8,128)}, f32[12288,128]{1,0:T(8,128)S(1)}, u32[]{:S(2)}) %copy-start) | copy-done | bytes 6291480
  55.9 2.4 %collective-permute-start.4 = (f32[72,128]{1,0:T(8,128)S(1)}, f32[72,128]{1,0:T(8,128)S(1)}, u32[]{:S(2)}, u32[]{:S(2)}) collective-permute-start(f32[72,128]{1,0:T(8,128)S(1)} %shard_map.160.s0), channel_id=1, source_target_pairs={{0,48},{1,49},{2,50},{3,51},{4,52},{5,53},{6,54},{7,55},{8,56},{9,... | collective-permute-start | bytes 110600 | tf_op jit(solution)/shard_map/ppermute | solution.py:294
  60.4 15.7 %all_to_all.35 = f32[8,64,128]{2,1,0:T(8,128)S(1)} all-to-all(f32[8,64,128]{2,1,0:T(8,128)S(1)} %get-tuple-element.49), channel_id=1, replica_groups={{0,2,4,6,8,10,12,14},{1,3,5,7,9,11,13,15},{16,18,20,22,24,26,28,30},{17..., dimensions={0} | all-to-all | bytes 524288 | tf_op jit(solution)/shard_map/all_to_all | solution.py:303
  81.7 2.8 %copy-done.1 = f32[12288,128]{1,0:T(8,128)S(1)} copy-done((f32[12288,128]{1,0:T(8,128)S(1)}, f32[12288,128]{1,0:T(8,128)}, u32[]{:S(2)}) %copy-start.1) | copy-done | bytes 6291480
  87.8 3.8 %collective-permute-done.10.arriving = f32[16,128]{1,0:T(8,128)S(1)} collective-permute-done((f32[16,128]{1,0:T(8,128)S(1)}, f32[16,128]{1,0:T(8,128)S(1)}, u32[]{:S(2)}, u32[]{:S(2)}) %collective-permute-start.10) | collective-permute-done | bytes 8224 | tf_op jit(solution)/shard_map/ppermute | solution.py:50
  94.6 15.2 %all_to_all.36.received = f32[8,64,128]{2,1,0:T(8,128)S(1)} all-to-all(f32[8,64,128]{2,1,0:T(8,128)S(1)} %add.147), channel_id=1, replica_groups={{0,2,4,6,8,10,12,14},{1,3,5,7,9,11,13,15},{16,18,20,22,24,26,28,30},{17..., dimensions={0} | all-to-all | bytes 524288 | tf_op jit(solution)/shard_map/all_to_all | solution.py:303
  111.7 2.9 %collective-permute-start.13 = (f32[72,128]{1,0:T(8,128)S(1)}, f32[72,128]{1,0:T(8,128)S(1)}, u32[]{:S(2)}, u32[]{:S(2)}) collective-permute-start(f32[72,128]{1,0:T(8,128)S(1)} %shard_map.167.s0), channel_id=1, source_target_pairs={{0,32},{1,33},{2,34},{3,35},{4,36},{5,37},{6,38},{7,39},{8,40},{9,... | collective-permute-start | bytes 110600 | tf_op jit(solution)/shard_map/ppermute | solution.py:294
  118.7 14.0 %all_to_all.37 = f32[8,72,128]{2,1,0:T(8,128)S(1)} all-to-all(f32[8,72,128]{2,1,0:T(8,128)S(1)} %get-tuple-element.59), channel_id=1, replica_groups={{0,2,4,6,8,10,12,14},{1,3,5,7,9,11,13,15},{16,18,20,22,24,26,28,30},{17..., dimensions={0} | all-to-all | bytes 589824 | tf_op jit(solution)/shard_map/all_to_all | solution.py:303
  139.9 2.2 collective-permute-done.17.refs_2_
  143.3 4.2 %collective-permute-done.19.arriving = f32[16,128]{1,0:T(8,128)S(1)} collective-permute-done((f32[16,128]{1,0:T(8,128)S(1)}, f32[16,128]{1,0:T(8,128)S(1)}, u32[]{:S(2)}, u32[]{:S(2)}) %collective-permute-start.19) | collective-permute-done | bytes 8224 | tf_op jit(solution)/shard_map/ppermute | solution.py:50
  150.6 14.9 %all_to_all.38.received = f32[8,64,128]{2,1,0:T(8,128)S(1)} all-to-all(f32[8,64,128]{2,1,0:T(8,128)S(1)} %add.148), channel_id=1, replica_groups={{0,2,4,6,8,10,12,14},{1,3,5,7,9,11,13,15},{16,18,20,22,24,26,28,30},{17..., dimensions={0} | all-to-all | bytes 524288 | tf_op jit(solution)/shard_map/all_to_all | solution.py:303
  165.7 3.2 %collective-permute-start.22 = (f32[72,128]{1,0:T(8,128)S(1)}, f32[72,128]{1,0:T(8,128)S(1)}, u32[]{:S(2)}, u32[]{:S(2)}) collective-permute-start(f32[72,128]{1,0:T(8,128)S(1)} %shard_map.174.s0), channel_id=1, source_target_pairs={{0,32},{1,33},{2,34},{3,35},{4,36},{5,37},{6,38},{7,39},{8,40},{9,... | collective-permute-start | bytes 110600 | tf_op jit(solution)/shard_map/ppermute | solution.py:294
  173.5 13.9 %all_to_all.39 = f32[8,72,128]{2,1,0:T(8,128)S(1)} all-to-all(f32[8,72,128]{2,1,0:T(8,128)S(1)} %get-tuple-element.73), channel_id=1, replica_groups={{0,2,4,6,8,10,12,14},{1,3,5,7,9,11,13,15},{16,18,20,22,24,26,28,30},{17..., dimensions={0} | all-to-all | bytes 589824 | tf_op jit(solution)/shard_map/all_to_all | solution.py:303
  194.6 2.2 collective-permute-done.26.refs_2_
  198.5 4.2 %collective-permute-done.28.arriving = f32[16,128]{1,0:T(8,128)S(1)} collective-permute-done((f32[16,128]{1,0:T(8,128)S(1)}, f32[16,128]{1,0:T(8,128)S(1)}, u32[]{:S(2)}, u32[]{:S(2)}) %collective-permute-start.28) | collective-permute-done | bytes 8224 | tf_op jit(solution)/shard_map/ppermute | solution.py:50
  206.5 4.8 %all-to-all-start.6 = ((f32[8,64,128]{2,1,0:T(8,128)}), f32[8,64,128]{2,1,0:T(8,128)S(1)}, u32[]{:S(2)}, u32[]{:S(2)}) async-start(f32[8,64,128]{2,1,0:T(8,128)} %add.149), calls=%async_computation.6 | async-start | bytes 524288 | tf_op jit(solution)/shard_map/all_to_all | solution.py:303
  211.2 11.0 %all-to-all-done.6 = f32[8,64,128]{2,1,0:T(8,128)S(1)} async-done(((f32[8,64,128]{2,1,0:T(8,128)}), f32[8,64,128]{2,1,0:T(8,128)S(1)}, u32[]{:S(2)}, u32[]{:S(2)}) %all-to-all-start.6) | async-done | bytes 262176 | tf_op jit(solution)/shard_map/all_to_all | solution.py:303
  (160 shorter events, 70.2 us)
Async XLA Ops:
  10.6 4.9 %collective-permute-start = (f32[16,128]{1,0:T(8,128)S(1)}, f32[16,128]{1,0:T(8,128)S(1)}, u32[]{:S(2)}, u32[]{:S(2)}) collective-permute-start(f32[16,128]{1,0:T(8,128)S(1)} %slice.31.fterms), channel_id=1, source_target_pairs={{0,64},{64,128},{128,192},{192,0},{1,65},{65,129},{129,193},{193,1... | collective-permute-start | bytes 24584 | tf_op jit(solution)/shard_map/ppermute | solution.py:50
  19.3 34.5 %all-to-all-start = ((f32[8,64,128]{2,1,0:T(8,128)}), f32[8,64,128]{2,1,0:T(8,128)S(1)}, u32[]{:S(2)}, u32[]{:S(2)}) async-start(f32[8,64,128]{2,1,0:T(8,128)} %add.144.after), calls=%async_computation | async-start | bytes 524288 | tf_op jit(solution)/shard_map/all_to_all | solution.py:303
  31.0 5.2 %collective-permute-start.6 = (f32[16,256]{1,0:T(8,128)S(1)}, f32[16,256]{1,0:T(8,128)S(1)}, u32[]{:S(2)}, u32[]{:S(2)}) collective-permute-start(f32[16,256]{1,0:T(8,128)S(1)} %get-tuple-element.104), channel_id=1, source_target_pairs={{0,32},{1,33},{2,34},{3,35},{4,36},{5,37},{6,38},{7,39},{8,40},{9,... | collective-permute-start | bytes 49160 | tf_op jit(solution)/shard_map/ppermute | solution.py:294
  31.6 4.9 %collective-permute-start.5 = (f32[16,256]{1,0:T(8,128)S(1)}, f32[16,256]{1,0:T(8,128)S(1)}, u32[]{:S(2)}, u32[]{:S(2)}) collective-permute-start(f32[16,256]{1,0:T(8,128)S(1)} %get-tuple-element.104), channel_id=1, source_target_pairs={{0,16},{1,17},{2,18},{3,19},{4,20},{5,21},{6,22},{7,23},{8,24},{9,... | collective-permute-start | bytes 49160 | tf_op jit(solution)/shard_map/ppermute | solution.py:294
  53.9 5.2 %collective-permute-start.2 = (f32[72,128]{1,0:T(8,128)S(1)}, f32[72,128]{1,0:T(8,128)S(1)}, u32[]{:S(2)}, u32[]{:S(2)}) collective-permute-start(f32[72,128]{1,0:T(8,128)S(1)} %shard_map.160.s0), channel_id=1, source_target_pairs={{0,16},{1,17},{2,18},{3,19},{4,20},{5,21},{6,22},{7,23},{8,24},{9,... | collective-permute-start | bytes 110600 | tf_op jit(solution)/shard_map/ppermute | solution.py:294
  54.0 5.5 %collective-permute-start.3 = (f32[72,128]{1,0:T(8,128)S(1)}, f32[72,128]{1,0:T(8,128)S(1)}, u32[]{:S(2)}, u32[]{:S(2)}) collective-permute-start(f32[72,128]{1,0:T(8,128)S(1)} %shard_map.160.s0), channel_id=1, source_target_pairs={{0,32},{1,33},{2,34},{3,35},{4,36},{5,37},{6,38},{7,39},{8,40},{9,... | collective-permute-start | bytes 110600 | tf_op jit(solution)/shard_map/ppermute | solution.py:294
  78.3 7.7 %collective-permute-start.9 = (f32[16,128]{1,0:T(8,128)S(1)}, f32[16,128]{1,0:T(8,128)S(1)}, u32[]{:S(2)}, u32[]{:S(2)}) collective-permute-start(f32[16,128]{1,0:T(8,128)S(1)} %shard_map.163), channel_id=1, source_target_pairs={{0,192},{64,0},{128,64},{192,128},{1,193},{65,1},{129,65},{193,129... | collective-permute-start | bytes 24584 | tf_op jit(solution)/shard_map/ppermute | solution.py:50
  86.6 4.9 %collective-permute-start.10 = (f32[16,128]{1,0:T(8,128)S(1)}, f32[16,128]{1,0:T(8,128)S(1)}, u32[]{:S(2)}, u32[]{:S(2)}) collective-permute-start(f32[16,128]{1,0:T(8,128)S(1)} %get-tuple-element.54.fterms), channel_id=1, source_target_pairs={{0,64},{64,128},{128,192},{192,0},{1,65},{65,129},{129,193},{193,1... | collective-permute-start | bytes 24584 | tf_op jit(solution)/shard_map/ppermute | solution.py:50
  109.9 5.2 %collective-permute-start.12 = (f32[72,128]{1,0:T(8,128)S(1)}, f32[72,128]{1,0:T(8,128)S(1)}, u32[]{:S(2)}, u32[]{:S(2)}) collective-permute-start(f32[72,128]{1,0:T(8,128)S(1)} %shard_map.167.s0), channel_id=1, source_target_pairs={{0,16},{1,17},{2,18},{3,19},{4,20},{5,21},{6,22},{7,23},{8,24},{9,... | collective-permute-start | bytes 110600 | tf_op jit(solution)/shard_map/ppermute | solution.py:294
  111.7 5.5 %collective-permute-start.13 = (f32[72,128]{1,0:T(8,128)S(1)}, f32[72,128]{1,0:T(8,128)S(1)}, u32[]{:S(2)}, u32[]{:S(2)}) collective-permute-start(f32[72,128]{1,0:T(8,128)S(1)} %shard_map.167.s0), channel_id=1, source_target_pairs={{0,32},{1,33},{2,34},{3,35},{4,36},{5,37},{6,38},{7,39},{8,40},{9,... | collective-permute-start | bytes 110600 | tf_op jit(solution)/shard_map/ppermute | solution.py:294
  134.9 7.2 %collective-permute-start.18 = (f32[24,128]{1,0:T(8,128)S(1)}, f32[24,128]{1,0:T(8,128)S(1)}, u32[]{:S(2)}, u32[]{:S(2)}) collective-permute-start(f32[24,128]{1,0:T(8,128)S(1)} %get-tuple-element.63), channel_id=1, source_target_pairs={{0,192},{64,0},{128,64},{192,128},{1,193},{65,1},{129,65},{193,129... | collective-permute-start | bytes 36872 | tf_op jit(solution)/shard_map/ppermute | solution.py:50
  135.0 4.9 %collective-permute-start.16 = (f32[8,128]{1,0:T(8,128)S(1)}, f32[8,128]{1,0:T(8,128)S(1)}, u32[]{:S(2)}, u32[]{:S(2)}) collective-permute-start(f32[8,128]{1,0:T(8,128)S(1)} %get-tuple-element.60.refs_0_), channel_id=1, source_target_pairs={{0,64},{64,128},{128,192},{192,0},{1,65},{65,129},{129,193},{193,1... | collective-permute-start | bytes 12296 | tf_op jit(solution)/shard_map/ppermute | solution.py:50
  137.0 5.1 %collective-permute-start.17 = (f32[8,128]{1,0:T(8,128)S(1)}, f32[8,128]{1,0:T(8,128)S(1)}, u32[]{:S(2)}, u32[]{:S(2)}) collective-permute-start(f32[8,128]{1,0:T(8,128)S(1)} %get-tuple-element.60.refs_0_), channel_id=1, source_target_pairs={{0,128},{64,192},{128,0},{192,64},{1,129},{65,193},{129,1},{193,65... | collective-permute-start | bytes 12296 | tf_op jit(solution)/shard_map/ppermute | solution.py:50
  142.6 4.9 %collective-permute-start.19 = (f32[16,128]{1,0:T(8,128)S(1)}, f32[16,128]{1,0:T(8,128)S(1)}, u32[]{:S(2)}, u32[]{:S(2)}) collective-permute-start(f32[16,128]{1,0:T(8,128)S(1)} %get-tuple-element.68.fterms), channel_id=1, source_target_pairs={{0,64},{64,128},{128,192},{192,0},{1,65},{65,129},{129,193},{193,1... | collective-permute-start | bytes 24584 | tf_op jit(solution)/shard_map/ppermute | solution.py:50
  165.6 5.2 %collective-permute-start.21 = (f32[72,128]{1,0:T(8,128)S(1)}, f32[72,128]{1,0:T(8,128)S(1)}, u32[]{:S(2)}, u32[]{:S(2)}) collective-permute-start(f32[72,128]{1,0:T(8,128)S(1)} %shard_map.174.s0), channel_id=1, source_target_pairs={{0,16},{1,17},{2,18},{3,19},{4,20},{5,21},{6,22},{7,23},{8,24},{9,... | collective-permute-start | bytes 110600 | tf_op jit(solution)/shard_map/ppermute | solution.py:294
  165.7 5.5 %collective-permute-start.22 = (f32[72,128]{1,0:T(8,128)S(1)}, f32[72,128]{1,0:T(8,128)S(1)}, u32[]{:S(2)}, u32[]{:S(2)}) collective-permute-start(f32[72,128]{1,0:T(8,128)S(1)} %shard_map.174.s0), channel_id=1, source_target_pairs={{0,32},{1,33},{2,34},{3,35},{4,36},{5,37},{6,38},{7,39},{8,40},{9,... | collective-permute-start | bytes 110600 | tf_op jit(solution)/shard_map/ppermute | solution.py:294
  189.6 7.2 %collective-permute-start.27 = (f32[24,128]{1,0:T(8,128)S(1)}, f32[24,128]{1,0:T(8,128)S(1)}, u32[]{:S(2)}, u32[]{:S(2)}) collective-permute-start(f32[24,128]{1,0:T(8,128)S(1)} %get-tuple-element.77), channel_id=1, source_target_pairs={{0,192},{64,0},{128,64},{192,128},{1,193},{65,1},{129,65},{193,129... | collective-permute-start | bytes 36872 | tf_op jit(solution)/shard_map/ppermute | solution.py:50
  189.8 4.8 %collective-permute-start.25 = (f32[8,128]{1,0:T(8,128)S(1)}, f32[8,128]{1,0:T(8,128)S(1)}, u32[]{:S(2)}, u32[]{:S(2)}) collective-permute-start(f32[8,128]{1,0:T(8,128)S(1)} %get-tuple-element.74.refs_0_), channel_id=1, source_target_pairs={{0,64},{64,128},{128,192},{192,0},{1,65},{65,129},{129,193},{193,1... | collective-permute-start | bytes 12296 | tf_op jit(solution)/shard_map/ppermute | solution.py:50
  191.7 5.1 %collective-permute-start.26 = (f32[8,128]{1,0:T(8,128)S(1)}, f32[8,128]{1,0:T(8,128)S(1)}, u32[]{:S(2)}, u32[]{:S(2)}) collective-permute-start(f32[8,128]{1,0:T(8,128)S(1)} %get-tuple-element.74.refs_0_), channel_id=1, source_target_pairs={{0,128},{64,192},{128,0},{192,64},{1,129},{65,193},{129,1},{193,65... | collective-permute-start | bytes 12296 | tf_op jit(solution)/shard_map/ppermute | solution.py:50
  197.9 4.9 %collective-permute-start.28 = (f32[16,128]{1,0:T(8,128)S(1)}, f32[16,128]{1,0:T(8,128)S(1)}, u32[]{:S(2)}, u32[]{:S(2)}) collective-permute-start(f32[16,128]{1,0:T(8,128)S(1)} %get-tuple-element.84.fterms), channel_id=1, source_target_pairs={{0,64},{64,128},{128,192},{192,0},{1,65},{65,129},{129,193},{193,1... | collective-permute-start | bytes 24584 | tf_op jit(solution)/shard_map/ppermute | solution.py:50
  206.5 15.8 %all-to-all-start.6 = ((f32[8,64,128]{2,1,0:T(8,128)}), f32[8,64,128]{2,1,0:T(8,128)S(1)}, u32[]{:S(2)}, u32[]{:S(2)}) async-start(f32[8,64,128]{2,1,0:T(8,128)} %add.149), calls=%async_computation.6 | async-start | bytes 524288 | tf_op jit(solution)/shard_map/all_to_all | solution.py:303
  222.3 5.3 %collective-permute-start.32 = (f32[16,128]{1,0:T(8,128)S(1)}, f32[16,128]{1,0:T(8,128)S(1)}, u32[]{:S(2)}, u32[]{:S(2)}) collective-permute-start(f32[16,128]{1,0:T(8,128)S(1)} %get-tuple-element.101), channel_id=1, source_target_pairs={{0,48},{1,49},{2,50},{3,51},{4,52},{5,53},{6,54},{7,55},{8,56},{9,... | collective-permute-start | bytes 24584 | tf_op jit(solution)/shard_map/ppermute | solution.py:294
  224.4 4.9 %collective-permute-start.30 = (f32[16,128]{1,0:T(8,128)S(1)}, f32[16,128]{1,0:T(8,128)S(1)}, u32[]{:S(2)}, u32[]{:S(2)}) collective-permute-start(f32[16,128]{1,0:T(8,128)S(1)} %get-tuple-element.102), channel_id=1, source_target_pairs={{0,16},{1,17},{2,18},{3,19},{4,20},{5,21},{6,22},{7,23},{8,24},{9,... | collective-permute-start | bytes 24584 | tf_op jit(solution)/shard_map/ppermute | solution.py:294
  224.4 5.2 %collective-permute-start.31 = (f32[16,128]{1,0:T(8,128)S(1)}, f32[16,128]{1,0:T(8,128)S(1)}, u32[]{:S(2)}, u32[]{:S(2)}) collective-permute-start(f32[16,128]{1,0:T(8,128)S(1)} %get-tuple-element.100), channel_id=1, source_target_pairs={{0,32},{1,33},{2,34},{3,35},{4,36},{5,37},{6,38},{7,39},{8,40},{9,... | collective-permute-start | bytes 24584 | tf_op jit(solution)/shard_map/ppermute | solution.py:294
  (29 other events, 513.5 us)

commit v3 on v2

--- a/solution.py
+++ b/solution.py
@@ -14,7 +14,7 @@
 NY, NZ, NC = 4, 8, 2
 CHIPS = NY * NZ
 OWN = 16
-STRIP = NY * OWN
+HALF = CHIPS * OWN
 
 KC, KF = 64, 16
 GC, GF = 128 // KC, 128 // KF
@@ -33,15 +33,18 @@
     return jax.ShapeDtypeStruct(dims, f32)
 
 
-def kernel_call(body, out, specs, scratch=(), megabytes=4, cost=None):
+def kernel_call(
+    body, out, specs, scratch=(), megabytes=4, out_specs=None, cost=None, aliases=None
+):
     return pl.pallas_call(
         body,
         out_shape=out,
         in_specs=specs,
-        out_specs=jax.tree.map(lambda _: vmem, out),
+        out_specs=out_specs or jax.tree.map(lambda _: vmem, out),
         scratch_shapes=list(scratch),
         compiler_params=pltpu.CompilerParams(vmem_limit_bytes=megabytes << 20),
         cost_estimate=cost,
+        input_output_aliases=aliases or {},
     )
 
 
@@ -115,46 +118,45 @@
     return sum(partial[pl.ds(q, slices, stride=8), :] for q in range(8))
 
 
-def first_force_kernel(cjac, fjac, cwarm, fwarm, terms, cbuf, fbuf, partial, csem, fsem):
-    parts = 4
-    share = KC // parts * COMP * BLK
-    ccopies = [
-        pltpu.make_async_copy(
-            cjac.at[pl.ds(p * share, share)], cbuf.at[pl.ds(p * share, share)], csem.at[p]
-        )
-        for p in range(parts)
-    ]
-    fcopy = pltpu.make_async_copy(fjac, fbuf, fsem)
-    fcopy.start()
-    for copy in ccopies:
+def first_force_kernel(
+    cjac, fjac, cwarm, fwarm, cterms, fterms, cbuf, fbuf, partial, csem, fsem
+):
+    width = COMP * BLK
+    parts = ((fjac, fbuf, fsem, KF, KC), (cjac, cbuf, csem, KC, 0))
+    copies = []
+    for jac, buf, sems, blocks, _ in parts:
+        share = blocks // sems.shape[0]
+        for p in range(sems.shape[0]):
+            rows = pl.ds(p * share * width, share * width)
+            copies.append(pltpu.make_async_copy(jac.at[rows], buf.at[rows], sems.at[p]))
+    for copy in copies:
         copy.start()
-    width = COMP * BLK
     rows = jnp.concatenate([cwarm[...], fwarm[...], jnp.zeros((128 - KC - KF, width), f32)], 0)
     rows = jnp.concatenate([rows, jnp.zeros((128, 256 - width), f32)], 1)
     turned = jnp.concatenate([rows[:, :128].T, rows[:, 128:].T], 0)[:width]
-
-    def block(jac, at, k):
-        y = jnp.broadcast_to(turned[:, k : k + 1], (width, 128))
-        terms_k = jac[at * width : (at + 1) * width, :] * y
-        partial[k * 8 : (k + 1) * 8, :] = jnp.sum(terms_k.reshape(width // 8, 8, 128), 0)
-
-    fcopy.wait()
-    for m in range(KF):
-        block(fbuf, m, KC + m)
-    for p, copy in enumerate(ccopies):
-        copy.wait()
-        for m in range(KC // parts):
-            block(cbuf, p * (KC // parts) + m, p * (KC // parts) + m)
-    terms[...] = sum(partial[pl.ds(q, KC + KF, stride=8), :] for q in range(8))
-
-
-def layout_kernel(cjac, fjac, after, cout, fout, done, cbuf, fbuf, sems):
+    for jac, buf, sems, blocks, base in parts:
+        share = blocks // sems.shape[0]
+        for m in range(blocks):
+            if m % share == 0:
+                copies.pop(0).wait()
+            y = jnp.broadcast_to(turned[:, base + m : base + m + 1], (width, 128))
+            products = buf[m * width : (m + 1) * width, :] * y
+            partial[(base + m) * 8 : (base + m + 1) * 8, :] = jnp.sum(
+                products.reshape(width // 8, 8, 128), 0
+            )
+    cterms[...] = sum(partial[pl.ds(q, KC, stride=8), :] for q in range(8))
+    fterms[...] = sum(partial[pl.ds(KC * 8 + q, KF, stride=8), :] for q in range(8))
+
+
+def layout_kernel(cjac, fjac, after, cout, fout, done, cbuf, fbuf, cturn, fturn, sems, outs):
     copies = [pltpu.make_async_copy(fjac, fbuf, sems.at[0])]
-    copies.append(pltpu.make_async_copy(cjac, cbuf, sems.at[1]))
+    for p in range(4):
+        rows = pl.ds(p * KC * COMP * BLK // 4, KC * COMP * BLK // 4)
+        copies.append(pltpu.make_async_copy(cjac.at[rows], cbuf.at[rows], sems.at[1 + p]))
     for copy in copies:
         copy.start()
 
-    def turn(jac, out, parts, depth, slices):
+    def turn(jac, out, parts, depth, first, count):
         k = 128 // parts
 
         def one(s, _):
@@ -165,51 +167,68 @@
             out[rows_of(s), :] = jnp.concatenate(rows, 0).T
             return _
 
-        lax.fori_loop(0, slices, one, 0, unroll=8)
+        lax.fori_loop(first, first + count, one, 0, unroll=8)
 
     copies[0].wait()
-    turn(fbuf, fout, GF, IF, SF)
-    copies[1].wait()
-    turn(cbuf, cout, GC, IC, SC)
+    turn(fbuf, fturn, GF, IF, 0, SF)
+    leaving = [pltpu.make_async_copy(fturn, fout, outs.at[0])]
+    leaving[0].start()
+    for copy in copies[1:]:
+        copy.wait()
+    share = SC // 6
+    for part in range(6):
+        turn(cbuf, cturn, GC, IC, part * share, share)
+        rows = pl.ds(part * share * 128, share * 128)
+        leaving.append(pltpu.make_async_copy(cturn.at[rows], cout.at[rows], outs.at[part + 1]))
+        leaving[-1].start()
     done[...] = jnp.zeros_like(done)
+    for copy in leaving:
+        copy.wait()
 
 
 def force_kernel(jac, y, terms):
     terms[...] = folded(accumulate(jac, y, SC), GC)
 
 
-def scatter_kernel(rows, swap, cterms, fterms, arriving, own, other, total, wide):
+def scatter_kernel(rows, swap, cterms, fterms, own, other, total, wide):
     left = left_half(KC)
-    near = left_half(KF)
+    count = 2 * KC + KF
     wide[0:KC, :] = jnp.where(left, cterms[...], 0.0)
     wide[KC : 2 * KC, :] = jnp.where(left, 0.0, cterms[...])
-    wide[2 * KC : 2 * KC + KF, :] = jnp.where(near, fterms[...], 0.0)
-    wide[2 * KC + KF :, :] = jnp.where(near, 0.0, arriving[...])
+    wide[2 * KC :, :] = jnp.where(left_half(KF), fterms[...], 0.0)
     x = wide[...]
-    wide[...] = jnp.where(swap[...] > 0, pltpu.roll(x, BLK, 1), x)
+    wide[...] = jnp.where(swap[0:count, :] > 0, pltpu.roll(x, BLK, 1), x)
     total[...] = jnp.zeros_like(total)
-    for m in range(2 * KC + 2 * KF):
+    for m in range(count):
         at = pl.ds(rows[m], 1)
         total[at, :] = total[at, :] + wide[m : m + 1, :]
-    half = CHIPS * OWN
-    own[...] = total[0:half, :].reshape(own.shape)
-    other[...] = total[half:, :].reshape(other.shape)
-
-
-def strip_kernel(received, spread, after, strip):
-    strip[0:STRIP, :] = jnp.sum(received[...], 0)
-    strip[STRIP:, :] = jnp.broadcast_to(jnp.sum(spread[...]), (8, 128))
-
-
-def owner_kernel(with_sums, s0, s1, s2, s3, free, mass, last, total, pieces):
-    both = s0[...] + s1[...] + s2[...] + s3[...]
-    total[...] = both[0:STRIP]
-    piece = free[...] + mass[...] * both[0:STRIP]
+    own[...] = total[0:HALF, :]
+    other[...] = total[HALF:, :]
+
+
+def arrive_kernel(rows, swap, arriving, own_in, other_in, own, other, wide):
+    base = 2 * KC + KF
+    x = jnp.where(left_half(KF), 0.0, arriving[...])
+    wide[...] = jnp.where(swap[base:, :] > 0, pltpu.roll(x, BLK, 1), x)
+    for m in range(KF):
+        row = rows[base + m]
+        mine = row < HALF
+        value = wide[m : m + 1, :]
+        for half, here, at in ((own, mine, row), (other, ~mine, row - HALF)):
+            at = pl.ds(jnp.where(here, at, 0), 1)
+            half[at, :] = half[at, :] + jnp.where(here, value, 0.0)
+
+
+def owner_kernel(with_sums, received, free, mass, last, spread, done, owned, pieces):
+    total = jnp.sum(received[...], 0)
+    owned[...] = total
+    piece = free[...] + mass[...] * total
     if with_sums:
-        change = both[0:STRIP] - last[...]
+        change = total - last[...]
         curve = jnp.sum(mass[...] * change * change)
         row = lax.broadcasted_iota(jnp.int32, (8, 128), 0)
-        piece = jnp.concatenate([piece, jnp.where(row == 0, both[STRIP:], curve)], 0)
+        sums = jnp.where(row == 0, jnp.sum(spread[...]), curve)
+        piece = jnp.concatenate([piece, sums], 0)
     pieces[...] = jnp.broadcast_to(piece, pieces.shape)
 
 
@@ -218,8 +237,8 @@
     picked = jnp.concatenate([panel[pl.ds(rows[base + m], 1), :] for m in range(KF)], 0)
     far[0:KF, :] = jnp.where(swap[base:, :] > 0, pltpu.roll(picked, BLK, 1), picked)
     if with_sums:
-        size = STRIP + 8
-        total = sum(panel[p * size + STRIP : (p + 1) * size, :] for p in range(NC * NZ))
+        size = OWN + 8
+        total = sum(panel[p * size + OWN : (p + 1) * size, :] for p in range(NC * CHIPS))
         sums[0][...] = total
         far[KF:, :] = total
 
@@ -289,17 +308,8 @@
     fterms[...] = folded(accumulate(jac, fnext, SF), GF)
 
 
-def along_y(x, by):
-    line = NZ * NC
-    return lax.ppermute(
-        x, "grp", [(i, (i + by * line) % (NY * line)) for i in range(NY * line)]
-    )
-
-
 def exchange(parts):
-    groups = [
-        [(y * NZ + z) * NC + core for z in range(NZ)] for y in range(NY) for core in range(NC)
-    ]
+    groups = [[chip * NC + core for chip in range(CHIPS)] for core in range(NC)]
     return lax.all_to_all(parts, "grp", 0, 0, axis_index_groups=groups, tiled=True)
 
 
@@ -333,19 +343,10 @@
         [contact_bodies[:, 0], contact_bodies[:, 1], face_own, face_far]
     )
     owner = targets // (2 * OWN)
-    me = lax.axis_index("grp")
-    slot = (owner - me) % NC * NZ + owner // NC % NZ
-    row = owner // (NC * NZ) * OWN + targets % (2 * OWN) // 2
-    sum_rows = slot * STRIP + row
-    panel_rows = [slot * STRIP + row] + [slot * (STRIP + 8) + row] * (ITERS - 1)
-    my_y = me // (NC * NZ)
-
-    def strip_of(x):
-        parts = jnp.stack([x] + [along_y(x, by) for by in range(1, NY)])
-        return parts[(my_y - jnp.arange(NY)) % NY].reshape(-1, x.shape[-1])
-
-    constants = strip_of(jnp.concatenate([free_own, mass_own], 1))
-    free_strip, mass_strip = constants[:, :128], constants[:, 128:]
+    slot = (owner - lax.axis_index("grp")) % NC * CHIPS + owner // NC
+    row = targets % (2 * OWN) // 2
+    sum_rows = slot * OWN + row
+    panel_rows = [slot * OWN + row] + [slot * (OWN + 8) + row] * (ITERS - 1)
     order = jnp.arange(targets.shape[0])
     right = ((order >= KC) & (order < 2 * KC)) | (order >= 2 * KC + KF)
     swap = jnp.broadcast_to(
@@ -355,38 +356,44 @@
     ffric = to_lanes(class_lookup(face_class, friction_table), GF)
 
     def core_half(cterms, fterms, arriving):
-        halves = kernel_call(
+        own, other = kernel_call(
             scatter_kernel,
-            (shape(NZ, STRIP, 128), shape(NZ, STRIP, 128)),
+            (shape(HALF, 128), shape(HALF, 128)),
+            [smem] + [vmem] * 3,
+            [pltpu.VMEM((NC * HALF, 128), f32), pltpu.VMEM((2 * KC + KF, 128), f32)],
+        )(sum_rows, swap, cterms, fterms)
+        own, other = kernel_call(
+            arrive_kernel,
+            (shape(HALF, 128), shape(HALF, 128)),
             [smem] + [vmem] * 4,
-            [pltpu.VMEM((NC * CHIPS * OWN, 128), f32), pltpu.VMEM((2 * KC + 2 * KF, 128), f32)],
-        )(sum_rows, swap, cterms, fterms, arriving)
-        return halves[0] + other_core(halves[1])
+            [pltpu.VMEM((KF, 128), f32)],
+            aliases={3: 0, 4: 1},
+        )(sum_rows, swap, arriving, own, other)
+        return (own + other_core(other)).reshape(CHIPS, OWN, 128)
 
     betas = momentum_weights(ITERS)
     cwarm = warm_contact * live[0, :KC, None]
     crows, frows = contact_jac.reshape(-1, 128), face_jac.reshape(-1, 128)
     cbuf, fbuf = pltpu.VMEM((SC * 128, 128), f32), pltpu.VMEM((SF * 128, 128), f32)
-    terms = kernel_call(
+    cterms, fterms = kernel_call(
         first_force_kernel,
-        shape(KC + KF, 128),
+        (shape(KC, 128), shape(KF, 128)),
         [hbm, hbm, vmem, vmem],
         [
             cbuf,
             fbuf,
             pltpu.VMEM(((KC + KF) * 8, 128), f32),
+            pltpu.SemaphoreType.DMA((16,)),
             pltpu.SemaphoreType.DMA((4,)),
-            pltpu.SemaphoreType.DMA,
         ],
-        60,
+        56,
     )(crows, frows, cwarm, warm_face)
-    cterms, fterms = terms[:KC], terms[KC:]
     arriving = shifted(fterms, "slab", 1)
     cnow = to_lanes(cwarm, GC)
     fnow = to_lanes(warm_face, GF)
     cy, fy = cnow, fnow
     spread = jnp.zeros((8, 128), f32)
-    total = free_strip
+    owned = free_own
     for turn in range(ITERS):
         half = core_half(cterms, fterms, arriving)
         received = exchange(half)
@@ -394,21 +401,25 @@
             cjac, fjac, done = kernel_call(
                 layout_kernel,
                 (shape(SC * 128, 128), shape(SF * 128, 128), shape(8, 128)),
-                [hbm, hbm, vmem],
-                [cbuf, fbuf, pltpu.SemaphoreType.DMA((2,))],
-                20,
+                [hbm, hbm, hbm],
+                [
+                    cbuf,
+                    fbuf,
+                    cbuf,
+                    fbuf,
+                    pltpu.SemaphoreType.DMA((5,)),
+                    pltpu.SemaphoreType.DMA((7,)),
+                ],
+                56,
+                (hbm, hbm, vmem),
                 pl.CostEstimate(flops=0, bytes_accessed=40 << 20, transcendentals=0),
-            )(crows, frows, half)
-        strip = kernel_call(strip_kernel, shape(STRIP + 8, 128), [vmem] * 3)(
-            received, spread, done
-        )
-        strips = [strip] + [along_y(strip, by) for by in range(1, NY)]
+            )(crows, frows, half[0, 0:8])
         extra = 8 if turn > 0 else 0
-        total, pieces = kernel_call(
+        owned, pieces = kernel_call(
             functools.partial(owner_kernel, turn > 0),
-            (shape(STRIP, 128), shape(NZ, STRIP + extra, 128)),
-            [vmem] * 7,
-        )(*strips, free_strip, mass_strip, total)
+            (shape(OWN, 128), shape(CHIPS, OWN + extra, 128)),
+            [vmem] * 6,
+        )(received, free_own, mass_own, owned, spread, done)
         panel = all_gather(pieces)
         picked = kernel_call(
             functools.partial(far_kernel, turn > 0),
@@ -443,13 +454,7 @@
         arriving = shifted(fterms, "slab", 1)
         cterms = kernel_call(force_kernel, shape(KC, 128), [vmem] * 2)(cjac, cy)
     received = exchange(core_half(cterms, fterms, arriving))
-    strip = jnp.sum(received, 0).reshape(NY, OWN, 128)
-
-    def block_at(by):
-        return lax.dynamic_index_in_dim(strip, (my_y + by) % NY, 0, keepdims=False)
-
-    owned = block_at(0) + sum(along_y(block_at(by), by) for by in range(1, NY))
-    final = free_own + mass_own * owned
+    final = free_own + mass_own * jnp.sum(received, 0)
     return (from_lanes(cnow, GC), from_lanes(fnow, GF), final.reshape(-1))
 
 

time: 233 us -> 210 us (0.901)
  waiting for transfers between devices: 58.5 us -> 35 us
  blocking collectives: 73.7 us -> 93.5 us
  starting transfers between devices: 43.2 us -> 26 us
  Pallas kernels: 33.8 us -> 39.3 us
  local copies, waits for them, and re-layouts: 14.1 us -> 8.84 us
    ppermute x15 -> x0, starting transfers between devices: 21.6 us -> none  [along_y(): lax.ppermute(x, 'grp', [(i, (i + by * line) % (NY * line)) for i in range...]
    all_to_all x5, blocking collectives: 73.7 us -> 93.5 us  [exchange(): lax.all_to_all(parts, 'grp', 0, 0, axis_index_groups=groups, tiled=True)]
    ppermute x15 -> x0, waiting for transfers between devices: 14.9 us -> none  [along_y(): lax.ppermute(x, 'grp', [(i, (i + by * line) % (NY * line)) for i in range...]
    ppermute x11, waiting for transfers between devices: 21.9 us -> 13.2 us  [shifted(): lax.ppermute(x, axis, [(i, (i + by) % devices) for i in range(devices)])]
    unnamed x39, local copies, waits for them, and re-layouts: 11 us -> 6.48 us
    pallas_call x11 -> x12, Pallas kernels: 13.5 us -> 16.7 us  [the longest x1 7.73 us: on_device(): kernel_call(first_force_kernel, (shape(KC, 128), shape(KF, 128)), [hbm, h...]
    all_to_all x2, starting transfers between devices: 13.3 us -> 16 us  [exchange(): lax.all_to_all(parts, 'grp', 0, 0, axis_index_groups=groups, tiled=True)]
    pallas_call x1, Pallas kernels: 9.95 us -> 12.3 us  [on_device(): kernel_call(layout_kernel, (shape(SC * 128, 128), shape(SF * 128, 128), s...]
  transfers between devices with their start and end apart: 35 -> 20, of which waited for: 29 -> 16; matrix products, arithmetic and copies ran while one was open for 2% -> 2% of each run, Pallas kernels for 7% -> 11%
where the time goes in v3:
time: 210 us; the launch traced here: 209 us
  blocking collectives  93.5 us (45%)
  Pallas kernels  39.3 us (19%)
  waiting for transfers between devices  35 us (17%)
  starting transfers between devices  26 us (12%)
  local copies, waits for them, and re-layouts  8.84 us (4%)
  other arithmetic  4.21 us (2%)
  between operations  2.45 us (1%)
    all_to_all x5, blocking collectives, exchange(): lax.all_to_all(parts, 'grp', 0, 0, axis_index_groups=groups, tiled=True)  93.5 us
    all_to_all x2, starting transfers between devices, exchange(): lax.all_to_all(parts, 'grp', 0, 0, axis_index_groups=groups, tiled=True)  16 us
    ppermute x11, waiting for transfers between devices, shifted(): lax.ppermute(x, axis, [(i, (i + by) % devices) for i in range(devices)])  13.2 us
    pallas_call x1, Pallas kernels, on_device(): kernel_call(layout_kernel, (shape(SC * 128, 128), shape(SF * 128, 128), s...  12.3 us
    all_to_all x2, waiting for transfers between devices, exchange(): lax.all_to_all(parts, 'grp', 0, 0, axis_index_groups=groups, tiled=True)  10.9 us
    ppermute x7, waiting for transfers between devices, other_core(): return lax.ppermute(x, 'grp', [(i, i ^ 1) for i in range(devices)])  10.9 us
    ppermute x11, starting transfers between devices, shifted(): lax.ppermute(x, axis, [(i, (i + by) % devices) for i in range(devices)])  9.6 us
    pallas_call x1, Pallas kernels, on_device(): kernel_call(first_force_kernel, (shape(KC, 128), shape(KF, 128)), [hbm, h...  7.73 us
  transfers between devices with their start and end apart: 20, of which 16 were waited for; matrix products, arithmetic and copies ran while one was open for 2% of the time, Pallas kernels for 11%

profile of v3, /device:TPU:32, one launch (start us, length us, event | category | flops | bytes accessed | tf_op | source)
XLA Modules:
  0.0 209.3 jit_solution(8062755674140337570)
XLA Ops:
  1.4 1.5 broadcast_multiply_fusion.cwarm
  2.9 7.7 %shard_map.157 = (f32[64,128]{1,0:T(8,128)}, f32[16,128]{1,0:T(8,128)}) custom-call(f32[12288,128]{1,0:T(8,128)} %bitcast.70, f32[3072,128]{1,0:T(8,128)} %bitcast.72, f32[64,192]{1,0:T(8,128)} %broadcast_multiply_fusion.cwarm, f32[16,192]{1,0:T(8,128)} %fwarm.1), custom_call_target="tpu_custom_call" | custom-call | tf_op jit(solution)/shard_map/pallas_call | solution.py:378
  10.7 1.6 collective-permute-start
  16.6 1.5 collective-permute-done.1
  18.9 11.4 %all-to-all-start = ((f32[32,16,128]{2,1,0:T(8,128)}), f32[32,16,128]{2,1,0:T(8,128)S(1)}, u32[]{:S(2)}, u32[]{:S(2)}) async-start(f32[32,16,128]{2,1,0:T(8,128)} %bitcast.7), calls=%async_computation | async-start | bytes 524288 | tf_op jit(solution)/shard_map/all_to_all | solution.py:313
  31.6 12.3 %shard_map.160 = (f32[12288,128]{1,0:T(8,128)}, f32[3072,128]{1,0:T(8,128)}, f32[8,128]{1,0:T(8,128)}) custom-call(f32[12288,128]{1,0:T(8,128)} %bitcast.71, f32[3072,128]{1,0:T(8,128)} %bitcast.73, f32[8,128]{1,0:T(8,128)} %slice_bitcast_fusion.after), custom_call_target="tpu_custom_call" | custom-call | bytes 41943040 | tf_op jit(solution)/shard_map/pallas_call | solution.py:401
  44.6 21.7 %all_to_all.35 = f32[32,16,128]{2,1,0:T(8,128)S(1)} all-to-all(f32[32,16,128]{2,1,0:T(8,128)S(1)} %get-tuple-element.62), channel_id=1, replica_groups={{0,2,4,6,8,10,12,14,16,18,20,22,24,26,28,30,32,34,36,38,40,42,44,46,48,..., dimensions={0} | all-to-all | bytes 524288 | tf_op jit(solution)/shard_map/all_to_all | solution.py:313
  68.6 1.6 collective-permute-start.3
  71.8 2.8 %copy-done = f32[12288,128]{1,0:T(8,128)S(1)} copy-done((f32[12288,128]{1,0:T(8,128)S(1)}, f32[12288,128]{1,0:T(8,128)}, u32[]{:S(2)}) %copy-start) | copy-done | bytes 6291480
  79.4 2.5 %collective-permute-done.4.arriving = f32[16,128]{1,0:T(8,128)S(1)} collective-permute-done((f32[16,128]{1,0:T(8,128)S(1)}, f32[16,128]{1,0:T(8,128)S(1)}, u32[]{:S(2)}, u32[]{:S(2)}) %collective-permute-start.4) | collective-permute-done | bytes 8224 | tf_op jit(solution)/shard_map/ppermute | solution.py:53
  82.6 1.5 collective-permute-done.5
  84.2 16.9 %all_to_all.36.received = f32[32,16,128]{2,1,0:T(8,128)S(1)} all-to-all(f32[32,16,128]{2,1,0:T(8,128)S(1)} %bitcast.76), channel_id=1, replica_groups={{0,2,4,6,8,10,12,14,16,18,20,22,24,26,28,30,32,34,36,38,40,42,44,46,48,..., dimensions={0} | all-to-all | bytes 524288 | tf_op jit(solution)/shard_map/all_to_all | solution.py:313
  101.3 18.9 %all_to_all.37 = f32[32,24,128]{2,1,0:T(8,128)S(1)} all-to-all(f32[32,24,128]{2,1,0:T(8,128)S(1)} %get-tuple-element.75), channel_id=1, replica_groups={{0,2,4,6,8,10,12,14,16,18,20,22,24,26,28,30,32,34,36,38,40,42,44,46,48,..., dimensions={0} | all-to-all | bytes 786432 | tf_op jit(solution)/shard_map/all_to_all | solution.py:313
  120.2 1.7 collective-permute-done.6
  126.2 1.9 collective-permute-done.8.refs_2_
  132.4 2.1 collective-permute-done.10.arriving
  135.3 1.5 collective-permute-done.11
  136.8 17.1 %all_to_all.38.received = f32[32,16,128]{2,1,0:T(8,128)S(1)} all-to-all(f32[32,16,128]{2,1,0:T(8,128)S(1)} %bitcast.77), channel_id=1, replica_groups={{0,2,4,6,8,10,12,14,16,18,20,22,24,26,28,30,32,34,36,38,40,42,44,46,48,..., dimensions={0} | all-to-all | bytes 524288 | tf_op jit(solution)/shard_map/all_to_all | solution.py:313
  154.5 18.9 %all_to_all.39 = f32[32,24,128]{2,1,0:T(8,128)S(1)} all-to-all(f32[32,24,128]{2,1,0:T(8,128)S(1)} %get-tuple-element.91), channel_id=1, replica_groups={{0,2,4,6,8,10,12,14,16,18,20,22,24,26,28,30,32,34,36,38,40,42,44,46,48,..., dimensions={0} | all-to-all | bytes 786432 | tf_op jit(solution)/shard_map/all_to_all | solution.py:313
  173.4 1.7 collective-permute-done.12
  179.4 2.4 %collective-permute-done.14.refs_2_ = f32[8,128]{1,0:T(8,128)S(1)} collective-permute-done((f32[8,128]{1,0:T(8,128)S(1)}, f32[8,128]{1,0:T(8,128)S(1)}, u32[]{:S(2)}, u32[]{:S(2)}) %collective-permute-start.14) | collective-permute-done | bytes 4128 | tf_op jit(solution)/shard_map/ppermute | solution.py:53
  186.0 2.3 %collective-permute-done.16.arriving = f32[16,128]{1,0:T(8,128)S(1)} collective-permute-done((f32[16,128]{1,0:T(8,128)S(1)}, f32[16,128]{1,0:T(8,128)S(1)}, u32[]{:S(2)}, u32[]{:S(2)}) %collective-permute-start.16) | collective-permute-done | bytes 8224 | tf_op jit(solution)/shard_map/ppermute | solution.py:53
  191.4 4.7 %all-to-all-start.6 = ((f32[32,16,128]{2,1,0:T(8,128)}), f32[32,16,128]{2,1,0:T(8,128)S(1)}, u32[]{:S(2)}, u32[]{:S(2)}) async-start(f32[32,16,128]{2,1,0:T(8,128)} %bitcast.34), calls=%async_computation.6 | async-start | bytes 524288 | tf_op jit(solution)/shard_map/all_to_all | solution.py:313
  197.7 10.9 %all-to-all-done.6 = f32[32,16,128]{2,1,0:T(8,128)S(1)} async-done(((f32[32,16,128]{2,1,0:T(8,128)}), f32[32,16,128]{2,1,0:T(8,128)S(1)}, u32[]{:S(2)}, u32[]{:S(2)}) %all-to-all-start.6) | async-done | bytes 262176 | tf_op jit(solution)/shard_map/all_to_all | solution.py:313
  (123 shorter events, 39.7 us)
Async XLA Ops:
  2.9 63.5 %copy-start.10 = (s32[64,64]{1,0:T(8,128)S(1)}, s32[64,64]{1,0:T(8,128)}, u32[]{:S(2)}) copy-start(s32[64,64]{1,0:T(8,128)} %param.16) | copy-start | bytes 49156
  10.7 55.7 %copy-start.12 = (f32[8]{0:T(128)S(1)}, f32[8]{0:T(128)}, u32[]{:S(2)}) copy-start(f32[8]{0:T(128)} %param.26) | copy-start | bytes 100
  10.7 5.1 %collective-permute-start = (f32[16,128]{1,0:T(8,128)}, f32[16,128]{1,0:T(8,128)S(1)}, u32[]{:S(2)}, u32[]{:S(2)}) collective-permute-start(f32[16,128]{1,0:T(8,128)} %get-tuple-element.55.fterms), channel_id=1, source_target_pairs={{0,64},{64,128},{128,192},{192,0},{1,65},{65,129},{129,193},{193,1... | collective-permute-start | bytes 24584 | tf_op jit(solution)/shard_map/ppermute | solution.py:53
  12.4 57.8 %copy-start.11 = (s32[16,64]{1,0:T(8,128)S(1)}, s32[16,64]{1,0:T(8,128)}, u32[]{:S(2)}) copy-start(s32[16,64]{1,0:T(8,128)} %param.21) | copy-start | bytes 12292
  12.4 57.8 %copy-start.8 = (f32[64,192]{1,0:T(8,128)S(1)}, f32[64,192]{1,0:T(8,128)}, u32[]{:S(2)}) copy-start(f32[64,192]{1,0:T(8,128)} %broadcast_multiply_fusion.cwarm) | copy-start | bytes 147460
  16.6 1.6 collective-permute-start.1
  18.9 25.0 %all-to-all-start = ((f32[32,16,128]{2,1,0:T(8,128)}), f32[32,16,128]{2,1,0:T(8,128)S(1)}, u32[]{:S(2)}, u32[]{:S(2)}) async-start(f32[32,16,128]{2,1,0:T(8,128)} %bitcast.7), calls=%async_computation | async-start | bytes 524288 | tf_op jit(solution)/shard_map/all_to_all | solution.py:313
  66.4 1.5 collective-permute-start.2
  68.6 7.5 %collective-permute-start.3 = (f32[16,128]{1,0:T(8,128)S(1)}, f32[16,128]{1,0:T(8,128)S(1)}, u32[]{:S(2)}, u32[]{:S(2)}) collective-permute-start(f32[16,128]{1,0:T(8,128)S(1)} %shard_map.163), channel_id=1, source_target_pairs={{0,192},{64,0},{128,64},{192,128},{1,193},{65,1},{129,65},{193,129... | collective-permute-start | bytes 24584 | tf_op jit(solution)/shard_map/ppermute | solution.py:53
  76.7 5.1 %collective-permute-start.4 = (f32[16,128]{1,0:T(8,128)S(1)}, f32[16,128]{1,0:T(8,128)S(1)}, u32[]{:S(2)}, u32[]{:S(2)}) collective-permute-start(f32[16,128]{1,0:T(8,128)S(1)} %get-tuple-element.67.fterms), channel_id=1, source_target_pairs={{0,64},{64,128},{128,192},{192,0},{1,65},{65,129},{129,193},{193,1... | collective-permute-start | bytes 24584 | tf_op jit(solution)/shard_map/ppermute | solution.py:53
  82.6 1.6 collective-permute-start.5
  120.2 1.7 collective-permute-start.6
  122.6 6.3 %collective-permute-start.9 = (f32[24,128]{1,0:T(8,128)S(1)}, f32[24,128]{1,0:T(8,128)S(1)}, u32[]{:S(2)}, u32[]{:S(2)}) collective-permute-start(f32[24,128]{1,0:T(8,128)S(1)} %get-tuple-element.79), channel_id=1, source_target_pairs={{0,192},{64,0},{128,64},{192,128},{1,193},{65,1},{129,65},{193,129... | collective-permute-start | bytes 36872 | tf_op jit(solution)/shard_map/ppermute | solution.py:53
  123.0 5.1 %collective-permute-start.8 = (f32[8,128]{1,0:T(8,128)S(1)}, f32[8,128]{1,0:T(8,128)S(1)}, u32[]{:S(2)}, u32[]{:S(2)}) collective-permute-start(f32[8,128]{1,0:T(8,128)S(1)} %get-tuple-element.76.refs_0_), channel_id=1, source_target_pairs={{0,128},{64,192},{128,0},{192,64},{1,129},{65,193},{129,1},{193,65... | collective-permute-start | bytes 12296 | tf_op jit(solution)/shard_map/ppermute | solution.py:53
  124.0 4.9 %collective-permute-start.7 = (f32[8,128]{1,0:T(8,128)S(1)}, f32[8,128]{1,0:T(8,128)S(1)}, u32[]{:S(2)}, u32[]{:S(2)}) collective-permute-start(f32[8,128]{1,0:T(8,128)S(1)} %get-tuple-element.76.refs_0_), channel_id=1, source_target_pairs={{0,64},{64,128},{128,192},{192,0},{1,65},{65,129},{129,193},{193,1... | collective-permute-start | bytes 12296 | tf_op jit(solution)/shard_map/ppermute | solution.py:53
  129.5 4.9 %collective-permute-start.10 = (f32[16,128]{1,0:T(8,128)S(1)}, f32[16,128]{1,0:T(8,128)S(1)}, u32[]{:S(2)}, u32[]{:S(2)}) collective-permute-start(f32[16,128]{1,0:T(8,128)S(1)} %get-tuple-element.83.fterms), channel_id=1, source_target_pairs={{0,64},{64,128},{128,192},{192,0},{1,65},{65,129},{129,193},{193,1... | collective-permute-start | bytes 24584 | tf_op jit(solution)/shard_map/ppermute | solution.py:53
  135.2 1.6 collective-permute-start.11
  173.4 1.7 collective-permute-start.12
  175.8 6.6 %collective-permute-start.15 = (f32[24,128]{1,0:T(8,128)S(1)}, f32[24,128]{1,0:T(8,128)S(1)}, u32[]{:S(2)}, u32[]{:S(2)}) collective-permute-start(f32[24,128]{1,0:T(8,128)S(1)} %get-tuple-element.95), channel_id=1, source_target_pairs={{0,192},{64,0},{128,64},{192,128},{1,193},{65,1},{129,65},{193,129... | collective-permute-start | bytes 36872 | tf_op jit(solution)/shard_map/ppermute | solution.py:53
  176.7 5.1 %collective-permute-start.14 = (f32[8,128]{1,0:T(8,128)S(1)}, f32[8,128]{1,0:T(8,128)S(1)}, u32[]{:S(2)}, u32[]{:S(2)}) collective-permute-start(f32[8,128]{1,0:T(8,128)S(1)} %get-tuple-element.92.refs_0_), channel_id=1, source_target_pairs={{0,128},{64,192},{128,0},{192,64},{1,129},{65,193},{129,1},{193,65... | collective-permute-start | bytes 12296 | tf_op jit(solution)/shard_map/ppermute | solution.py:53
  177.6 4.8 %collective-permute-start.13 = (f32[8,128]{1,0:T(8,128)S(1)}, f32[8,128]{1,0:T(8,128)S(1)}, u32[]{:S(2)}, u32[]{:S(2)}) collective-permute-start(f32[8,128]{1,0:T(8,128)S(1)} %get-tuple-element.92.refs_0_), channel_id=1, source_target_pairs={{0,64},{64,128},{128,192},{192,0},{1,65},{65,129},{129,193},{193,1... | collective-permute-start | bytes 12296 | tf_op jit(solution)/shard_map/ppermute | solution.py:53
  183.5 4.9 %collective-permute-start.16 = (f32[16,128]{1,0:T(8,128)S(1)}, f32[16,128]{1,0:T(8,128)S(1)}, u32[]{:S(2)}, u32[]{:S(2)}) collective-permute-start(f32[16,128]{1,0:T(8,128)S(1)} %get-tuple-element.101.fterms), channel_id=1, source_target_pairs={{0,64},{64,128},{128,192},{192,0},{1,65},{65,129},{129,193},{193,1... | collective-permute-start | bytes 24584 | tf_op jit(solution)/shard_map/ppermute | solution.py:53
  189.0 1.6 collective-permute-start.17
  191.4 17.3 %all-to-all-start.6 = ((f32[32,16,128]{2,1,0:T(8,128)}), f32[32,16,128]{2,1,0:T(8,128)S(1)}, u32[]{:S(2)}, u32[]{:S(2)}) async-start(f32[32,16,128]{2,1,0:T(8,128)} %bitcast.34), calls=%async_computation.6 | async-start | bytes 524288 | tf_op jit(solution)/shard_map/all_to_all | solution.py:313
  (14 other events, 223.7 us)

commit v4 on v3

--- a/solution.py
+++ b/solution.py
@@ -118,29 +118,15 @@
     return sum(partial[pl.ds(q, slices, stride=8), :] for q in range(8))
 
 
-def first_force_kernel(
-    cjac, fjac, cwarm, fwarm, cterms, fterms, cbuf, fbuf, partial, csem, fsem
-):
+def first_force_kernel(cjac, fjac, cwarm, fwarm, cterms, fterms, partial):
     width = COMP * BLK
-    parts = ((fjac, fbuf, fsem, KF, KC), (cjac, cbuf, csem, KC, 0))
-    copies = []
-    for jac, buf, sems, blocks, _ in parts:
-        share = blocks // sems.shape[0]
-        for p in range(sems.shape[0]):
-            rows = pl.ds(p * share * width, share * width)
-            copies.append(pltpu.make_async_copy(jac.at[rows], buf.at[rows], sems.at[p]))
-    for copy in copies:
-        copy.start()
     rows = jnp.concatenate([cwarm[...], fwarm[...], jnp.zeros((128 - KC - KF, width), f32)], 0)
     rows = jnp.concatenate([rows, jnp.zeros((128, 256 - width), f32)], 1)
     turned = jnp.concatenate([rows[:, :128].T, rows[:, 128:].T], 0)[:width]
-    for jac, buf, sems, blocks, base in parts:
-        share = blocks // sems.shape[0]
+    for jac, blocks, base in ((fjac, KF, KC), (cjac, KC, 0)):
         for m in range(blocks):
-            if m % share == 0:
-                copies.pop(0).wait()
             y = jnp.broadcast_to(turned[:, base + m : base + m + 1], (width, 128))
-            products = buf[m * width : (m + 1) * width, :] * y
+            products = jac[m * width : (m + 1) * width, :] * y
             partial[(base + m) * 8 : (base + m + 1) * 8, :] = jnp.sum(
                 products.reshape(width // 8, 8, 128), 0
             )
@@ -148,14 +134,7 @@
     fterms[...] = sum(partial[pl.ds(KC * 8 + q, KF, stride=8), :] for q in range(8))
 
 
-def layout_kernel(cjac, fjac, after, cout, fout, done, cbuf, fbuf, cturn, fturn, sems, outs):
-    copies = [pltpu.make_async_copy(fjac, fbuf, sems.at[0])]
-    for p in range(4):
-        rows = pl.ds(p * KC * COMP * BLK // 4, KC * COMP * BLK // 4)
-        copies.append(pltpu.make_async_copy(cjac.at[rows], cbuf.at[rows], sems.at[1 + p]))
-    for copy in copies:
-        copy.start()
-
+def layout_kernel(cjac, fjac, after, cout, fout, done, cturn, fturn, outs):
     def turn(jac, out, parts, depth, first, count):
         k = 128 // parts
 
@@ -169,15 +148,12 @@
 
         lax.fori_loop(first, first + count, one, 0, unroll=8)
 
-    copies[0].wait()
-    turn(fbuf, fturn, GF, IF, 0, SF)
+    turn(fjac, fturn, GF, IF, 0, SF)
     leaving = [pltpu.make_async_copy(fturn, fout, outs.at[0])]
     leaving[0].start()
-    for copy in copies[1:]:
-        copy.wait()
     share = SC // 6
     for part in range(6):
-        turn(cbuf, cturn, GC, IC, part * share, share)
+        turn(cjac, cturn, GC, IC, part * share, share)
         rows = pl.ds(part * share * 128, share * 128)
         leaving.append(pltpu.make_async_copy(cturn.at[rows], cout.at[rows], outs.at[part + 1]))
         leaving[-1].start()
@@ -219,35 +195,50 @@
             half[at, :] = half[at, :] + jnp.where(here, value, 0.0)
 
 
-def owner_kernel(with_sums, received, free, mass, last, spread, done, owned, pieces):
+def owner_kernel(received, free, mass, last, spread, done, owned, pieces):
     total = jnp.sum(received[...], 0)
     owned[...] = total
     piece = free[...] + mass[...] * total
-    if with_sums:
-        change = total - last[...]
-        curve = jnp.sum(mass[...] * change * change)
-        row = lax.broadcasted_iota(jnp.int32, (8, 128), 0)
-        sums = jnp.where(row == 0, jnp.sum(spread[...]), curve)
-        piece = jnp.concatenate([piece, sums], 0)
-    pieces[...] = jnp.broadcast_to(piece, pieces.shape)
-
-
-def far_kernel(with_sums, rows, swap, panel, far, *sums):
+    change = total - last[...]
+    curve = jnp.sum(mass[...] * change * change)
+    row = lax.broadcasted_iota(jnp.int32, (2, 128), 0)
+    sums = jnp.where(row == 0, jnp.sum(spread[...]), curve)
+    pairs = [piece[2 * p : 2 * p + 2] for p in range(OWN // 2)] + [sums]
+    pieces[...] = jnp.broadcast_to(jnp.concatenate(pairs, 1)[None], pieces.shape)
+
+
+def pair_at(panels, slot, pair):
+    mine = slot < CHIPS
+    chip = jnp.where(mine, slot, slot - CHIPS)
+    lanes = pl.ds(pl.multiple_of(pair * 128, 128), 128)
+    own, other = (panel[pl.ds(chip, 1), :, lanes] for panel in panels)
+    return jnp.where(mine, own, other).reshape(2, 128)
+
+
+def far_kernel(slots, pairs, odd, swap, own, other, far, sums):
     base = 2 * KC + KF
-    picked = jnp.concatenate([panel[pl.ds(rows[base + m], 1), :] for m in range(KF)], 0)
-    far[0:KF, :] = jnp.where(swap[base:, :] > 0, pltpu.roll(picked, BLK, 1), picked)
-    if with_sums:
-        size = OWN + 8
-        total = sum(panel[p * size + OWN : (p + 1) * size, :] for p in range(NC * CHIPS))
-        sums[0][...] = total
-        far[KF:, :] = total
-
-
-def gradient_kernel(rows, swap, panel, jac, y, live, grad, fown, picked, partial):
-    for m in range(2 * KC + KF):
-        picked[m : m + 1, :] = panel[pl.ds(rows[m], 1), :]
-    x = picked[...]
-    x = jnp.where(swap[0 : 2 * KC + KF, :] > 0, pltpu.roll(x, BLK, 1), x)
+    picked = [pair_at((own, other), slots[base + m], pairs[base + m]) for m in range(KF)]
+    upper = jnp.concatenate([two[0:1] for two in picked], 0)
+    lower = jnp.concatenate([two[1:2] for two in picked], 0)
+    x = jnp.where(odd[base:, :] > 0, lower, upper)
+    far[0:KF, :] = jnp.where(swap[base:, :] > 0, pltpu.roll(x, BLK, 1), x)
+    at = OWN // 2 * 128
+    total = sum(panel[chip, :, at : at + 128] for panel in (own, other) for chip in range(CHIPS))
+    total = jnp.concatenate([total, jnp.zeros((6, 128), f32)], 0)
+    sums[...] = total
+    far[KF:, :] = total
+
+
+def gradient_kernel(
+    slots, pairs, odd, swap, own, other, jac, y, live, grad, fown, upper, lower, partial
+):
+    count = 2 * KC + KF
+    for m in range(count):
+        two = pair_at((own, other), slots[m], pairs[m])
+        upper[m : m + 1, :] = two[0:1]
+        lower[m : m + 1, :] = two[1:2]
+    x = jnp.where(odd[0:count, :] > 0, lower[...], upper[...])
+    x = jnp.where(swap[0:count, :] > 0, pltpu.roll(x, BLK, 1), x)
     fown[...] = x[2 * KC :]
     joined = jnp.where(left_half(KC), x[0:KC], x[KC : 2 * KC])
     velocity = jnp.concatenate([joined] * GC, 0).T
@@ -315,7 +306,7 @@
 
 def all_gather(pieces):
     half = exchange(pieces)
-    return jnp.stack([half, other_core(half)]).reshape(-1, 128)
+    return half, other_core(half)
 
 
 def on_device(
@@ -346,7 +337,8 @@
     slot = (owner - lax.axis_index("grp")) % NC * CHIPS + owner // NC
     row = targets % (2 * OWN) // 2
     sum_rows = slot * OWN + row
-    panel_rows = [slot * OWN + row] + [slot * (OWN + 8) + row] * (ITERS - 1)
+    pair = row // 2
+    odd = jnp.broadcast_to((row % 2).astype(f32)[:, None], (targets.shape[0], 128))
     order = jnp.arange(targets.shape[0])
     right = ((order >= KC) & (order < 2 * KC)) | (order >= 2 * KC + KF)
     swap = jnp.broadcast_to(
@@ -374,19 +366,13 @@
     betas = momentum_weights(ITERS)
     cwarm = warm_contact * live[0, :KC, None]
     crows, frows = contact_jac.reshape(-1, 128), face_jac.reshape(-1, 128)
-    cbuf, fbuf = pltpu.VMEM((SC * 128, 128), f32), pltpu.VMEM((SF * 128, 128), f32)
+    cturn, fturn = pltpu.VMEM((SC * 128, 128), f32), pltpu.VMEM((SF * 128, 128), f32)
     cterms, fterms = kernel_call(
         first_force_kernel,
         (shape(KC, 128), shape(KF, 128)),
-        [hbm, hbm, vmem, vmem],
-        [
-            cbuf,
-            fbuf,
-            pltpu.VMEM(((KC + KF) * 8, 128), f32),
-            pltpu.SemaphoreType.DMA((16,)),
-            pltpu.SemaphoreType.DMA((4,)),
-        ],
-        56,
+        [vmem] * 4,
+        [pltpu.VMEM(((KC + KF) * 8, 128), f32)],
+        10,
     )(crows, frows, cwarm, warm_face)
     arriving = shifted(fterms, "slab", 1)
     cnow = to_lanes(cwarm, GC)
@@ -401,42 +387,38 @@
             cjac, fjac, done = kernel_call(
                 layout_kernel,
                 (shape(SC * 128, 128), shape(SF * 128, 128), shape(8, 128)),
-                [hbm, hbm, hbm],
-                [
-                    cbuf,
-                    fbuf,
-                    cbuf,
-                    fbuf,
-                    pltpu.SemaphoreType.DMA((5,)),
-                    pltpu.SemaphoreType.DMA((7,)),
-                ],
-                56,
+                [vmem, vmem, vmem],
+                [cturn, fturn, pltpu.SemaphoreType.DMA((7,))],
+                52,
                 (hbm, hbm, vmem),
                 pl.CostEstimate(flops=0, bytes_accessed=40 << 20, transcendentals=0),
-            )(crows, frows, half[0, 0:8])
-        extra = 8 if turn > 0 else 0
+            )(crows, frows, half)
         owned, pieces = kernel_call(
-            functools.partial(owner_kernel, turn > 0),
-            (shape(OWN, 128), shape(CHIPS, OWN + extra, 128)),
+            owner_kernel,
+            (shape(OWN, 128), shape(CHIPS, 2, (OWN // 2 + 1) * 128)),
             [vmem] * 6,
         )(received, free_own, mass_own, owned, spread, done)
-        panel = all_gather(pieces)
-        picked = kernel_call(
-            functools.partial(far_kernel, turn > 0),
-            (shape(KF + extra, 128), shape(8, 128))[: 2 if turn > 0 else 1],
-            [smem, vmem, vmem],
-        )(panel_rows[turn], swap, panel)
-        returning = shifted(picked[0], "slab", -1)
+        panels = all_gather(pieces)
+        far, slab_sums = kernel_call(
+            far_kernel,
+            (shape(KF + 8, 128), shape(8, 128)),
+            [smem, smem] + [vmem] * 4,
+        )(slot, pair, odd, swap, *panels)
+        returning = shifted(far, "slab", -1)
         if turn == 0:
             steps = [jnp.broadcast_to(first_step[:, None], (1, 128))] * 3
         else:
-            steps = [picked[1]] + [shifted(picked[1], "slab", by) for by in (1, 2)]
+            steps = [slab_sums] + [shifted(slab_sums, "slab", by) for by in (1, 2)]
         grad, fown = kernel_call(
             gradient_kernel,
             (shape(SC, 128), shape(KF, 128)),
-            [smem] + [vmem] * 5,
-            [pltpu.VMEM((2 * KC + KF, 128), f32), pltpu.VMEM((SC * 8, 128), f32)],
-        )(panel_rows[turn], swap, panel, cjac, cy, live)
+            [smem, smem] + [vmem] * 7,
+            [
+                pltpu.VMEM((2 * KC + KF, 128), f32),
+                pltpu.VMEM((2 * KC + KF, 128), f32),
+                pltpu.VMEM((SC * 8, 128), f32),
+            ],
+        )(slot, pair, odd, swap, *panels, cjac, cy, live)
         body = functools.partial(update_kernel, turn == 0, betas[turn], turn == ITERS - 1)
         cnow, fnow, cy, fy, spread, fterms = kernel_call(
             body,

time: 210 us -> 204 us (0.971)
  blocking collectives: 93.5 us -> 89.9 us
  Pallas kernels: 39.3 us -> 36.6 us
    all_to_all x5, blocking collectives: 93.5 us -> 89.9 us  [exchange(): lax.all_to_all(parts, 'grp', 0, 0, axis_index_groups=groups, tiled=True)]
    pallas_call x10, Pallas kernels: 15 us -> 11.7 us  [the longest x3 5.8 us: on_device(): kernel_call(gradient_kernel, (shape(SC, 128), shape(KF, 128)), [smem, sme...]
    unnamed x39 -> x31, local copies, waits for them, and re-layouts: 6.48 us -> 9.23 us
  transfers between devices with their start and end apart: 20 -> 20, of which waited for: 16 -> 16; matrix products, arithmetic and copies ran while one was open for 2% -> 1% of each run, Pallas kernels for 11% -> 13%
where the time goes in v4:
time: 204 us
  blocking collectives  89.9 us (44%)
  Pallas kernels  36.6 us (18%)
  waiting for transfers between devices  35.2 us (17%)
  starting transfers between devices  25.7 us (13%)
  local copies, waits for them, and re-layouts  10.4 us (5%)
  other arithmetic  3.46 us (2%)
  between operations  2.4 us (1%)
    all_to_all x5, blocking collectives, exchange(): lax.all_to_all(parts, 'grp', 0, 0, axis_index_groups=groups, tiled=True)  89.9 us
    all_to_all x2, starting transfers between devices, exchange(): lax.all_to_all(parts, 'grp', 0, 0, axis_index_groups=groups, tiled=True)  16 us
    ppermute x11, waiting for transfers between devices, shifted(): lax.ppermute(x, axis, [(i, (i + by) % devices) for i in range(devices)])  13.6 us
    pallas_call x1, Pallas kernels, on_device(): kernel_call(layout_kernel, (shape(SC * 128, 128), shape(SF * 128, 128), s...  12.9 us
    all_to_all x2, waiting for transfers between devices, exchange(): lax.all_to_all(parts, 'grp', 0, 0, axis_index_groups=groups, tiled=True)  10.9 us
    ppermute x7, waiting for transfers between devices, other_core(): return lax.ppermute(x, 'grp', [(i, i ^ 1) for i in range(devices)])  10.6 us
    ppermute x11, starting transfers between devices, shifted(): lax.ppermute(x, axis, [(i, (i + by) % devices) for i in range(devices)])  9.35 us
    unnamed x31, local copies, waits for them, and re-layouts  9.23 us
  transfers between devices with their start and end apart: 20, of which 16 were waited for; matrix products, arithmetic and copies ran while one was open for 1% of the time, Pallas kernels for 13%

profile of v4, /device:TPU:32, one launch (start us, length us, event | category | flops | bytes accessed | tf_op | source)
XLA Modules:
  0.0 203.6 jit_solution(11193950881148393409)
XLA Ops:
  2.3 2.8 %copy-done.2 = f32[64,3,64,128]{3,2,1,0:T(8,128)S(1)} copy-done((f32[64,3,64,128]{3,2,1,0:T(8,128)S(1)}, f32[64,3,64,128]{3,2,1,0:T(8,128)}, u32[]{:S(2)}) %copy-start.2) | copy-done | bytes 6291480
  7.2 2.3 %shard_map.157 = (f32[64,128]{1,0:T(8,128)S(1)}, f32[16,128]{1,0:T(8,128)S(1)}) custom-call(f32[12288,128]{1,0:T(8,128)S(1)} %bitcast.45, f32[3072,128]{1,0:T(8,128)S(1)} %bitcast.47, f32[64,192]{1,0:T(8,128)S(1)} %broadcast_multiply_fusion.cwarm, f32[16,192]{1,0:T(8,128)S(1)} %copy-done.6), custom_call_target="tpu_custom_call" | custom-call | tf_op jit(solution)/shard_map/pallas_call | solution.py:370
  9.6 1.6 collective-permute-start
  12.7 1.8 collective-permute-done.arriving
  17.6 11.4 %all-to-all-start = ((f32[32,16,128]{2,1,0:T(8,128)}), f32[32,16,128]{2,1,0:T(8,128)S(1)}, u32[]{:S(2)}, u32[]{:S(2)}) async-start(f32[32,16,128]{2,1,0:T(8,128)} %bitcast.7.after), calls=%async_computation | async-start | bytes 524288 | tf_op jit(solution)/shard_map/all_to_all | solution.py:304
  29.0 12.9 %shard_map.160 = (f32[12288,128]{1,0:T(8,128)}, f32[3072,128]{1,0:T(8,128)S(1)}, f32[8,128]{1,0:T(8,128)S(1)}) custom-call(f32[12288,128]{1,0:T(8,128)} %bitcast.44, f32[3072,128]{1,0:T(8,128)} %bitcast.46, f32[32,16,128]{2,1,0:T(8,128)} %bitcast.7.after), custom_call_target="tpu_custom_call" | custom-call | bytes 41943040 | tf_op jit(solution)/shard_map/pallas_call | solution.py:387
  42.1 22.3 %all_to_all.35.own = f32[32,2,1152]{2,1,0:T(2,128)S(1)} all-to-all(f32[32,2,1152]{2,1,0:T(2,128)S(1)} %get-tuple-element.63), channel_id=1, replica_groups={{0,2,4,6,8,10,12,14,16,18,20,22,24,26,28,30,32,34,36,38,40,42,44,46,48,..., dimensions={0} | all-to-all | bytes 589824 | tf_op jit(solution)/shard_map/all_to_all | solution.py:304
  67.3 1.5 collective-permute-start.3
  70.5 2.8 %copy-done = f32[12288,128]{1,0:T(8,128)S(1)} copy-done((f32[12288,128]{1,0:T(8,128)S(1)}, f32[12288,128]{1,0:T(8,128)}, u32[]{:S(2)}) %copy-start) | copy-done | bytes 6291480
  73.2 1.9 shard_map.162
  78.2 2.5 %collective-permute-done.4.arriving = f32[16,128]{1,0:T(8,128)S(1)} collective-permute-done((f32[16,128]{1,0:T(8,128)S(1)}, f32[16,128]{1,0:T(8,128)S(1)}, u32[]{:S(2)}, u32[]{:S(2)}) %collective-permute-start.4) | collective-permute-done | bytes 8224 | tf_op jit(solution)/shard_map/ppermute | solution.py:53
  83.0 17.0 %all_to_all.36.received = f32[32,16,128]{2,1,0:T(8,128)S(1)} all-to-all(f32[32,16,128]{2,1,0:T(8,128)S(1)} %bitcast.55), channel_id=1, replica_groups={{0,2,4,6,8,10,12,14,16,18,20,22,24,26,28,30,32,34,36,38,40,42,44,46,48,..., dimensions={0} | all-to-all | bytes 524288 | tf_op jit(solution)/shard_map/all_to_all | solution.py:304
  100.2 16.8 %all_to_all.37.own = f32[32,2,1152]{2,1,0:T(2,128)S(1)} all-to-all(f32[32,2,1152]{2,1,0:T(2,128)S(1)} %get-tuple-element.77), channel_id=1, replica_groups={{0,2,4,6,8,10,12,14,16,18,20,22,24,26,28,30,32,34,36,38,40,42,44,46,48,..., dimensions={0} | all-to-all | bytes 589824 | tf_op jit(solution)/shard_map/all_to_all | solution.py:304
  117.1 1.6 collective-permute-done.6.other
  121.4 1.9 shard_map.170
  129.0 2.1 %collective-permute-done.10.arriving = f32[16,128]{1,0:T(8,128)S(1)} collective-permute-done((f32[16,128]{1,0:T(8,128)S(1)}, f32[16,128]{1,0:T(8,128)S(1)}, u32[]{:S(2)}, u32[]{:S(2)}) %collective-permute-start.10) | collective-permute-done | bytes 8224 | tf_op jit(solution)/shard_map/ppermute | solution.py:53
  133.5 17.0 %all_to_all.38.received = f32[32,16,128]{2,1,0:T(8,128)S(1)} all-to-all(f32[32,16,128]{2,1,0:T(8,128)S(1)} %bitcast.56), channel_id=1, replica_groups={{0,2,4,6,8,10,12,14,16,18,20,22,24,26,28,30,32,34,36,38,40,42,44,46,48,..., dimensions={0} | all-to-all | bytes 524288 | tf_op jit(solution)/shard_map/all_to_all | solution.py:304
  151.1 16.8 %all_to_all.39.own = f32[32,2,1152]{2,1,0:T(2,128)S(1)} all-to-all(f32[32,2,1152]{2,1,0:T(2,128)S(1)} %get-tuple-element.93), channel_id=1, replica_groups={{0,2,4,6,8,10,12,14,16,18,20,22,24,26,28,30,32,34,36,38,40,42,44,46,48,..., dimensions={0} | all-to-all | bytes 589824 | tf_op jit(solution)/shard_map/all_to_all | solution.py:304
  168.0 1.6 collective-permute-done.12.other
  172.3 1.9 shard_map.177
  174.3 1.9 collective-permute-done.14.refs_2_
  180.4 2.3 %collective-permute-done.16.arriving = f32[16,128]{1,0:T(8,128)S(1)} collective-permute-done((f32[16,128]{1,0:T(8,128)S(1)}, f32[16,128]{1,0:T(8,128)S(1)}, u32[]{:S(2)}, u32[]{:S(2)}) %collective-permute-start.16) | collective-permute-done | bytes 8224 | tf_op jit(solution)/shard_map/ppermute | solution.py:53
  185.7 4.6 %all-to-all-start.6 = ((f32[32,16,128]{2,1,0:T(8,128)}), f32[32,16,128]{2,1,0:T(8,128)S(1)}, u32[]{:S(2)}, u32[]{:S(2)}) async-start(f32[32,16,128]{2,1,0:T(8,128)} %bitcast.24), calls=%async_computation.6 | async-start | bytes 524288 | tf_op jit(solution)/shard_map/all_to_all | solution.py:304
  192.0 10.9 %all-to-all-done.6 = f32[32,16,128]{2,1,0:T(8,128)S(1)} async-done(((f32[32,16,128]{2,1,0:T(8,128)}), f32[32,16,128]{2,1,0:T(8,128)S(1)}, u32[]{:S(2)}, u32[]{:S(2)}) %all-to-all-start.6) | async-done | bytes 262176 | tf_op jit(solution)/shard_map/all_to_all | solution.py:304
  (111 shorter events, 40.8 us)
Async XLA Ops:
  9.5 54.8 %copy-start.8 = (s32[64,64]{1,0:T(8,128)S(1)}, s32[64,64]{1,0:T(8,128)}, u32[]{:S(2)}) copy-start(s32[64,64]{1,0:T(8,128)} %param.16) | copy-start | bytes 49156
  9.6 54.8 %copy-start.10 = (f32[8]{0:T(128)S(1)}, f32[8]{0:T(128)}, u32[]{:S(2)}) copy-start(f32[8]{0:T(128)} %param.26) | copy-start | bytes 100
  9.6 59.2 %copy-start.9 = (s32[16,64]{1,0:T(8,128)S(1)}, s32[16,64]{1,0:T(8,128)}, u32[]{:S(2)}) copy-start(s32[16,64]{1,0:T(8,128)} %param.21) | copy-start | bytes 12292
  9.6 59.4 %copy-start.7 = (f32[16,192]{1,0:T(8,128)S(1)}, f32[16,192]{1,0:T(8,128)}, u32[]{:S(2)}) copy-start(f32[16,192]{1,0:T(8,128)} %fwarm.1) | copy-start | bytes 36868
  9.6 4.9 %collective-permute-start = (f32[16,128]{1,0:T(8,128)S(1)}, f32[16,128]{1,0:T(8,128)S(1)}, u32[]{:S(2)}, u32[]{:S(2)}) collective-permute-start(f32[16,128]{1,0:T(8,128)S(1)} %get-tuple-element.56.fterms), channel_id=1, source_target_pairs={{0,64},{64,128},{128,192},{192,0},{1,65},{65,129},{129,193},{193,1... | collective-permute-start | bytes 24584 | tf_op jit(solution)/shard_map/ppermute | solution.py:53
  15.2 1.6 collective-permute-start.1
  17.6 24.3 %all-to-all-start = ((f32[32,16,128]{2,1,0:T(8,128)}), f32[32,16,128]{2,1,0:T(8,128)S(1)}, u32[]{:S(2)}, u32[]{:S(2)}) async-start(f32[32,16,128]{2,1,0:T(8,128)} %bitcast.7.after), calls=%async_computation | async-start | bytes 524288 | tf_op jit(solution)/shard_map/all_to_all | solution.py:304
  64.4 1.6 collective-permute-start.2
  67.3 7.9 %collective-permute-start.3 = (f32[24,128]{1,0:T(8,128)S(1)}, f32[24,128]{1,0:T(8,128)S(1)}, u32[]{:S(2)}, u32[]{:S(2)}) collective-permute-start(f32[24,128]{1,0:T(8,128)S(1)} %get-tuple-element.67), channel_id=1, source_target_pairs={{0,192},{64,0},{128,64},{192,128},{1,193},{65,1},{129,65},{193,129... | collective-permute-start | bytes 36872 | tf_op jit(solution)/shard_map/ppermute | solution.py:53
  75.7 4.9 %collective-permute-start.4 = (f32[16,128]{1,0:T(8,128)S(1)}, f32[16,128]{1,0:T(8,128)S(1)}, u32[]{:S(2)}, u32[]{:S(2)}) collective-permute-start(f32[16,128]{1,0:T(8,128)S(1)} %get-tuple-element.69.fterms), channel_id=1, source_target_pairs={{0,64},{64,128},{128,192},{192,0},{1,65},{65,129},{129,193},{193,1... | collective-permute-start | bytes 24584 | tf_op jit(solution)/shard_map/ppermute | solution.py:53
  81.4 1.6 collective-permute-start.5
  117.1 1.6 collective-permute-start.6
  119.3 6.3 %collective-permute-start.9 = (f32[24,128]{1,0:T(8,128)S(1)}, f32[24,128]{1,0:T(8,128)S(1)}, u32[]{:S(2)}, u32[]{:S(2)}) collective-permute-start(f32[24,128]{1,0:T(8,128)S(1)} %get-tuple-element.81), channel_id=1, source_target_pairs={{0,192},{64,0},{128,64},{192,128},{1,193},{65,1},{129,65},{193,129... | collective-permute-start | bytes 36872 | tf_op jit(solution)/shard_map/ppermute | solution.py:53
  119.7 5.1 %collective-permute-start.8 = (f32[8,128]{1,0:T(8,128)S(1)}, f32[8,128]{1,0:T(8,128)S(1)}, u32[]{:S(2)}, u32[]{:S(2)}) collective-permute-start(f32[8,128]{1,0:T(8,128)S(1)} %get-tuple-element.78.refs_0_), channel_id=1, source_target_pairs={{0,128},{64,192},{128,0},{192,64},{1,129},{65,193},{129,1},{193,65... | collective-permute-start | bytes 12296 | tf_op jit(solution)/shard_map/ppermute | solution.py:53
  120.7 4.9 %collective-permute-start.7 = (f32[8,128]{1,0:T(8,128)S(1)}, f32[8,128]{1,0:T(8,128)S(1)}, u32[]{:S(2)}, u32[]{:S(2)}) collective-permute-start(f32[8,128]{1,0:T(8,128)S(1)} %get-tuple-element.78.refs_0_), channel_id=1, source_target_pairs={{0,64},{64,128},{128,192},{192,0},{1,65},{65,129},{129,193},{193,1... | collective-permute-start | bytes 12296 | tf_op jit(solution)/shard_map/ppermute | solution.py:53
  126.2 4.9 %collective-permute-start.10 = (f32[16,128]{1,0:T(8,128)S(1)}, f32[16,128]{1,0:T(8,128)S(1)}, u32[]{:S(2)}, u32[]{:S(2)}) collective-permute-start(f32[16,128]{1,0:T(8,128)S(1)} %get-tuple-element.85.fterms), channel_id=1, source_target_pairs={{0,64},{64,128},{128,192},{192,0},{1,65},{65,129},{129,193},{193,1... | collective-permute-start | bytes 24584 | tf_op jit(solution)/shard_map/ppermute | solution.py:53
  131.8 1.6 collective-permute-start.11
  168.0 1.6 collective-permute-start.12
  170.2 6.6 %collective-permute-start.15 = (f32[24,128]{1,0:T(8,128)S(1)}, f32[24,128]{1,0:T(8,128)S(1)}, u32[]{:S(2)}, u32[]{:S(2)}) collective-permute-start(f32[24,128]{1,0:T(8,128)S(1)} %get-tuple-element.97), channel_id=1, source_target_pairs={{0,192},{64,0},{128,64},{192,128},{1,193},{65,1},{129,65},{193,129... | collective-permute-start | bytes 36872 | tf_op jit(solution)/shard_map/ppermute | solution.py:53
  171.1 5.1 %collective-permute-start.14 = (f32[8,128]{1,0:T(8,128)S(1)}, f32[8,128]{1,0:T(8,128)S(1)}, u32[]{:S(2)}, u32[]{:S(2)}) collective-permute-start(f32[8,128]{1,0:T(8,128)S(1)} %get-tuple-element.94.refs_0_), channel_id=1, source_target_pairs={{0,128},{64,192},{128,0},{192,64},{1,129},{65,193},{129,1},{193,65... | collective-permute-start | bytes 12296 | tf_op jit(solution)/shard_map/ppermute | solution.py:53
  172.0 4.8 %collective-permute-start.13 = (f32[8,128]{1,0:T(8,128)S(1)}, f32[8,128]{1,0:T(8,128)S(1)}, u32[]{:S(2)}, u32[]{:S(2)}) collective-permute-start(f32[8,128]{1,0:T(8,128)S(1)} %get-tuple-element.94.refs_0_), channel_id=1, source_target_pairs={{0,64},{64,128},{128,192},{192,0},{1,65},{65,129},{129,193},{193,1... | collective-permute-start | bytes 12296 | tf_op jit(solution)/shard_map/ppermute | solution.py:53
  177.8 4.9 %collective-permute-start.16 = (f32[16,128]{1,0:T(8,128)S(1)}, f32[16,128]{1,0:T(8,128)S(1)}, u32[]{:S(2)}, u32[]{:S(2)}) collective-permute-start(f32[16,128]{1,0:T(8,128)S(1)} %get-tuple-element.103.fterms), channel_id=1, source_target_pairs={{0,64},{64,128},{128,192},{192,0},{1,65},{65,129},{129,193},{193,1... | collective-permute-start | bytes 24584 | tf_op jit(solution)/shard_map/ppermute | solution.py:53
  183.4 1.6 collective-permute-start.17
  185.7 17.2 %all-to-all-start.6 = ((f32[32,16,128]{2,1,0:T(8,128)}), f32[32,16,128]{2,1,0:T(8,128)S(1)}, u32[]{:S(2)}, u32[]{:S(2)}) async-start(f32[32,16,128]{2,1,0:T(8,128)} %bitcast.24), calls=%async_computation.6 | async-start | bytes 524288 | tf_op jit(solution)/shard_map/all_to_all | solution.py:304
  (10 other events, 107.1 us)

commit v5 on v4

--- a/solution.py
+++ b/solution.py
@@ -134,28 +134,38 @@
     fterms[...] = sum(partial[pl.ds(KC * 8 + q, KF, stride=8), :] for q in range(8))
 
 
-def layout_kernel(cjac, fjac, after, cout, fout, done, cturn, fturn, outs):
+def layout_kernel(
+    cjac, fjac, after, cout, fout, done, cbuf, fbuf, cturn, fturn, sems, outs
+):
+    width = COMP * BLK
+    copies = [pltpu.make_async_copy(fjac, fbuf, sems.at[COMP])]
+    for c in range(COMP):
+        rows = pl.ds(c * BLK, BLK)
+        copies.append(pltpu.make_async_copy(cjac.at[:, rows], cbuf.at[:, rows], sems.at[c]))
+    for copy in copies:
+        copy.start()
+
     def turn(jac, out, parts, depth, first, count):
         k = 128 // parts
+        flat = jac.reshape(k * width, 128)
 
         def one(s, _):
             row = s // depth * BLK + s % depth
-            rows = [
-                jac[pl.ds(row + p * depth, k, stride=COMP * BLK), :] for p in range(parts)
-            ]
+            rows = [flat[pl.ds(row + p * depth, k, stride=width), :] for p in range(parts)]
             out[rows_of(s), :] = jnp.concatenate(rows, 0).T
             return _
 
         lax.fori_loop(first, first + count, one, 0, unroll=8)
 
-    turn(fjac, fturn, GF, IF, 0, SF)
-    leaving = [pltpu.make_async_copy(fturn, fout, outs.at[0])]
+    copies[0].wait()
+    turn(fbuf, fturn, GF, IF, 0, SF)
+    leaving = [pltpu.make_async_copy(fturn, fout, outs.at[COMP])]
     leaving[0].start()
-    share = SC // 6
-    for part in range(6):
-        turn(cjac, cturn, GC, IC, part * share, share)
-        rows = pl.ds(part * share * 128, share * 128)
-        leaving.append(pltpu.make_async_copy(cturn.at[rows], cout.at[rows], outs.at[part + 1]))
+    for c in range(COMP):
+        copies[1 + c].wait()
+        turn(cbuf, cturn, GC, IC, c * IC, IC)
+        rows = pl.ds(c * IC * 128, IC * 128)
+        leaving.append(pltpu.make_async_copy(cturn.at[rows], cout.at[rows], outs.at[c]))
         leaving[-1].start()
     done[...] = jnp.zeros_like(done)
     for copy in leaving:
@@ -207,43 +217,44 @@
     pieces[...] = jnp.broadcast_to(jnp.concatenate(pairs, 1)[None], pieces.shape)
 
 
-def pair_at(panels, slot, pair):
-    mine = slot < CHIPS
-    chip = jnp.where(mine, slot, slot - CHIPS)
-    lanes = pl.ds(pl.multiple_of(pair * 128, 128), 128)
-    own, other = (panel[pl.ds(chip, 1), :, lanes] for panel in panels)
-    return jnp.where(mine, own, other).reshape(2, 128)
-
-
-def far_kernel(slots, pairs, odd, swap, own, other, far, sums):
+def pick(chips, pairs, odd, afar, panels, scratch, first, count):
+    for m in range(count):
+        lanes = pl.ds(pl.multiple_of(pairs[first + m] * 128, 128), 128)
+        chip = pl.ds(chips[first + m], 1)
+        for panel, both in zip(panels, scratch):
+            both[2 * m : 2 * m + 2, :] = panel[chip, :, lanes].reshape(2, 128)
+    at = pl.ds(first, count)
+    lower, other = odd[at, :] > 0, afar[at, :] > 0
+    rows = [
+        jnp.where(
+            lower, both[pl.ds(1, count, stride=2), :], both[pl.ds(0, count, stride=2), :]
+        )
+        for both in scratch
+    ]
+    return jnp.where(other, rows[1], rows[0])
+
+
+def far_kernel(chips, pairs, odd, afar, swap, own, other, far, *scratch):
     base = 2 * KC + KF
-    picked = [pair_at((own, other), slots[base + m], pairs[base + m]) for m in range(KF)]
-    upper = jnp.concatenate([two[0:1] for two in picked], 0)
-    lower = jnp.concatenate([two[1:2] for two in picked], 0)
-    x = jnp.where(odd[base:, :] > 0, lower, upper)
+    x = pick(chips, pairs, odd, afar, (own, other), scratch, base, KF)
     far[0:KF, :] = jnp.where(swap[base:, :] > 0, pltpu.roll(x, BLK, 1), x)
     at = OWN // 2 * 128
     total = sum(panel[chip, :, at : at + 128] for panel in (own, other) for chip in range(CHIPS))
-    total = jnp.concatenate([total, jnp.zeros((6, 128), f32)], 0)
-    sums[...] = total
-    far[KF:, :] = total
+    far[KF:, :] = jnp.concatenate([total, jnp.zeros((6, 128), f32)], 0)
 
 
 def gradient_kernel(
-    slots, pairs, odd, swap, own, other, jac, y, live, grad, fown, upper, lower, partial
+    chips, pairs, odd, afar, swap, own, other, sums, jac, y, live, grad, fown, sums_out, *scratch
 ):
     count = 2 * KC + KF
-    for m in range(count):
-        two = pair_at((own, other), slots[m], pairs[m])
-        upper[m : m + 1, :] = two[0:1]
-        lower[m : m + 1, :] = two[1:2]
-    x = jnp.where(odd[0:count, :] > 0, lower[...], upper[...])
+    x = pick(chips, pairs, odd, afar, (own, other), scratch[:2], 0, count)
     x = jnp.where(swap[0:count, :] > 0, pltpu.roll(x, BLK, 1), x)
     fown[...] = x[2 * KC :]
     joined = jnp.where(left_half(KC), x[0:KC], x[KC : 2 * KC])
     velocity = jnp.concatenate([joined] * GC, 0).T
-    raw = product(jac, velocity, partial, SC)
+    raw = product(jac, velocity, scratch[2], SC)
     grad[...] = (raw + regular_weight * y[...]) * live[...]
+    sums_out[...] = sums[KF:, :]
 
 
 def cone(pushed, friction):
@@ -339,6 +350,8 @@
     sum_rows = slot * OWN + row
     pair = row // 2
     odd = jnp.broadcast_to((row % 2).astype(f32)[:, None], (targets.shape[0], 128))
+    afar = jnp.broadcast_to((slot // CHIPS).astype(f32)[:, None], (targets.shape[0], 128))
+    chip = slot % CHIPS
     order = jnp.arange(targets.shape[0])
     right = ((order >= KC) & (order < 2 * KC)) | (order >= 2 * KC + KF)
     swap = jnp.broadcast_to(
@@ -387,38 +400,46 @@
             cjac, fjac, done = kernel_call(
                 layout_kernel,
                 (shape(SC * 128, 128), shape(SF * 128, 128), shape(8, 128)),
-                [vmem, vmem, vmem],
-                [cturn, fturn, pltpu.SemaphoreType.DMA((7,))],
-                52,
+                [hbm, hbm, vmem],
+                [
+                    pltpu.VMEM((KC, COMP * BLK, 128), f32),
+                    pltpu.VMEM((KF, COMP * BLK, 128), f32),
+                    cturn,
+                    fturn,
+                    pltpu.SemaphoreType.DMA((COMP + 1,)),
+                    pltpu.SemaphoreType.DMA((COMP + 1,)),
+                ],
+                54,
                 (hbm, hbm, vmem),
                 pl.CostEstimate(flops=0, bytes_accessed=40 << 20, transcendentals=0),
-            )(crows, frows, half)
+            )(
+                contact_jac.reshape(KC, COMP * BLK, 128),
+                face_jac.reshape(KF, COMP * BLK, 128),
+                half,
+            )
         owned, pieces = kernel_call(
             owner_kernel,
             (shape(OWN, 128), shape(CHIPS, 2, (OWN // 2 + 1) * 128)),
             [vmem] * 6,
         )(received, free_own, mass_own, owned, spread, done)
         panels = all_gather(pieces)
-        far, slab_sums = kernel_call(
+        far = kernel_call(
             far_kernel,
-            (shape(KF + 8, 128), shape(8, 128)),
-            [smem, smem] + [vmem] * 4,
-        )(slot, pair, odd, swap, *panels)
+            shape(KF + 8, 128),
+            [smem, smem] + [vmem] * 5,
+            [pltpu.VMEM((2 * KF, 128), f32)] * 2,
+        )(chip, pair, odd, afar, swap, *panels)
         returning = shifted(far, "slab", -1)
+        grad, fown, slab_sums = kernel_call(
+            gradient_kernel,
+            (shape(SC, 128), shape(KF, 128), shape(8, 128)),
+            [smem, smem] + [vmem] * 9,
+            [pltpu.VMEM((2 * (2 * KC + KF), 128), f32)] * 2 + [pltpu.VMEM((SC * 8, 128), f32)],
+        )(chip, pair, odd, afar, swap, *panels, far, cjac, cy, live)
         if turn == 0:
             steps = [jnp.broadcast_to(first_step[:, None], (1, 128))] * 3
         else:
             steps = [slab_sums] + [shifted(slab_sums, "slab", by) for by in (1, 2)]
-        grad, fown = kernel_call(
-            gradient_kernel,
-            (shape(SC, 128), shape(KF, 128)),
-            [smem, smem] + [vmem] * 7,
-            [
-                pltpu.VMEM((2 * KC + KF, 128), f32),
-                pltpu.VMEM((2 * KC + KF, 128), f32),
-                pltpu.VMEM((SC * 8, 128), f32),
-            ],
-        )(slot, pair, odd, swap, *panels, cjac, cy, live)
         body = functools.partial(update_kernel, turn == 0, betas[turn], turn == ITERS - 1)
         cnow, fnow, cy, fy, spread, fterms = kernel_call(
             body,

time: 204 us -> 209 us (1.025)
  waiting for transfers between devices: 35.2 us -> 38.9 us
    ppermute x11, waiting for transfers between devices: 13.6 us -> 17.3 us  [shifted(): lax.ppermute(x, axis, [(i, (i + by) % devices) for i in range(devices)])]
    unnamed x31 -> x37, local copies, waits for them, and re-layouts: 9.23 us -> 10 us
  transfers between devices with their start and end apart: 20 -> 20, of which waited for: 16 -> 16; matrix products, arithmetic and copies ran while one was open for 1% -> 1% of each run, Pallas kernels for 13% -> 12%
where the time goes in v5:
time: 209 us; the launch traced here: 208 us
  blocking collectives  90 us (43%)
  waiting for transfers between devices  38.9 us (19%)
  Pallas kernels  36.1 us (17%)
  starting transfers between devices  26.2 us (13%)
  local copies, waits for them, and re-layouts  11.3 us (5%)
  other arithmetic  3.46 us (2%)
  between operations  2.42 us (1%)
    all_to_all x5, blocking collectives, exchange(): lax.all_to_all(parts, 'grp', 0, 0, axis_index_groups=groups, tiled=True)  90 us
    ppermute x11, waiting for transfers between devices, shifted(): lax.ppermute(x, axis, [(i, (i + by) % devices) for i in range(devices)])  17.3 us
    all_to_all x2, starting transfers between devices, exchange(): lax.all_to_all(parts, 'grp', 0, 0, axis_index_groups=groups, tiled=True)  16 us
    pallas_call x1, Pallas kernels, on_device(): kernel_call(layout_kernel, (shape(SC * 128, 128), shape(SF * 128, 128), s...  12.9 us
    all_to_all x2, waiting for transfers between devices, exchange(): lax.all_to_all(parts, 'grp', 0, 0, axis_index_groups=groups, tiled=True)  10.9 us
    ppermute x7, waiting for transfers between devices, other_core(): return lax.ppermute(x, 'grp', [(i, i ^ 1) for i in range(devices)])  10.6 us
    unnamed x37, local copies, waits for them, and re-layouts  10 us
    ppermute x11, starting transfers between devices, shifted(): lax.ppermute(x, axis, [(i, (i + by) % devices) for i in range(devices)])  9.71 us
  transfers between devices with their start and end apart: 20, of which 16 were waited for; matrix products, arithmetic and copies ran while one was open for 1% of the time, Pallas kernels for 12%

profile of v5, /device:TPU:32, one launch (start us, length us, event | category | flops | bytes accessed | tf_op | source)
XLA Modules:
  0.0 208.3 jit_solution(11422753756143055208)
XLA Ops:
  2.3 2.8 %copy-done.2 = f32[64,3,64,128]{3,2,1,0:T(8,128)S(1)} copy-done((f32[64,3,64,128]{3,2,1,0:T(8,128)S(1)}, f32[64,3,64,128]{3,2,1,0:T(8,128)}, u32[]{:S(2)}) %copy-start.2) | copy-done | bytes 6291480
  7.2 2.3 %shard_map.157 = (f32[64,128]{1,0:T(8,128)S(1)}, f32[16,128]{1,0:T(8,128)S(1)}) custom-call(f32[12288,128]{1,0:T(8,128)S(1)} %bitcast.47, f32[3072,128]{1,0:T(8,128)S(1)} %bitcast.49, f32[64,192]{1,0:T(8,128)S(1)} %broadcast_multiply_fusion.cwarm, f32[16,192]{1,0:T(8,128)S(1)} %copy-done.7), custom_call_target="tpu_custom_call" | custom-call | tf_op jit(solution)/shard_map/pallas_call | solution.py:383
  12.7 1.8 collective-permute-done.arriving
  17.6 11.4 %all-to-all-start = ((f32[32,16,128]{2,1,0:T(8,128)}), f32[32,16,128]{2,1,0:T(8,128)S(1)}, u32[]{:S(2)}, u32[]{:S(2)}) async-start(f32[32,16,128]{2,1,0:T(8,128)} %bitcast.7.after), calls=%async_computation | async-start | bytes 524288 | tf_op jit(solution)/shard_map/all_to_all | solution.py:315
  29.0 12.9 %shard_map.160 = (f32[12288,128]{1,0:T(8,128)}, f32[3072,128]{1,0:T(8,128)}, f32[8,128]{1,0:T(8,128)}) custom-call(f32[64,192,128]{2,1,0:T(8,128)} %bitcast.46, f32[16,192,128]{2,1,0:T(8,128)} %bitcast.48, f32[32,16,128]{2,1,0:T(8,128)} %bitcast.7.after), custom_call_target="tpu_custom_call" | custom-call | bytes 41943040 | tf_op jit(solution)/shard_map/pallas_call | solution.py:400
  42.9 22.3 %all_to_all.35.own = f32[32,2,1152]{2,1,0:T(2,128)S(1)} all-to-all(f32[32,2,1152]{2,1,0:T(2,128)S(1)} %get-tuple-element.60), channel_id=1, replica_groups={{0,2,4,6,8,10,12,14,16,18,20,22,24,26,28,30,32,34,36,38,40,42,44,46,48,..., dimensions={0} | all-to-all | bytes 589824 | tf_op jit(solution)/shard_map/all_to_all | solution.py:315
  67.6 1.6 collective-permute-start.3
  70.8 2.8 %copy-done = f32[12288,128]{1,0:T(8,128)S(1)} copy-done((f32[12288,128]{1,0:T(8,128)S(1)}, f32[12288,128]{1,0:T(8,128)}, u32[]{:S(2)}) %copy-start) | copy-done | bytes 6291480
  73.6 2.3 %shard_map.163 = (f32[96,128]{1,0:T(8,128)S(1)}, f32[16,128]{1,0:T(8,128)S(1)}, f32[8,128]{1,0:T(8,128)}) custom-call(s32[160]{0:T(256)S(1)} %get-tuple-element.119.chips, s32[160]{0:T(256)S(1)} %get-tuple-element.116.pairs, f32[160,128]{1,0:T(8,128)S(1)} %broadcast_in_dim.12.odd, f32[160,128]{1,0:T(8,128)S(1)} %broadcast_in_dim.13.afar, ...), custom_call_target="tpu_custom_call" | custom-call | tf_op jit(solution)/shard_map/pallas_call | solution.py:433
  78.9 2.5 %collective-permute-done.4.arriving = f32[16,128]{1,0:T(8,128)S(1)} collective-permute-done((f32[16,128]{1,0:T(8,128)S(1)}, f32[16,128]{1,0:T(8,128)S(1)}, u32[]{:S(2)}, u32[]{:S(2)}) %collective-permute-start.4) | collective-permute-done | bytes 8224 | tf_op jit(solution)/shard_map/ppermute | solution.py:53
  84.0 17.0 %all_to_all.36.received = f32[32,16,128]{2,1,0:T(8,128)S(1)} all-to-all(f32[32,16,128]{2,1,0:T(8,128)S(1)} %bitcast.57), channel_id=1, replica_groups={{0,2,4,6,8,10,12,14,16,18,20,22,24,26,28,30,32,34,36,38,40,42,44,46,48,..., dimensions={0} | all-to-all | bytes 524288 | tf_op jit(solution)/shard_map/all_to_all | solution.py:315
  101.2 16.8 %all_to_all.37.own = f32[32,2,1152]{2,1,0:T(2,128)S(1)} all-to-all(f32[32,2,1152]{2,1,0:T(2,128)S(1)} %get-tuple-element.73), channel_id=1, replica_groups={{0,2,4,6,8,10,12,14,16,18,20,22,24,26,28,30,32,34,36,38,40,42,44,46,48,..., dimensions={0} | all-to-all | bytes 589824 | tf_op jit(solution)/shard_map/all_to_all | solution.py:315
  118.0 1.6 collective-permute-done.6.other
  120.6 1.8 shard_map.170
  124.3 3.3 %collective-permute-done.8.refs_2_ = f32[8,128]{1,0:T(8,128)S(1)} collective-permute-done((f32[8,128]{1,0:T(8,128)S(1)}, f32[8,128]{1,0:T(8,128)S(1)}, u32[]{:S(2)}, u32[]{:S(2)}) %collective-permute-start.8) | collective-permute-done | bytes 4128 | tf_op jit(solution)/shard_map/ppermute | solution.py:53
  131.9 2.1 %collective-permute-done.10.arriving = f32[16,128]{1,0:T(8,128)S(1)} collective-permute-done((f32[16,128]{1,0:T(8,128)S(1)}, f32[16,128]{1,0:T(8,128)S(1)}, u32[]{:S(2)}, u32[]{:S(2)}) %collective-permute-start.10) | collective-permute-done | bytes 8224 | tf_op jit(solution)/shard_map/ppermute | solution.py:53
  136.3 17.0 %all_to_all.38.received = f32[32,16,128]{2,1,0:T(8,128)S(1)} all-to-all(f32[32,16,128]{2,1,0:T(8,128)S(1)} %bitcast.58), channel_id=1, replica_groups={{0,2,4,6,8,10,12,14,16,18,20,22,24,26,28,30,32,34,36,38,40,42,44,46,48,..., dimensions={0} | all-to-all | bytes 524288 | tf_op jit(solution)/shard_map/all_to_all | solution.py:315
  154.0 16.8 %all_to_all.39.own = f32[32,2,1152]{2,1,0:T(2,128)S(1)} all-to-all(f32[32,2,1152]{2,1,0:T(2,128)S(1)} %get-tuple-element.88), channel_id=1, replica_groups={{0,2,4,6,8,10,12,14,16,18,20,22,24,26,28,30,32,34,36,38,40,42,44,46,48,..., dimensions={0} | all-to-all | bytes 589824 | tf_op jit(solution)/shard_map/all_to_all | solution.py:315
  170.8 1.6 collective-permute-done.12.other
  173.9 1.8 shard_map.177
  177.1 3.8 %collective-permute-done.14.refs_2_ = f32[8,128]{1,0:T(8,128)S(1)} collective-permute-done((f32[8,128]{1,0:T(8,128)S(1)}, f32[8,128]{1,0:T(8,128)S(1)}, u32[]{:S(2)}, u32[]{:S(2)}) %collective-permute-start.14) | collective-permute-done | bytes 4128 | tf_op jit(solution)/shard_map/ppermute | solution.py:53
  185.1 2.3 %collective-permute-done.16.arriving = f32[16,128]{1,0:T(8,128)S(1)} collective-permute-done((f32[16,128]{1,0:T(8,128)S(1)}, f32[16,128]{1,0:T(8,128)S(1)}, u32[]{:S(2)}, u32[]{:S(2)}) %collective-permute-start.16) | collective-permute-done | bytes 8224 | tf_op jit(solution)/shard_map/ppermute | solution.py:53
  190.5 4.6 %all-to-all-start.6 = ((f32[32,16,128]{2,1,0:T(8,128)}), f32[32,16,128]{2,1,0:T(8,128)S(1)}, u32[]{:S(2)}, u32[]{:S(2)}) async-start(f32[32,16,128]{2,1,0:T(8,128)} %bitcast.26), calls=%async_computation.6 | async-start | bytes 524288 | tf_op jit(solution)/shard_map/all_to_all | solution.py:315
  196.8 10.9 %all-to-all-done.6 = f32[32,16,128]{2,1,0:T(8,128)S(1)} async-done(((f32[32,16,128]{2,1,0:T(8,128)}), f32[32,16,128]{2,1,0:T(8,128)S(1)}, u32[]{:S(2)}, u32[]{:S(2)}) %all-to-all-start.6) | async-done | bytes 262176 | tf_op jit(solution)/shard_map/all_to_all | solution.py:315
  (118 shorter events, 41.7 us)
Async XLA Ops:
  9.5 55.6 %copy-start.11 = (s32[64,64]{1,0:T(8,128)S(1)}, s32[64,64]{1,0:T(8,128)}, u32[]{:S(2)}) copy-start(s32[64,64]{1,0:T(8,128)} %param.16) | copy-start | bytes 49156
  9.6 55.6 %copy-start.13 = (f32[8]{0:T(128)S(1)}, f32[8]{0:T(128)}, u32[]{:S(2)}) copy-start(f32[8]{0:T(128)} %param.26) | copy-start | bytes 100
  9.6 59.6 %copy-start.12 = (s32[16,64]{1,0:T(8,128)S(1)}, s32[16,64]{1,0:T(8,128)}, u32[]{:S(2)}) copy-start(s32[16,64]{1,0:T(8,128)} %param.21) | copy-start | bytes 12292
  9.6 59.8 %copy-start.8 = (f32[16,192]{1,0:T(8,128)S(1)}, f32[16,192]{1,0:T(8,128)}, u32[]{:S(2)}) copy-start(f32[16,192]{1,0:T(8,128)} %fwarm.1) | copy-start | bytes 36868
  9.6 4.9 %collective-permute-start = (f32[16,128]{1,0:T(8,128)S(1)}, f32[16,128]{1,0:T(8,128)S(1)}, u32[]{:S(2)}, u32[]{:S(2)}) collective-permute-start(f32[16,128]{1,0:T(8,128)S(1)} %get-tuple-element.53.fterms), channel_id=1, source_target_pairs={{0,64},{64,128},{128,192},{192,0},{1,65},{65,129},{129,193},{193,1... | collective-permute-start | bytes 24584 | tf_op jit(solution)/shard_map/ppermute | solution.py:53
  15.2 1.6 collective-permute-start.1
  17.6 24.3 %all-to-all-start = ((f32[32,16,128]{2,1,0:T(8,128)}), f32[32,16,128]{2,1,0:T(8,128)S(1)}, u32[]{:S(2)}, u32[]{:S(2)}) async-start(f32[32,16,128]{2,1,0:T(8,128)} %bitcast.7.after), calls=%async_computation | async-start | bytes 524288 | tf_op jit(solution)/shard_map/all_to_all | solution.py:315
  65.1 1.6 collective-permute-start.2
  67.6 8.4 %collective-permute-start.3 = (f32[24,128]{1,0:T(8,128)S(1)}, f32[24,128]{1,0:T(8,128)S(1)}, u32[]{:S(2)}, u32[]{:S(2)}) collective-permute-start(f32[24,128]{1,0:T(8,128)S(1)} %shard_map.162.sums), channel_id=1, source_target_pairs={{0,192},{64,0},{128,64},{192,128},{1,193},{65,1},{129,65},{193,129... | collective-permute-start | bytes 36872 | tf_op jit(solution)/shard_map/ppermute | solution.py:53
  76.5 4.9 %collective-permute-start.4 = (f32[16,128]{1,0:T(8,128)S(1)}, f32[16,128]{1,0:T(8,128)S(1)}, u32[]{:S(2)}, u32[]{:S(2)}) collective-permute-start(f32[16,128]{1,0:T(8,128)S(1)} %get-tuple-element.65.fterms), channel_id=1, source_target_pairs={{0,64},{64,128},{128,192},{192,0},{1,65},{65,129},{129,193},{193,1... | collective-permute-start | bytes 24584 | tf_op jit(solution)/shard_map/ppermute | solution.py:53
  82.1 1.8 collective-permute-start.5
  118.0 1.6 collective-permute-start.6
  120.3 8.2 %collective-permute-start.9 = (f32[24,128]{1,0:T(8,128)S(1)}, f32[24,128]{1,0:T(8,128)S(1)}, u32[]{:S(2)}, u32[]{:S(2)}) collective-permute-start(f32[24,128]{1,0:T(8,128)S(1)} %shard_map.169.sums), channel_id=1, source_target_pairs={{0,192},{64,0},{128,64},{192,128},{1,193},{65,1},{129,65},{193,129... | collective-permute-start | bytes 36872 | tf_op jit(solution)/shard_map/ppermute | solution.py:53
  122.4 5.2 %collective-permute-start.8 = (f32[8,128]{1,0:T(8,128)S(1)}, f32[8,128]{1,0:T(8,128)S(1)}, u32[]{:S(2)}, u32[]{:S(2)}) collective-permute-start(f32[8,128]{1,0:T(8,128)S(1)} %get-tuple-element.74.refs_0_), channel_id=1, source_target_pairs={{0,128},{64,192},{128,0},{192,64},{1,129},{65,193},{129,1},{193,65... | collective-permute-start | bytes 12296 | tf_op jit(solution)/shard_map/ppermute | solution.py:53
  123.5 5.0 %collective-permute-start.7 = (f32[8,128]{1,0:T(8,128)S(1)}, f32[8,128]{1,0:T(8,128)S(1)}, u32[]{:S(2)}, u32[]{:S(2)}) collective-permute-start(f32[8,128]{1,0:T(8,128)S(1)} %get-tuple-element.74.refs_0_), channel_id=1, source_target_pairs={{0,64},{64,128},{128,192},{192,0},{1,65},{65,129},{129,193},{193,1... | collective-permute-start | bytes 12296 | tf_op jit(solution)/shard_map/ppermute | solution.py:53
  129.0 4.9 %collective-permute-start.10 = (f32[16,128]{1,0:T(8,128)S(1)}, f32[16,128]{1,0:T(8,128)S(1)}, u32[]{:S(2)}, u32[]{:S(2)}) collective-permute-start(f32[16,128]{1,0:T(8,128)S(1)} %get-tuple-element.80.fterms), channel_id=1, source_target_pairs={{0,64},{64,128},{128,192},{192,0},{1,65},{65,129},{129,193},{193,1... | collective-permute-start | bytes 24584 | tf_op jit(solution)/shard_map/ppermute | solution.py:53
  134.7 1.6 collective-permute-start.11
  170.8 1.6 collective-permute-start.12
  173.0 8.5 %collective-permute-start.15 = (f32[24,128]{1,0:T(8,128)S(1)}, f32[24,128]{1,0:T(8,128)S(1)}, u32[]{:S(2)}, u32[]{:S(2)}) collective-permute-start(f32[24,128]{1,0:T(8,128)S(1)} %shard_map.176.sums), channel_id=1, source_target_pairs={{0,192},{64,0},{128,64},{192,128},{1,193},{65,1},{129,65},{193,129... | collective-permute-start | bytes 36872 | tf_op jit(solution)/shard_map/ppermute | solution.py:53
  175.7 5.2 %collective-permute-start.14 = (f32[8,128]{1,0:T(8,128)S(1)}, f32[8,128]{1,0:T(8,128)S(1)}, u32[]{:S(2)}, u32[]{:S(2)}) collective-permute-start(f32[8,128]{1,0:T(8,128)S(1)} %get-tuple-element.89.refs_0_), channel_id=1, source_target_pairs={{0,128},{64,192},{128,0},{192,64},{1,129},{65,193},{129,1},{193,65... | collective-permute-start | bytes 12296 | tf_op jit(solution)/shard_map/ppermute | solution.py:53
  176.7 4.8 %collective-permute-start.13 = (f32[8,128]{1,0:T(8,128)S(1)}, f32[8,128]{1,0:T(8,128)S(1)}, u32[]{:S(2)}, u32[]{:S(2)}) collective-permute-start(f32[8,128]{1,0:T(8,128)S(1)} %get-tuple-element.89.refs_0_), channel_id=1, source_target_pairs={{0,64},{64,128},{128,192},{192,0},{1,65},{65,129},{129,193},{193,1... | collective-permute-start | bytes 12296 | tf_op jit(solution)/shard_map/ppermute | solution.py:53
  182.6 4.9 %collective-permute-start.16 = (f32[16,128]{1,0:T(8,128)S(1)}, f32[16,128]{1,0:T(8,128)S(1)}, u32[]{:S(2)}, u32[]{:S(2)}) collective-permute-start(f32[16,128]{1,0:T(8,128)S(1)} %get-tuple-element.97.fterms), channel_id=1, source_target_pairs={{0,64},{64,128},{128,192},{192,0},{1,65},{65,129},{129,193},{193,1... | collective-permute-start | bytes 24584 | tf_op jit(solution)/shard_map/ppermute | solution.py:53
  188.1 1.6 collective-permute-start.17
  190.5 17.2 %all-to-all-start.6 = ((f32[32,16,128]{2,1,0:T(8,128)}), f32[32,16,128]{2,1,0:T(8,128)S(1)}, u32[]{:S(2)}, u32[]{:S(2)}) async-start(f32[32,16,128]{2,1,0:T(8,128)} %bitcast.26), calls=%async_computation.6 | async-start | bytes 524288 | tf_op jit(solution)/shard_map/all_to_all | solution.py:315
  (13 other events, 167.4 us)

commit v6 on v5

--- a/solution.py
+++ b/solution.py
@@ -20,6 +20,7 @@
 GC, GF = 128 // KC, 128 // KF
 IC, IF = BLK // GC, BLK // GF
 SC, SF = COMP * IC, COMP * IF
+PITCH = COMP * BLK + 8
 
 regular_weight = 0.05
 tiny_sum = 1e-06
@@ -137,8 +138,8 @@
 def layout_kernel(
     cjac, fjac, after, cout, fout, done, cbuf, fbuf, cturn, fturn, sems, outs
 ):
-    width = COMP * BLK
-    copies = [pltpu.make_async_copy(fjac, fbuf, sems.at[COMP])]
+    whole = pl.ds(0, COMP * BLK)
+    copies = [pltpu.make_async_copy(fjac, fbuf.at[:, whole], sems.at[COMP])]
     for c in range(COMP):
         rows = pl.ds(c * BLK, BLK)
         copies.append(pltpu.make_async_copy(cjac.at[:, rows], cbuf.at[:, rows], sems.at[c]))
@@ -147,11 +148,11 @@
 
     def turn(jac, out, parts, depth, first, count):
         k = 128 // parts
-        flat = jac.reshape(k * width, 128)
+        flat = jac.reshape(k * PITCH, 128)
 
         def one(s, _):
             row = s // depth * BLK + s % depth
-            rows = [flat[pl.ds(row + p * depth, k, stride=width), :] for p in range(parts)]
+            rows = [flat[pl.ds(row + p * depth, k, stride=PITCH), :] for p in range(parts)]
             out[rows_of(s), :] = jnp.concatenate(rows, 0).T
             return _
 
@@ -234,17 +235,19 @@
     return jnp.where(other, rows[1], rows[0])
 
 
-def far_kernel(chips, pairs, odd, afar, swap, own, other, far, *scratch):
+def far_kernel(chips, pairs, odd, afar, swap, own, other, far, sums, *scratch):
     base = 2 * KC + KF
     x = pick(chips, pairs, odd, afar, (own, other), scratch, base, KF)
     far[0:KF, :] = jnp.where(swap[base:, :] > 0, pltpu.roll(x, BLK, 1), x)
     at = OWN // 2 * 128
     total = sum(panel[chip, :, at : at + 128] for panel in (own, other) for chip in range(CHIPS))
-    far[KF:, :] = jnp.concatenate([total, jnp.zeros((6, 128), f32)], 0)
+    total = jnp.concatenate([total, jnp.zeros((6, 128), f32)], 0)
+    sums[...] = total
+    far[KF:, :] = total
 
 
 def gradient_kernel(
-    chips, pairs, odd, afar, swap, own, other, sums, jac, y, live, grad, fown, sums_out, *scratch
+    chips, pairs, odd, afar, swap, own, other, jac, y, live, grad, fown, *scratch
 ):
     count = 2 * KC + KF
     x = pick(chips, pairs, odd, afar, (own, other), scratch[:2], 0, count)
@@ -254,7 +257,6 @@
     velocity = jnp.concatenate([joined] * GC, 0).T
     raw = product(jac, velocity, scratch[2], SC)
     grad[...] = (raw + regular_weight * y[...]) * live[...]
-    sums_out[...] = sums[KF:, :]
 
 
 def cone(pushed, friction):
@@ -402,14 +404,14 @@
                 (shape(SC * 128, 128), shape(SF * 128, 128), shape(8, 128)),
                 [hbm, hbm, vmem],
                 [
-                    pltpu.VMEM((KC, COMP * BLK, 128), f32),
-                    pltpu.VMEM((KF, COMP * BLK, 128), f32),
+                    pltpu.VMEM((KC, PITCH, 128), f32),
+                    pltpu.VMEM((KF, PITCH, 128), f32),
                     cturn,
                     fturn,
                     pltpu.SemaphoreType.DMA((COMP + 1,)),
                     pltpu.SemaphoreType.DMA((COMP + 1,)),
                 ],
-                54,
+                52,
                 (hbm, hbm, vmem),
                 pl.CostEstimate(flops=0, bytes_accessed=40 << 20, transcendentals=0),
             )(
@@ -420,26 +422,26 @@
         owned, pieces = kernel_call(
             owner_kernel,
             (shape(OWN, 128), shape(CHIPS, 2, (OWN // 2 + 1) * 128)),
-            [vmem] * 6,
+            [vmem] * 5 + [hbm],
         )(received, free_own, mass_own, owned, spread, done)
         panels = all_gather(pieces)
-        far = kernel_call(
+        far, slab_sums = kernel_call(
             far_kernel,
-            shape(KF + 8, 128),
+            (shape(KF + 8, 128), shape(8, 128)),
             [smem, smem] + [vmem] * 5,
             [pltpu.VMEM((2 * KF, 128), f32)] * 2,
         )(chip, pair, odd, afar, swap, *panels)
         returning = shifted(far, "slab", -1)
-        grad, fown, slab_sums = kernel_call(
-            gradient_kernel,
-            (shape(SC, 128), shape(KF, 128), shape(8, 128)),
-            [smem, smem] + [vmem] * 9,
-            [pltpu.VMEM((2 * (2 * KC + KF), 128), f32)] * 2 + [pltpu.VMEM((SC * 8, 128), f32)],
-        )(chip, pair, odd, afar, swap, *panels, far, cjac, cy, live)
         if turn == 0:
             steps = [jnp.broadcast_to(first_step[:, None], (1, 128))] * 3
         else:
             steps = [slab_sums] + [shifted(slab_sums, "slab", by) for by in (1, 2)]
+        grad, fown = kernel_call(
+            gradient_kernel,
+            (shape(SC, 128), shape(KF, 128)),
+            [smem, smem] + [vmem] * 8,
+            [pltpu.VMEM((2 * (2 * KC + KF), 128), f32)] * 2 + [pltpu.VMEM((SC * 8, 128), f32)],
+        )(chip, pair, odd, afar, swap, *panels, cjac, cy, live)
         body = functools.partial(update_kernel, turn == 0, betas[turn], turn == ITERS - 1)
         cnow, fnow, cy, fy, spread, fterms = kernel_call(
             body,

time: 209 us -> 199 us (0.952)
  Pallas kernels: 36.1 us -> 30.4 us
  blocking collectives: 90 us -> 84.6 us
    pallas_call x1, Pallas kernels: 12.9 us -> 7.19 us  [on_device(): kernel_call(layout_kernel, (shape(SC * 128, 128), shape(SF * 128, 128), s...]
    all_to_all x2, waiting for transfers between devices: 10.9 us -> 16.3 us  [exchange(): lax.all_to_all(parts, 'grp', 0, 0, axis_index_groups=groups, tiled=True)]
    all_to_all x5, blocking collectives: 90 us -> 84.6 us  [exchange(): lax.all_to_all(parts, 'grp', 0, 0, axis_index_groups=groups, tiled=True)]
    ppermute x11, waiting for transfers between devices: 17.3 us -> 13.9 us  [shifted(): lax.ppermute(x, axis, [(i, (i + by) % devices) for i in range(devices)])]
    unnamed x37 -> x31, local copies, waits for them, and re-layouts: 10 us -> 9.23 us
  transfers between devices with their start and end apart: 20 -> 20, of which waited for: 16 -> 17; matrix products, arithmetic and copies ran while one was open for 1% -> 1% of each run, Pallas kernels for 12% -> 10%
where the time goes in v6:
time: 199 us; the launch traced here: 198 us
  blocking collectives  84.6 us (43%)
  waiting for transfers between devices  40.9 us (21%)
  Pallas kernels  30.4 us (15%)
  starting transfers between devices  25.7 us (13%)
  local copies, waits for them, and re-layouts  10.5 us (5%)
  other arithmetic  3.46 us (2%)
  between operations  2.38 us (1%)
    all_to_all x5, blocking collectives, exchange(): lax.all_to_all(parts, 'grp', 0, 0, axis_index_groups=groups, tiled=True)  84.6 us
    all_to_all x2, waiting for transfers between devices, exchange(): lax.all_to_all(parts, 'grp', 0, 0, axis_index_groups=groups, tiled=True)  16.3 us
    all_to_all x2, starting transfers between devices, exchange(): lax.all_to_all(parts, 'grp', 0, 0, axis_index_groups=groups, tiled=True)  16 us
    ppermute x11, waiting for transfers between devices, shifted(): lax.ppermute(x, axis, [(i, (i + by) % devices) for i in range(devices)])  13.9 us
    ppermute x7, waiting for transfers between devices, other_core(): return lax.ppermute(x, 'grp', [(i, i ^ 1) for i in range(devices)])  10.6 us
    ppermute x11, starting transfers between devices, shifted(): lax.ppermute(x, axis, [(i, (i + by) % devices) for i in range(devices)])  9.34 us
    unnamed x31, local copies, waits for them, and re-layouts  9.23 us
    pallas_call x1, Pallas kernels, on_device(): kernel_call(layout_kernel, (shape(SC * 128, 128), shape(SF * 128, 128), s...  7.19 us
  transfers between devices with their start and end apart: 20, of which 17 were waited for; matrix products, arithmetic and copies ran while one was open for 1% of the time, Pallas kernels for 10%

profile of v6, /device:TPU:32, one launch (start us, length us, event | category | flops | bytes accessed | tf_op | source)
XLA Modules:
  0.0 197.9 jit_solution(15869379229114288238)
XLA Ops:
  2.3 2.8 %copy-done.2 = f32[64,3,64,128]{3,2,1,0:T(8,128)S(1)} copy-done((f32[64,3,64,128]{3,2,1,0:T(8,128)S(1)}, f32[64,3,64,128]{3,2,1,0:T(8,128)}, u32[]{:S(2)}) %copy-start.2) | copy-done | bytes 6291480
  7.2 2.3 %shard_map.157 = (f32[64,128]{1,0:T(8,128)S(1)}, f32[16,128]{1,0:T(8,128)S(1)}) custom-call(f32[12288,128]{1,0:T(8,128)S(1)} %bitcast.47, f32[3072,128]{1,0:T(8,128)S(1)} %bitcast.49, f32[64,192]{1,0:T(8,128)S(1)} %broadcast_multiply_fusion.cwarm, f32[16,192]{1,0:T(8,128)S(1)} %copy-done.6), custom_call_target="tpu_custom_call" | custom-call | tf_op jit(solution)/shard_map/pallas_call | solution.py:385
  12.7 1.8 collective-permute-done.arriving
  17.6 11.4 %all-to-all-start = ((f32[32,16,128]{2,1,0:T(8,128)}), f32[32,16,128]{2,1,0:T(8,128)S(1)}, u32[]{:S(2)}, u32[]{:S(2)}) async-start(f32[32,16,128]{2,1,0:T(8,128)} %bitcast.7.after), calls=%async_computation | async-start | bytes 524288 | tf_op jit(solution)/shard_map/all_to_all | solution.py:317
  29.0 7.2 %shard_map.160 = (f32[12288,128]{1,0:T(8,128)}, f32[3072,128]{1,0:T(8,128)S(1)}, f32[8,128]{1,0:T(8,128)S(1)}) custom-call(f32[64,192,128]{2,1,0:T(8,128)} %bitcast.46, f32[16,192,128]{2,1,0:T(8,128)} %bitcast.48, f32[32,16,128]{2,1,0:T(8,128)} %bitcast.7.after), custom_call_target="tpu_custom_call" | custom-call | bytes 41943040 | tf_op jit(solution)/shard_map/pallas_call | solution.py:402
  36.1 5.4 %all-to-all-done.received = f32[32,16,128]{2,1,0:T(8,128)S(1)} async-done(((f32[32,16,128]{2,1,0:T(8,128)}), f32[32,16,128]{2,1,0:T(8,128)S(1)}, u32[]{:S(2)}, u32[]{:S(2)}) %all-to-all-start) | async-done | bytes 262176 | tf_op jit(solution)/shard_map/all_to_all | solution.py:317
  41.7 16.9 %all_to_all.35.own = f32[32,2,1152]{2,1,0:T(2,128)S(1)} all-to-all(f32[32,2,1152]{2,1,0:T(2,128)S(1)} %get-tuple-element.63), channel_id=1, replica_groups={{0,2,4,6,8,10,12,14,16,18,20,22,24,26,28,30,32,34,36,38,40,42,44,46,48,..., dimensions={0} | all-to-all | bytes 589824 | tf_op jit(solution)/shard_map/all_to_all | solution.py:317
  64.8 2.8 %copy-done = f32[12288,128]{1,0:T(8,128)S(1)} copy-done((f32[12288,128]{1,0:T(8,128)S(1)}, f32[12288,128]{1,0:T(8,128)}, u32[]{:S(2)}) %copy-start) | copy-done | bytes 6291480
  67.6 1.8 shard_map.162
  72.4 2.5 %collective-permute-done.4.arriving = f32[16,128]{1,0:T(8,128)S(1)} collective-permute-done((f32[16,128]{1,0:T(8,128)S(1)}, f32[16,128]{1,0:T(8,128)S(1)}, u32[]{:S(2)}, u32[]{:S(2)}) %collective-permute-start.4) | collective-permute-done | bytes 8224 | tf_op jit(solution)/shard_map/ppermute | solution.py:54
  77.3 17.0 %all_to_all.36.received = f32[32,16,128]{2,1,0:T(8,128)S(1)} all-to-all(f32[32,16,128]{2,1,0:T(8,128)S(1)} %bitcast.57), channel_id=1, replica_groups={{0,2,4,6,8,10,12,14,16,18,20,22,24,26,28,30,32,34,36,38,40,42,44,46,48,..., dimensions={0} | all-to-all | bytes 524288 | tf_op jit(solution)/shard_map/all_to_all | solution.py:317
  94.5 16.8 %all_to_all.37.own = f32[32,2,1152]{2,1,0:T(2,128)S(1)} all-to-all(f32[32,2,1152]{2,1,0:T(2,128)S(1)} %get-tuple-element.77), channel_id=1, replica_groups={{0,2,4,6,8,10,12,14,16,18,20,22,24,26,28,30,32,34,36,38,40,42,44,46,48,..., dimensions={0} | all-to-all | bytes 589824 | tf_op jit(solution)/shard_map/all_to_all | solution.py:317
  111.3 1.6 collective-permute-done.6.other
  115.6 1.8 shard_map.170
  117.4 1.6 collective-permute-done.8.refs_2_
  123.3 2.1 %collective-permute-done.10.arriving = f32[16,128]{1,0:T(8,128)S(1)} collective-permute-done((f32[16,128]{1,0:T(8,128)S(1)}, f32[16,128]{1,0:T(8,128)S(1)}, u32[]{:S(2)}, u32[]{:S(2)}) %collective-permute-start.10) | collective-permute-done | bytes 8224 | tf_op jit(solution)/shard_map/ppermute | solution.py:54
  127.7 17.0 %all_to_all.38.received = f32[32,16,128]{2,1,0:T(8,128)S(1)} all-to-all(f32[32,16,128]{2,1,0:T(8,128)S(1)} %bitcast.58), channel_id=1, replica_groups={{0,2,4,6,8,10,12,14,16,18,20,22,24,26,28,30,32,34,36,38,40,42,44,46,48,..., dimensions={0} | all-to-all | bytes 524288 | tf_op jit(solution)/shard_map/all_to_all | solution.py:317
  145.4 16.8 %all_to_all.39.own = f32[32,2,1152]{2,1,0:T(2,128)S(1)} all-to-all(f32[32,2,1152]{2,1,0:T(2,128)S(1)} %get-tuple-element.93), channel_id=1, replica_groups={{0,2,4,6,8,10,12,14,16,18,20,22,24,26,28,30,32,34,36,38,40,42,44,46,48,..., dimensions={0} | all-to-all | bytes 589824 | tf_op jit(solution)/shard_map/all_to_all | solution.py:317
  162.2 1.6 collective-permute-done.12.other
  166.5 1.8 shard_map.177
  168.3 2.1 %collective-permute-done.14.refs_2_ = f32[8,128]{1,0:T(8,128)S(1)} collective-permute-done((f32[8,128]{1,0:T(8,128)S(1)}, f32[8,128]{1,0:T(8,128)S(1)}, u32[]{:S(2)}, u32[]{:S(2)}) %collective-permute-start.14) | collective-permute-done | bytes 4128 | tf_op jit(solution)/shard_map/ppermute | solution.py:54
  174.6 2.3 %collective-permute-done.16.arriving = f32[16,128]{1,0:T(8,128)S(1)} collective-permute-done((f32[16,128]{1,0:T(8,128)S(1)}, f32[16,128]{1,0:T(8,128)S(1)}, u32[]{:S(2)}, u32[]{:S(2)}) %collective-permute-start.16) | collective-permute-done | bytes 8224 | tf_op jit(solution)/shard_map/ppermute | solution.py:54
  180.0 4.6 %all-to-all-start.6 = ((f32[32,16,128]{2,1,0:T(8,128)}), f32[32,16,128]{2,1,0:T(8,128)S(1)}, u32[]{:S(2)}, u32[]{:S(2)}) async-start(f32[32,16,128]{2,1,0:T(8,128)} %bitcast.26), calls=%async_computation.6 | async-start | bytes 524288 | tf_op jit(solution)/shard_map/all_to_all | solution.py:317
  186.3 10.9 %all-to-all-done.6 = f32[32,16,128]{2,1,0:T(8,128)S(1)} async-done(((f32[32,16,128]{2,1,0:T(8,128)}), f32[32,16,128]{2,1,0:T(8,128)S(1)}, u32[]{:S(2)}, u32[]{:S(2)}) %all-to-all-start.6) | async-done | bytes 262176 | tf_op jit(solution)/shard_map/all_to_all | solution.py:317
  (112 shorter events, 42.5 us)
Async XLA Ops:
  9.5 49.1 %copy-start.8 = (s32[64,64]{1,0:T(8,128)S(1)}, s32[64,64]{1,0:T(8,128)}, u32[]{:S(2)}) copy-start(s32[64,64]{1,0:T(8,128)} %param.16) | copy-start | bytes 49156
  9.6 49.1 %copy-start.10 = (f32[8]{0:T(128)S(1)}, f32[8]{0:T(128)}, u32[]{:S(2)}) copy-start(f32[8]{0:T(128)} %param.26) | copy-start | bytes 100
  9.6 53.6 %copy-start.9 = (s32[16,64]{1,0:T(8,128)S(1)}, s32[16,64]{1,0:T(8,128)}, u32[]{:S(2)}) copy-start(s32[16,64]{1,0:T(8,128)} %param.21) | copy-start | bytes 12292
  9.6 53.8 %copy-start.7 = (f32[16,192]{1,0:T(8,128)S(1)}, f32[16,192]{1,0:T(8,128)}, u32[]{:S(2)}) copy-start(f32[16,192]{1,0:T(8,128)} %fwarm.1) | copy-start | bytes 36868
  9.6 4.9 %collective-permute-start = (f32[16,128]{1,0:T(8,128)S(1)}, f32[16,128]{1,0:T(8,128)S(1)}, u32[]{:S(2)}, u32[]{:S(2)}) collective-permute-start(f32[16,128]{1,0:T(8,128)S(1)} %get-tuple-element.56.fterms), channel_id=1, source_target_pairs={{0,64},{64,128},{128,192},{192,0},{1,65},{65,129},{129,193},{193,1... | collective-permute-start | bytes 24584 | tf_op jit(solution)/shard_map/ppermute | solution.py:54
  15.2 1.6 collective-permute-start.1
  17.6 24.0 %all-to-all-start = ((f32[32,16,128]{2,1,0:T(8,128)}), f32[32,16,128]{2,1,0:T(8,128)S(1)}, u32[]{:S(2)}, u32[]{:S(2)}) async-start(f32[32,16,128]{2,1,0:T(8,128)} %bitcast.7.after), calls=%async_computation | async-start | bytes 524288 | tf_op jit(solution)/shard_map/all_to_all | solution.py:317
  58.6 1.6 collective-permute-start.2
  61.6 7.8 %collective-permute-start.3 = (f32[24,128]{1,0:T(8,128)S(1)}, f32[24,128]{1,0:T(8,128)S(1)}, u32[]{:S(2)}, u32[]{:S(2)}) collective-permute-start(f32[24,128]{1,0:T(8,128)S(1)} %get-tuple-element.67), channel_id=1, source_target_pairs={{0,192},{64,0},{128,64},{192,128},{1,193},{65,1},{129,65},{193,129... | collective-permute-start | bytes 36872 | tf_op jit(solution)/shard_map/ppermute | solution.py:54
  70.0 4.9 %collective-permute-start.4 = (f32[16,128]{1,0:T(8,128)S(1)}, f32[16,128]{1,0:T(8,128)S(1)}, u32[]{:S(2)}, u32[]{:S(2)}) collective-permute-start(f32[16,128]{1,0:T(8,128)S(1)} %get-tuple-element.69.fterms), channel_id=1, source_target_pairs={{0,64},{64,128},{128,192},{192,0},{1,65},{65,129},{129,193},{193,1... | collective-permute-start | bytes 24584 | tf_op jit(solution)/shard_map/ppermute | solution.py:54
  75.6 1.6 collective-permute-start.5
  111.3 1.6 collective-permute-start.6
  113.6 6.3 %collective-permute-start.9 = (f32[24,128]{1,0:T(8,128)S(1)}, f32[24,128]{1,0:T(8,128)S(1)}, u32[]{:S(2)}, u32[]{:S(2)}) collective-permute-start(f32[24,128]{1,0:T(8,128)S(1)} %get-tuple-element.81), channel_id=1, source_target_pairs={{0,192},{64,0},{128,64},{192,128},{1,193},{65,1},{129,65},{193,129... | collective-permute-start | bytes 36872 | tf_op jit(solution)/shard_map/ppermute | solution.py:54
  113.9 5.1 %collective-permute-start.8 = (f32[8,128]{1,0:T(8,128)S(1)}, f32[8,128]{1,0:T(8,128)S(1)}, u32[]{:S(2)}, u32[]{:S(2)}) collective-permute-start(f32[8,128]{1,0:T(8,128)S(1)} %get-tuple-element.78.refs_0_), channel_id=1, source_target_pairs={{0,128},{64,192},{128,0},{192,64},{1,129},{65,193},{129,1},{193,65... | collective-permute-start | bytes 12296 | tf_op jit(solution)/shard_map/ppermute | solution.py:54
  114.9 5.0 %collective-permute-start.7 = (f32[8,128]{1,0:T(8,128)S(1)}, f32[8,128]{1,0:T(8,128)S(1)}, u32[]{:S(2)}, u32[]{:S(2)}) collective-permute-start(f32[8,128]{1,0:T(8,128)S(1)} %get-tuple-element.78.refs_0_), channel_id=1, source_target_pairs={{0,64},{64,128},{128,192},{192,0},{1,65},{65,129},{129,193},{193,1... | collective-permute-start | bytes 12296 | tf_op jit(solution)/shard_map/ppermute | solution.py:54
  120.4 4.9 %collective-permute-start.10 = (f32[16,128]{1,0:T(8,128)S(1)}, f32[16,128]{1,0:T(8,128)S(1)}, u32[]{:S(2)}, u32[]{:S(2)}) collective-permute-start(f32[16,128]{1,0:T(8,128)S(1)} %get-tuple-element.85.fterms), channel_id=1, source_target_pairs={{0,64},{64,128},{128,192},{192,0},{1,65},{65,129},{129,193},{193,1... | collective-permute-start | bytes 24584 | tf_op jit(solution)/shard_map/ppermute | solution.py:54
  126.1 1.6 collective-permute-start.11
  162.2 1.6 collective-permute-start.12
  164.5 6.6 %collective-permute-start.15 = (f32[24,128]{1,0:T(8,128)S(1)}, f32[24,128]{1,0:T(8,128)S(1)}, u32[]{:S(2)}, u32[]{:S(2)}) collective-permute-start(f32[24,128]{1,0:T(8,128)S(1)} %get-tuple-element.97), channel_id=1, source_target_pairs={{0,192},{64,0},{128,64},{192,128},{1,193},{65,1},{129,65},{193,129... | collective-permute-start | bytes 36872 | tf_op jit(solution)/shard_map/ppermute | solution.py:54
  165.3 5.1 %collective-permute-start.14 = (f32[8,128]{1,0:T(8,128)S(1)}, f32[8,128]{1,0:T(8,128)S(1)}, u32[]{:S(2)}, u32[]{:S(2)}) collective-permute-start(f32[8,128]{1,0:T(8,128)S(1)} %get-tuple-element.94.refs_0_), channel_id=1, source_target_pairs={{0,128},{64,192},{128,0},{192,64},{1,129},{65,193},{129,1},{193,65... | collective-permute-start | bytes 12296 | tf_op jit(solution)/shard_map/ppermute | solution.py:54
  166.2 4.8 %collective-permute-start.13 = (f32[8,128]{1,0:T(8,128)S(1)}, f32[8,128]{1,0:T(8,128)S(1)}, u32[]{:S(2)}, u32[]{:S(2)}) collective-permute-start(f32[8,128]{1,0:T(8,128)S(1)} %get-tuple-element.94.refs_0_), channel_id=1, source_target_pairs={{0,64},{64,128},{128,192},{192,0},{1,65},{65,129},{129,193},{193,1... | collective-permute-start | bytes 12296 | tf_op jit(solution)/shard_map/ppermute | solution.py:54
  172.1 4.9 %collective-permute-start.16 = (f32[16,128]{1,0:T(8,128)S(1)}, f32[16,128]{1,0:T(8,128)S(1)}, u32[]{:S(2)}, u32[]{:S(2)}) collective-permute-start(f32[16,128]{1,0:T(8,128)S(1)} %get-tuple-element.103.fterms), channel_id=1, source_target_pairs={{0,64},{64,128},{128,192},{192,0},{1,65},{65,129},{129,193},{193,1... | collective-permute-start | bytes 24584 | tf_op jit(solution)/shard_map/ppermute | solution.py:54
  177.6 1.6 collective-permute-start.17
  180.0 17.2 %all-to-all-start.6 = ((f32[32,16,128]{2,1,0:T(8,128)}), f32[32,16,128]{2,1,0:T(8,128)S(1)}, u32[]{:S(2)}, u32[]{:S(2)}) async-start(f32[32,16,128]{2,1,0:T(8,128)} %bitcast.26), calls=%async_computation.6 | async-start | bytes 524288 | tf_op jit(solution)/shard_map/all_to_all | solution.py:317
  (10 other events, 106.2 us)

commit v7 on v6

--- a/solution.py
+++ b/solution.py
@@ -119,20 +119,16 @@
     return sum(partial[pl.ds(q, slices, stride=8), :] for q in range(8))
 
 
-def first_force_kernel(cjac, fjac, cwarm, fwarm, cterms, fterms, partial):
-    width = COMP * BLK
-    rows = jnp.concatenate([cwarm[...], fwarm[...], jnp.zeros((128 - KC - KF, width), f32)], 0)
+def first_force_kernel(jac, warm, terms, partial):
+    blocks, width = warm.shape
+    rows = jnp.concatenate([warm[...], jnp.zeros((128 - blocks, width), f32)], 0)
     rows = jnp.concatenate([rows, jnp.zeros((128, 256 - width), f32)], 1)
     turned = jnp.concatenate([rows[:, :128].T, rows[:, 128:].T], 0)[:width]
-    for jac, blocks, base in ((fjac, KF, KC), (cjac, KC, 0)):
-        for m in range(blocks):
-            y = jnp.broadcast_to(turned[:, base + m : base + m + 1], (width, 128))
-            products = jac[m * width : (m + 1) * width, :] * y
-            partial[(base + m) * 8 : (base + m + 1) * 8, :] = jnp.sum(
-                products.reshape(width // 8, 8, 128), 0
-            )
-    cterms[...] = sum(partial[pl.ds(q, KC, stride=8), :] for q in range(8))
-    fterms[...] = sum(partial[pl.ds(KC * 8 + q, KF, stride=8), :] for q in range(8))
+    for m in range(blocks):
+        y = jnp.broadcast_to(turned[:, m : m + 1], (width, 128))
+        products = jac[m * width : (m + 1) * width, :] * y
+        partial[m * 8 : (m + 1) * 8, :] = jnp.sum(products.reshape(width // 8, 8, 128), 0)
+    terms[...] = sum(partial[pl.ds(q, blocks, stride=8), :] for q in range(8))
 
 
 def layout_kernel(
@@ -382,14 +378,19 @@
     cwarm = warm_contact * live[0, :KC, None]
     crows, frows = contact_jac.reshape(-1, 128), face_jac.reshape(-1, 128)
     cturn, fturn = pltpu.VMEM((SC * 128, 128), f32), pltpu.VMEM((SF * 128, 128), f32)
-    cterms, fterms = kernel_call(
-        first_force_kernel,
-        (shape(KC, 128), shape(KF, 128)),
-        [vmem] * 4,
-        [pltpu.VMEM(((KC + KF) * 8, 128), f32)],
-        10,
-    )(crows, frows, cwarm, warm_face)
+    def first_force(jac, warm):
+        blocks = warm.shape[0]
+        return kernel_call(
+            first_force_kernel,
+            shape(blocks, 128),
+            [vmem] * 2,
+            [pltpu.VMEM((blocks * 8, 128), f32)],
+            10,
+        )(jac, warm)
+
+    fterms = first_force(frows, warm_face)
     arriving = shifted(fterms, "slab", 1)
+    cterms = first_force(crows, cwarm)
     cnow = to_lanes(cwarm, GC)
     fnow = to_lanes(warm_face, GF)
     cy, fy = cnow, fnow

time: 199 us -> 198 us (level)
    unnamed x31 -> x25, local copies, waits for them, and re-layouts: 9.23 us -> 9.26 us
  transfers between devices with their start and end apart: 20 -> 20, of which waited for: 17 -> 16; matrix products, arithmetic and copies ran while one was open for 1% -> 3% of each run, Pallas kernels for 10% -> 11%
where the time goes in v7:
time: 198 us
  blocking collectives  84.6 us (43%)
  waiting for transfers between devices  39.2 us (20%)
  Pallas kernels  30.6 us (15%)
  starting transfers between devices  25.7 us (13%)
  local copies, waits for them, and re-layouts  11.2 us (6%)
  other arithmetic  4.13 us (2%)
  between operations  2.35 us (1%)
    all_to_all x5, blocking collectives, exchange(): lax.all_to_all(parts, 'grp', 0, 0, axis_index_groups=groups, tiled=True)  84.6 us
    all_to_all x2, waiting for transfers between devices, exchange(): lax.all_to_all(parts, 'grp', 0, 0, axis_index_groups=groups, tiled=True)  16.3 us
    all_to_all x2, starting transfers between devices, exchange(): lax.all_to_all(parts, 'grp', 0, 0, axis_index_groups=groups, tiled=True)  16 us
    ppermute x11, waiting for transfers between devices, shifted(): lax.ppermute(x, axis, [(i, (i + by) % devices) for i in range(devices)])  12.2 us
    ppermute x7, waiting for transfers between devices, other_core(): return lax.ppermute(x, 'grp', [(i, i ^ 1) for i in range(devices)])  10.6 us
    ppermute x11, starting transfers between devices, shifted(): lax.ppermute(x, axis, [(i, (i + by) % devices) for i in range(devices)])  9.35 us
    unnamed x25, local copies, waits for them, and re-layouts  9.26 us
    pallas_call x1, Pallas kernels, on_device(): kernel_call(layout_kernel, (shape(SC * 128, 128), shape(SF * 128, 128), s...  7.19 us
  transfers between devices with their start and end apart: 20, of which 16 were waited for; matrix products, arithmetic and copies ran while one was open for 3% of the time, Pallas kernels for 11%

profile of v7, /device:TPU:32, one launch (start us, length us, event | category | flops | bytes accessed | tf_op | source)
XLA Modules:
  0.0 197.7 jit_solution(16947928729346590527)
XLA Ops:
  8.1 2.8 %copy-done.2 = f32[64,3,64,128]{3,2,1,0:T(8,128)S(1)} copy-done((f32[64,3,64,128]{3,2,1,0:T(8,128)S(1)}, f32[64,3,64,128]{3,2,1,0:T(8,128)}, u32[]{:S(2)}) %copy-start.2) | copy-done | bytes 6291480
  10.9 1.9 shard_map.158.cterms
  17.3 11.4 %all-to-all-start = ((f32[32,16,128]{2,1,0:T(8,128)}), f32[32,16,128]{2,1,0:T(8,128)S(1)}, u32[]{:S(2)}, u32[]{:S(2)}) async-start(f32[32,16,128]{2,1,0:T(8,128)} %bitcast.7.after), calls=%async_computation | async-start | bytes 524288 | tf_op jit(solution)/shard_map/all_to_all | solution.py:313
  28.6 7.2 %shard_map.161 = (f32[12288,128]{1,0:T(8,128)}, f32[3072,128]{1,0:T(8,128)S(1)}, f32[8,128]{1,0:T(8,128)S(1)}) custom-call(f32[64,192,128]{2,1,0:T(8,128)} %bitcast.46, f32[16,192,128]{2,1,0:T(8,128)} %bitcast.48, f32[32,16,128]{2,1,0:T(8,128)} %bitcast.7.after), custom_call_target="tpu_custom_call" | custom-call | bytes 41943040 | tf_op jit(solution)/shard_map/pallas_call | solution.py:403
  35.8 5.4 %all-to-all-done.received = f32[32,16,128]{2,1,0:T(8,128)S(1)} async-done(((f32[32,16,128]{2,1,0:T(8,128)}), f32[32,16,128]{2,1,0:T(8,128)S(1)}, u32[]{:S(2)}, u32[]{:S(2)}) %all-to-all-start) | async-done | bytes 262176 | tf_op jit(solution)/shard_map/all_to_all | solution.py:313
  41.4 16.9 %all_to_all.35.own = f32[32,2,1152]{2,1,0:T(2,128)S(1)} all-to-all(f32[32,2,1152]{2,1,0:T(2,128)S(1)} %get-tuple-element.59), channel_id=1, replica_groups={{0,2,4,6,8,10,12,14,16,18,20,22,24,26,28,30,32,34,36,38,40,42,44,46,48,..., dimensions={0} | all-to-all | bytes 589824 | tf_op jit(solution)/shard_map/all_to_all | solution.py:313
  61.3 1.7 collective-permute-start.3
  64.7 2.8 %copy-done = f32[12288,128]{1,0:T(8,128)S(1)} copy-done((f32[12288,128]{1,0:T(8,128)S(1)}, f32[12288,128]{1,0:T(8,128)}, u32[]{:S(2)}) %copy-start) | copy-done | bytes 6291480
  67.5 1.8 shard_map.163
  72.2 2.6 %collective-permute-done.4.arriving = f32[16,128]{1,0:T(8,128)S(1)} collective-permute-done((f32[16,128]{1,0:T(8,128)S(1)}, f32[16,128]{1,0:T(8,128)S(1)}, u32[]{:S(2)}, u32[]{:S(2)}) %collective-permute-start.4) | collective-permute-done | bytes 8224 | tf_op jit(solution)/shard_map/ppermute | solution.py:54
  77.2 17.0 %all_to_all.36.received = f32[32,16,128]{2,1,0:T(8,128)S(1)} all-to-all(f32[32,16,128]{2,1,0:T(8,128)S(1)} %bitcast.57), channel_id=1, replica_groups={{0,2,4,6,8,10,12,14,16,18,20,22,24,26,28,30,32,34,36,38,40,42,44,46,48,..., dimensions={0} | all-to-all | bytes 524288 | tf_op jit(solution)/shard_map/all_to_all | solution.py:313
  94.4 16.8 %all_to_all.37.own = f32[32,2,1152]{2,1,0:T(2,128)S(1)} all-to-all(f32[32,2,1152]{2,1,0:T(2,128)S(1)} %get-tuple-element.73), channel_id=1, replica_groups={{0,2,4,6,8,10,12,14,16,18,20,22,24,26,28,30,32,34,36,38,40,42,44,46,48,..., dimensions={0} | all-to-all | bytes 589824 | tf_op jit(solution)/shard_map/all_to_all | solution.py:313
  111.2 1.6 collective-permute-done.6.other
  115.5 1.8 shard_map.171
  117.3 1.6 collective-permute-done.8.refs_2_
  123.2 2.1 %collective-permute-done.10.arriving = f32[16,128]{1,0:T(8,128)S(1)} collective-permute-done((f32[16,128]{1,0:T(8,128)S(1)}, f32[16,128]{1,0:T(8,128)S(1)}, u32[]{:S(2)}, u32[]{:S(2)}) %collective-permute-start.10) | collective-permute-done | bytes 8224 | tf_op jit(solution)/shard_map/ppermute | solution.py:54
  127.6 17.0 %all_to_all.38.received = f32[32,16,128]{2,1,0:T(8,128)S(1)} all-to-all(f32[32,16,128]{2,1,0:T(8,128)S(1)} %bitcast.58), channel_id=1, replica_groups={{0,2,4,6,8,10,12,14,16,18,20,22,24,26,28,30,32,34,36,38,40,42,44,46,48,..., dimensions={0} | all-to-all | bytes 524288 | tf_op jit(solution)/shard_map/all_to_all | solution.py:313
  145.3 16.8 %all_to_all.39.own = f32[32,2,1152]{2,1,0:T(2,128)S(1)} all-to-all(f32[32,2,1152]{2,1,0:T(2,128)S(1)} %get-tuple-element.89), channel_id=1, replica_groups={{0,2,4,6,8,10,12,14,16,18,20,22,24,26,28,30,32,34,36,38,40,42,44,46,48,..., dimensions={0} | all-to-all | bytes 589824 | tf_op jit(solution)/shard_map/all_to_all | solution.py:313
  162.1 1.6 collective-permute-done.12.other
  166.4 1.8 shard_map.178
  168.2 2.1 %collective-permute-done.14.refs_2_ = f32[8,128]{1,0:T(8,128)S(1)} collective-permute-done((f32[8,128]{1,0:T(8,128)S(1)}, f32[8,128]{1,0:T(8,128)S(1)}, u32[]{:S(2)}, u32[]{:S(2)}) %collective-permute-start.14) | collective-permute-done | bytes 4128 | tf_op jit(solution)/shard_map/ppermute | solution.py:54
  174.5 2.3 %collective-permute-done.16.arriving = f32[16,128]{1,0:T(8,128)S(1)} collective-permute-done((f32[16,128]{1,0:T(8,128)S(1)}, f32[16,128]{1,0:T(8,128)S(1)}, u32[]{:S(2)}, u32[]{:S(2)}) %collective-permute-start.16) | collective-permute-done | bytes 8224 | tf_op jit(solution)/shard_map/ppermute | solution.py:54
  179.9 4.6 %all-to-all-start.6 = ((f32[32,16,128]{2,1,0:T(8,128)}), f32[32,16,128]{2,1,0:T(8,128)S(1)}, u32[]{:S(2)}, u32[]{:S(2)}) async-start(f32[32,16,128]{2,1,0:T(8,128)} %bitcast.26), calls=%async_computation.6 | async-start | bytes 524288 | tf_op jit(solution)/shard_map/all_to_all | solution.py:313
  186.2 10.9 %all-to-all-done.6 = f32[32,16,128]{2,1,0:T(8,128)S(1)} async-done(((f32[32,16,128]{2,1,0:T(8,128)}), f32[32,16,128]{2,1,0:T(8,128)S(1)}, u32[]{:S(2)}, u32[]{:S(2)}) %all-to-all-start.6) | async-done | bytes 262176 | tf_op jit(solution)/shard_map/all_to_all | solution.py:313
  (107 shorter events, 42.8 us)
Async XLA Ops:
  3.4 10.9 %collective-permute-start = (f32[16,128]{1,0:T(8,128)S(1)}, f32[16,128]{1,0:T(8,128)S(1)}, u32[]{:S(2)}, u32[]{:S(2)}) collective-permute-start(f32[16,128]{1,0:T(8,128)S(1)} %shard_map.157.fterms), channel_id=1, source_target_pairs={{0,64},{64,128},{128,192},{192,0},{1,65},{65,129},{129,193},{193,1... | collective-permute-start | bytes 24584 | tf_op jit(solution)/shard_map/ppermute | solution.py:54
  12.8 45.6 %copy-start.8 = (s32[64,64]{1,0:T(8,128)S(1)}, s32[64,64]{1,0:T(8,128)}, u32[]{:S(2)}) copy-start(s32[64,64]{1,0:T(8,128)} %param.16) | copy-start | bytes 49156
  12.8 45.6 %copy-start.10 = (f32[8]{0:T(128)S(1)}, f32[8]{0:T(128)}, u32[]{:S(2)}) copy-start(f32[8]{0:T(128)} %param.26) | copy-start | bytes 100
  12.8 50.3 %copy-start.9 = (s32[16,64]{1,0:T(8,128)S(1)}, s32[16,64]{1,0:T(8,128)}, u32[]{:S(2)}) copy-start(s32[16,64]{1,0:T(8,128)} %param.21) | copy-start | bytes 12292
  12.8 50.4 %copy-start.7 = (f32[16,192]{1,0:T(8,128)S(1)}, f32[16,192]{1,0:T(8,128)}, u32[]{:S(2)}) copy-start(f32[16,192]{1,0:T(8,128)} %warm.1) | copy-start | bytes 36868
  14.9 1.6 collective-permute-start.1
  17.3 24.0 %all-to-all-start = ((f32[32,16,128]{2,1,0:T(8,128)}), f32[32,16,128]{2,1,0:T(8,128)S(1)}, u32[]{:S(2)}, u32[]{:S(2)}) async-start(f32[32,16,128]{2,1,0:T(8,128)} %bitcast.7.after), calls=%async_computation | async-start | bytes 524288 | tf_op jit(solution)/shard_map/all_to_all | solution.py:313
  58.3 1.6 collective-permute-start.2
  61.3 8.0 %collective-permute-start.3 = (f32[24,128]{1,0:T(8,128)S(1)}, f32[24,128]{1,0:T(8,128)S(1)}, u32[]{:S(2)}, u32[]{:S(2)}) collective-permute-start(f32[24,128]{1,0:T(8,128)S(1)} %get-tuple-element.63), channel_id=1, source_target_pairs={{0,192},{64,0},{128,64},{192,128},{1,193},{65,1},{129,65},{193,129... | collective-permute-start | bytes 36872 | tf_op jit(solution)/shard_map/ppermute | solution.py:54
  69.9 4.9 %collective-permute-start.4 = (f32[16,128]{1,0:T(8,128)S(1)}, f32[16,128]{1,0:T(8,128)S(1)}, u32[]{:S(2)}, u32[]{:S(2)}) collective-permute-start(f32[16,128]{1,0:T(8,128)S(1)} %get-tuple-element.65.fterms), channel_id=1, source_target_pairs={{0,64},{64,128},{128,192},{192,0},{1,65},{65,129},{129,193},{193,1... | collective-permute-start | bytes 24584 | tf_op jit(solution)/shard_map/ppermute | solution.py:54
  75.5 1.6 collective-permute-start.5
  111.2 1.6 collective-permute-start.6
  113.5 6.3 %collective-permute-start.9 = (f32[24,128]{1,0:T(8,128)S(1)}, f32[24,128]{1,0:T(8,128)S(1)}, u32[]{:S(2)}, u32[]{:S(2)}) collective-permute-start(f32[24,128]{1,0:T(8,128)S(1)} %get-tuple-element.77), channel_id=1, source_target_pairs={{0,192},{64,0},{128,64},{192,128},{1,193},{65,1},{129,65},{193,129... | collective-permute-start | bytes 36872 | tf_op jit(solution)/shard_map/ppermute | solution.py:54
  113.8 5.1 %collective-permute-start.8 = (f32[8,128]{1,0:T(8,128)S(1)}, f32[8,128]{1,0:T(8,128)S(1)}, u32[]{:S(2)}, u32[]{:S(2)}) collective-permute-start(f32[8,128]{1,0:T(8,128)S(1)} %get-tuple-element.74.refs_0_), channel_id=1, source_target_pairs={{0,128},{64,192},{128,0},{192,64},{1,129},{65,193},{129,1},{193,65... | collective-permute-start | bytes 12296 | tf_op jit(solution)/shard_map/ppermute | solution.py:54
  114.6 5.2 %collective-permute-start.7 = (f32[8,128]{1,0:T(8,128)S(1)}, f32[8,128]{1,0:T(8,128)S(1)}, u32[]{:S(2)}, u32[]{:S(2)}) collective-permute-start(f32[8,128]{1,0:T(8,128)S(1)} %get-tuple-element.74.refs_0_), channel_id=1, source_target_pairs={{0,64},{64,128},{128,192},{192,0},{1,65},{65,129},{129,193},{193,1... | collective-permute-start | bytes 12296 | tf_op jit(solution)/shard_map/ppermute | solution.py:54
  120.3 4.9 %collective-permute-start.10 = (f32[16,128]{1,0:T(8,128)S(1)}, f32[16,128]{1,0:T(8,128)S(1)}, u32[]{:S(2)}, u32[]{:S(2)}) collective-permute-start(f32[16,128]{1,0:T(8,128)S(1)} %get-tuple-element.81.fterms), channel_id=1, source_target_pairs={{0,64},{64,128},{128,192},{192,0},{1,65},{65,129},{129,193},{193,1... | collective-permute-start | bytes 24584 | tf_op jit(solution)/shard_map/ppermute | solution.py:54
  126.0 1.6 collective-permute-start.11
  162.1 1.6 collective-permute-start.12
  164.4 6.6 %collective-permute-start.15 = (f32[24,128]{1,0:T(8,128)S(1)}, f32[24,128]{1,0:T(8,128)S(1)}, u32[]{:S(2)}, u32[]{:S(2)}) collective-permute-start(f32[24,128]{1,0:T(8,128)S(1)} %get-tuple-element.93), channel_id=1, source_target_pairs={{0,192},{64,0},{128,64},{192,128},{1,193},{65,1},{129,65},{193,129... | collective-permute-start | bytes 36872 | tf_op jit(solution)/shard_map/ppermute | solution.py:54
  165.2 5.1 %collective-permute-start.14 = (f32[8,128]{1,0:T(8,128)S(1)}, f32[8,128]{1,0:T(8,128)S(1)}, u32[]{:S(2)}, u32[]{:S(2)}) collective-permute-start(f32[8,128]{1,0:T(8,128)S(1)} %get-tuple-element.90.refs_0_), channel_id=1, source_target_pairs={{0,128},{64,192},{128,0},{192,64},{1,129},{65,193},{129,1},{193,65... | collective-permute-start | bytes 12296 | tf_op jit(solution)/shard_map/ppermute | solution.py:54
  166.1 4.8 %collective-permute-start.13 = (f32[8,128]{1,0:T(8,128)S(1)}, f32[8,128]{1,0:T(8,128)S(1)}, u32[]{:S(2)}, u32[]{:S(2)}) collective-permute-start(f32[8,128]{1,0:T(8,128)S(1)} %get-tuple-element.90.refs_0_), channel_id=1, source_target_pairs={{0,64},{64,128},{128,192},{192,0},{1,65},{65,129},{129,193},{193,1... | collective-permute-start | bytes 12296 | tf_op jit(solution)/shard_map/ppermute | solution.py:54
  172.0 4.9 %collective-permute-start.16 = (f32[16,128]{1,0:T(8,128)S(1)}, f32[16,128]{1,0:T(8,128)S(1)}, u32[]{:S(2)}, u32[]{:S(2)}) collective-permute-start(f32[16,128]{1,0:T(8,128)S(1)} %get-tuple-element.99.fterms), channel_id=1, source_target_pairs={{0,64},{64,128},{128,192},{192,0},{1,65},{65,129},{129,193},{193,1... | collective-permute-start | bytes 24584 | tf_op jit(solution)/shard_map/ppermute | solution.py:54
  177.5 1.6 collective-permute-start.17
  179.9 17.2 %all-to-all-start.6 = ((f32[32,16,128]{2,1,0:T(8,128)}), f32[32,16,128]{2,1,0:T(8,128)S(1)}, u32[]{:S(2)}, u32[]{:S(2)}) async-start(f32[32,16,128]{2,1,0:T(8,128)} %bitcast.26), calls=%async_computation.6 | async-start | bytes 524288 | tf_op jit(solution)/shard_map/all_to_all | solution.py:313
  (7 other events, 67.5 us)
